TPU v7x, 32 devices: a whole 2x2x4 slice. The times are simulated.
32 devices in a mesh: gx: 4 (over z), gy: 8 (over y, x, core).
Axes of the slice: x: 2, y: 2, z: 4, core: 2. Of those that a mesh axis runs over, the one named last changes fastest.
Arguments:
- features: bfloat16 [32, 128, 16, 128], P('gx', 'gy'), may hold values from -6 to 6
- w_first: bfloat16 [27, 128, 128], replicated, may hold values from -0.109375 to 0.109375
- w_second: bfloat16 [27, 128, 128], replicated, may hold values from -0.109375 to 0.109375
- occupancy: int32 [4, 16, 2], P('gx', 'gy'), may hold values from 0 to 1, as said below
- cotangent: bfloat16 [32, 128, 16, 128], P('gx', 'gy'), may hold values from -6 to 6
Outputs:
- output: bfloat16 [32, 128, 16, 128], P('gx', 'gy')
- grad_features: bfloat16 [32, 128, 16, 128], P('gx', 'gy')
- grad_first: float32 [27, 128, 128], P(None, 'gy')
- grad_second: float32 [27, 128, 128], P(None, 'gy')
Inputs may be any that keep to these rules, and one draw needn't show every extreme that they name: `occupancy`: 1 marks an active block; the share of active blocks differs from one tile of 1 x 2 x 2 blocks to another.
All inputs are finite; a program needn't handle non-finite values.
Results may differ from a plain program's by a relative error of at most 0.0025.
The roundings to bfloat16 on the way count: a program that leaves them out, or rounds other values in their place, can miss the bound.
Values may be sent and summed in bfloat16 or wider, within the bound.
No kernel may reach another device: no remote copies, remote signals or barrier semaphores. Data moves between devices by JAX's collectives and lax.ppermute only.
A program may use at most 128 MiB of HBM per device.

v0:
```python
import math

import jax
import jax.numpy as jnp
from jax import lax
from jax.experimental import pallas as pl
from jax.experimental.pallas import tpu as pltpu
from jax.sharding import PartitionSpec as P

BF16 = jnp.bfloat16
F32 = jnp.float32
VMEM = pl.BlockSpec(memory_space=pltpu.VMEM)
HBM = pl.BlockSpec(memory_space=pltpu.HBM)
MIB = 1024 * 1024
BLOCK = 8


def call(kernel, out_shapes, args, spaces, scratch=(), flops=0, nbytes=0, vmem=16 * MIB, aliases=None):
    return pl.pallas_call(
        kernel,
        out_shape=out_shapes,
        in_specs=list(spaces) + [VMEM] * (len(args) - len(spaces)),
        out_specs=jax.tree.map(lambda _: VMEM, out_shapes),
        scratch_shapes=list(scratch),
        input_output_aliases=aliases or {},
        compiler_params=pltpu.CompilerParams(vmem_limit_bytes=vmem),
        cost_estimate=pl.CostEstimate(flops=flops, bytes_accessed=nbytes, transcendentals=0),
    )(*args)


def swap_pairs(count, odd):
    if not odd:
        return [(i, i ^ 1) for i in range(count)]
    ends = [(0, 0), (count - 1, count - 1)]
    inner = [(i, i + 1) for i in range(1, count - 1, 2)]
    return ends + inner + [(b, a) for a, b in inner]


def plane_mask(occ, block_x, size_y, size_z):
    row = lax.broadcasted_iota(jnp.int32, (size_y * size_z, 128), 0)
    block_y = row // (BLOCK * size_z)
    block_z = (row % size_z) // BLOCK
    mask = jnp.zeros((size_y * size_z, 128), F32)
    for i in range(size_y // BLOCK):
        for j in range(size_z // BLOCK):
            here = (block_y == i) & (block_z == j)
            mask = jnp.where(here, occ[block_x, i, j].astype(F32), mask)
    return mask


def pick(odd, if_even, if_odd):
    return jnp.where(odd == 0, if_even, if_odd)


def one_if(condition):
    return jnp.where(condition, 1.0, 0.0).astype(BF16)


def side_of(axis):
    index = lax.axis_index(axis)
    return index % 2, one_if(index > 0), one_if(index < lax.axis_size(axis) - 1)


def pack_sides(features, cotangent, occ):
    size_x, size_y, size_z, channels = features.shape
    rows = size_y * size_z

    def kernel(occ_hbm, first, second, mask, xa, xb, ya, yb, occ_ref, sem, occ_sem):
        odd_x, odd_y = lax.axis_index("gx") % 2, lax.axis_index("gy") % 2
        first_x = pick(odd_x, size_x - 1, 0)
        first_y = pick(odd_y, size_y - 1, 0)
        sides = ((xa, first_x), (xb, size_x - 1 - first_x))
        columns = ((ya, first_y), (yb, size_y - 1 - first_y))
        occ_copy = pltpu.make_async_copy(occ_hbm, occ_ref, occ_sem)
        occ_copy.start()
        copies = []
        for f, ref in enumerate((first, second)):
            for n, (out, x) in enumerate(sides):
                copies.append(pltpu.make_async_copy(ref.at[x], out.at[f], sem.at[f, n]))
            for n, (out, y) in enumerate(columns):
                copies.append(pltpu.make_async_copy(ref.at[:, y], out.at[f], sem.at[f, 2 + n]))
        for copy in copies:
            copy.start()
        occ_copy.wait()
        for n in range(size_x // BLOCK):
            mask[n] = plane_mask(occ_ref, n, size_y, size_z)
        for copy in copies:
            copy.wait()
        for out, x in sides:
            here = mask[x // BLOCK].astype(BF16).reshape(size_y, size_z, channels)
            for f in range(2):
                out[f] = out[f] * here
        for out, y in columns:
            at = pl.ds(pl.multiple_of(y * size_z, size_z), size_z)
            for x in range(size_x):
                here = mask[x // BLOCK, at, :].astype(BF16)
                for f in range(2):
                    out[f, x] = out[f, x] * here

    side = pltpu.VMEM((2, size_y, size_z, channels), BF16)
    column = pltpu.VMEM((2, size_x, size_z, channels), BF16)
    return call(
        kernel,
        (pltpu.VMEM((size_x // BLOCK, rows, channels), F32), side, side, column, column),
        [pltpu.with_memory_space_constraint(value, pltpu.HBM) for value in (occ, features, cotangent)],
        [HBM] * 3,
        scratch=[
            pltpu.SMEM(occ.shape, jnp.int32),
            pltpu.SemaphoreType.DMA((2, 4)),
            pltpu.SemaphoreType.DMA(()),
        ],
        nbytes=MIB,
        vmem=4 * MIB,
    )


def finish_columns(got_xa, got_xb, ya, yb):
    _, size_y, size_z, channels = got_xa.shape
    size_x = ya.shape[1]

    def kernel(xa, xb, ya, yb, out_a, out_b):
        odd, low_ok, high_ok = side_of("gx")
        first_y = pick(lax.axis_index("gy") % 2, size_y - 1, 0)
        for out, own, y in ((out_a, ya, first_y), (out_b, yb, size_y - 1 - first_y)):
            for f in range(2):
                out[f, 0] = pick(odd, xb[f, y], xa[f, y]) * low_ok
                out[f, size_x + 1] = pick(odd, xa[f, y], xb[f, y]) * high_ok
                out[f, 1 : size_x + 1] = own[f]

    shape = jax.ShapeDtypeStruct((2, size_x + 2, size_z, channels), BF16)
    return call(kernel, (shape, shape), (got_xa, got_xb, ya, yb), [], nbytes=MIB, vmem=4 * MIB)


def swap_sides(xa, xb):
    even, odd = (swap_pairs(lax.axis_size("gx"), which) for which in (False, True))
    return lax.ppermute(xa, "gx", even), lax.ppermute(xb, "gx", odd)


def swap_columns(ya, yb):
    even, odd = (swap_pairs(lax.axis_size("gy"), which) for which in (False, True))
    return lax.ppermute(ya, "gy", even), lax.ppermute(yb, "gy", odd)


def store_shifts(zc, x, ys, rows):
    size_z = zc.shape[2]
    count, lanes = rows.shape
    wide = rows.astype(F32)
    z = lax.broadcasted_iota(jnp.int32, (count, lanes), 0) % size_z
    below = jnp.where(z == 0, 0.0, pltpu.roll(wide, 1, 0)).astype(BF16)
    above = jnp.where(z == size_z - 1, 0.0, pltpu.roll(wide, count - 1, 0)).astype(BF16)
    shape = (count // size_z, size_z, lanes)
    for k, part in enumerate((below, rows, above)):
        zc[x, ys[0] : ys[1], :, k * lanes : (k + 1) * lanes] = part.reshape(shape)


def fill_own(zc, plane):
    size_x, size_y = zc.shape[0] - 2, zc.shape[1] - 2
    zc[0] = jnp.zeros(zc.shape[1:], BF16)
    zc[size_x + 1] = jnp.zeros(zc.shape[1:], BF16)
    for x in range(size_x):
        for y in (0, size_y + 1):
            zc[x + 1, y] = jnp.zeros(zc.shape[2:], BF16)
        store_shifts(zc, x + 1, (1, size_y + 1), plane(x))


def fill_sides(zc, f, xa, xb):
    size_x, size_y, size_z = zc.shape[0] - 2, zc.shape[1] - 2, zc.shape[2]
    rows = size_y * size_z
    odd, low_ok, high_ok = side_of("gx")
    channels = xa.shape[3]
    store_shifts(zc, 0, (1, size_y + 1), (pick(odd, xb[f], xa[f]) * low_ok).reshape(rows, channels))
    store_shifts(zc, size_x + 1, (1, size_y + 1), (pick(odd, xa[f], xb[f]) * high_ok).reshape(rows, channels))


def fill_columns(zc, f, ya, yb):
    size_x, size_y = zc.shape[0] - 2, zc.shape[1] - 2
    odd, low_ok, high_ok = side_of("gy")
    for x in range(size_x + 2):
        store_shifts(zc, x, (0, 1), pick(odd, yb[f, x], ya[f, x]) * low_ok)
        store_shifts(zc, x, (size_y + 1, size_y + 2), pick(odd, ya[f, x], yb[f, x]) * high_ok)


def straight(w):
    return lambda tap: w[tap]


def turned(w):
    return lambda tap: w[26 - tap].T


def lay_weights(taps, weight):
    channels = taps.shape[2] // 2
    zero = jnp.zeros((channels, channels), BF16)
    for j in range(3):
        for k in range(3):
            rows = slice(k * channels, (k + 1) * channels)
            for tap in range(3):
                value = weight(9 * tap + 3 * j + k)
                taps[3 * tap + j, rows, :channels] = value
                taps[3 * (tap + 1) + j, rows, channels:] = value
            taps[j, rows, channels:] = zero
            taps[9 + j, rows, :channels] = zero


def convolve(zc, taps, emit):
    size_x, size_y, size_z = zc.shape[0] - 2, zc.shape[1] - 2, zc.shape[2]
    depth = zc.shape[3]
    channels = depth // 3
    rows = size_y * size_z
    for x in range(0, size_x, 4):
        pieces = []
        for i in range(4):
            for j in range(3):
                halves = [zc[x + 2 * h + i, j : j + size_y].reshape(rows, depth) for h in range(2)]
                pieces.append(jnp.concatenate(halves, axis=0))
        both = jnp.dot(
            jnp.concatenate(pieces, axis=1),
            taps[...].reshape(12 * depth, 2 * channels),
            preferred_element_type=F32,
        )
        for h in range(2):
            for side in range(2):
                emit(x + 2 * h + side, both[h * rows : (h + 1) * rows, side * channels : (side + 1) * channels])


def add_halo_terms(total, zc, taps):
    size_x, size_y, size_z = zc.shape[0] - 2, zc.shape[1] - 2, zc.shape[2]
    depth = zc.shape[3]
    channels = depth // 3
    rows = size_y * size_z

    def weights(which):
        return jnp.concatenate([taps[n, :, :channels] for n in which], axis=0)

    for plane, x, first in ((0, 0, 0), (size_x + 1, size_x - 1, 6)):
        side = jnp.concatenate([zc[plane, j : j + size_y].reshape(rows, depth) for j in range(3)], axis=1)
        total[x] += jnp.dot(side, weights((first, first + 1, first + 2)), preferred_element_type=F32)
    none = jnp.zeros((size_z, depth), BF16)
    for column, y, j in ((0, 0, 0), (size_y + 1, size_y - 1, 2)):
        own = zc[1 : size_x + 1, column].reshape(size_x * size_z, depth)
        below = jnp.concatenate([none, own[:-size_z]], axis=0)
        above = jnp.concatenate([own[size_z:], none], axis=0)
        side = jnp.concatenate([below, own, above], axis=1)
        term = jnp.dot(side, weights((j, 3 + j, 6 + j)), preferred_element_type=F32)
        total[:, y * size_z : (y + 1) * size_z, :] += term.reshape(size_x, size_z, channels)


def field_shape(shape):
    size_x, size_y, size_z, channels = shape
    return (size_x + 2, size_y + 2, size_z, 3 * channels)


def taps_shape(channels):
    return (12, 3 * channels, 2 * channels)


def own_terms(mask, field, w, lay):
    size_x, size_y, size_z, channels = field.shape
    rows = size_y * size_z

    def kernel(mask, field, w, zc, taps, total):
        def plane(x):
            return field[x].reshape(rows, channels) * mask[x // BLOCK].astype(BF16)

        fill_own(zc, plane)
        lay_weights(taps, lay(w))

        def emit(x, value):
            total[x] = value

        convolve(zc, taps, emit)

    return call(
        kernel,
        (
            jax.ShapeDtypeStruct(field_shape(field.shape), BF16),
            jax.ShapeDtypeStruct(taps_shape(channels), BF16),
            jax.ShapeDtypeStruct((size_x, rows, channels), F32),
        ),
        (mask, field, w),
        [],
        flops=2 * 27 * size_x * rows * channels * channels,
        nbytes=4 * MIB,
        vmem=24 * MIB,
    )


def copy_sides(f, value, xa, xb, ya, yb):
    size_x, size_y = value.shape[:2]
    first_x = pick(lax.axis_index("gx") % 2, size_x - 1, 0)
    first_y = pick(lax.axis_index("gy") % 2, size_y - 1, 0)
    xa[f], xb[f] = value[first_x], value[size_x - 1 - first_x]
    for x in range(size_x):
        ya[f, x], yb[f, x] = value[x, first_y], value[x, size_y - 1 - first_y]


def side_shapes(shape):
    size_x, size_y, size_z, channels = shape
    side = jax.ShapeDtypeStruct((2, size_y, size_z, channels), BF16)
    column = jax.ShapeDtypeStruct((2, size_x, size_z, channels), BF16)
    return (side, side, column, column)


def grad_terms(left, zc, start, store):
    size_x, size_y, size_z = zc.shape[0] - 2, zc.shape[1] - 2, zc.shape[2]
    depth = zc.shape[3]
    channels = depth // 3
    shifts = [(i, j) for i in range(3) for j in range(3)]
    for group in [shifts[n : n + 2] for n in range(0, 9, 2)]:
        pieces = []
        for i, j in group:
            a, b = start(i, j)
            pieces.append(zc[a : a + size_x, b : b + size_y].reshape(size_x * size_y * size_z, depth))
        out = jnp.dot(left, jnp.concatenate(pieces, axis=1), preferred_element_type=F32)
        for n, (i, j) in enumerate(group):
            for k in range(3):
                store(9 * i + 3 * j, k, out[:, (3 * n + k) * channels : (3 * n + k + 1) * channels])


def scatter_block(keep, send, d, block):
    count = 2 * keep.shape[0]
    share = keep.shape[2]
    index = lax.axis_index("gy")
    half, place = index % 2, index // 2
    for j in range(count // 2):
        even = block[2 * j * share : (2 * j + 1) * share]
        odd = block[(2 * j + 1) * share : (2 * j + 2) * share]
        at = jnp.bitwise_xor(place, j)
        keep[at, d] = pick(half, even, odd)
        send[at, d] = pick(half, odd, even)


def terms_shape(channels):
    count_y = lax.axis_size("gy")
    return jax.ShapeDtypeStruct((count_y // 2, 27, channels // count_y, channels), F32)


def hidden_and_terms(mask, halos, zm, zu, taps, pre, shape):
    size_x, size_y, size_z, channels = shape
    rows = size_y * size_z

    def kernel(mask, xa, xb, ya, yb, taps, pre, zm_in, zu_in, zm, zu, hidden, slope, keep, send):
        for f, zc in enumerate((zm, zu)):
            fill_sides(zc, f, xa, xb)
            fill_columns(zc, f, ya, yb)
        slope[...] = pre[...]
        add_halo_terms(slope, zm, taps)
        for x in range(size_x):
            here = mask[x // BLOCK]
            value = slope[x]
            s = jax.nn.sigmoid(value)
            hidden[x] = (here * (value * s)).astype(BF16).reshape(size_y, size_z, channels)
            slope[x] = here * (s * (1.0 + value * (1.0 - s)))
        left = hidden[...].reshape(size_x * rows, channels).T

        def store(d, k, block):
            scatter_block(keep, send, d + 2 - k, block)

        grad_terms(left, zu, lambda i, j: (2 - i, 2 - j), store)

    field = jax.ShapeDtypeStruct(shape, BF16)
    wide = jax.ShapeDtypeStruct(pre.shape, F32)
    shifted = jax.ShapeDtypeStruct(zm.shape, BF16)
    terms = terms_shape(channels)
    return call(
        kernel,
        (shifted, shifted, field, wide, terms, terms),
        (mask, *halos, taps, pre, zm, zu),
        [],
        flops=2 * 27 * size_x * rows * channels * channels,
        nbytes=8 * MIB,
        vmem=24 * MIB,
        aliases={7: 0, 8: 1},
    )


def pre_grad_and_terms(hidden, slope, zm, zu, taps, grad):
    size_x, rows, channels = grad.shape
    size_y, size_z = zu.shape[1] - 2, zu.shape[2]
    shape = (size_x, size_y, size_z, channels)

    def kernel(hidden, slope, zm, zu, taps, grad, pre_grad, keep, send, xa, xb, ya, yb, total):
        total[...] = grad[...]
        add_halo_terms(total, zu, taps)
        for x in range(size_x):
            pre_grad[x] = (total[x] * slope[x]).astype(BF16).reshape(size_y, size_z, channels)
        for f, value in enumerate((hidden, pre_grad)):
            copy_sides(f, value, xa, xb, ya, yb)
        left = pre_grad[...].reshape(size_x * rows, channels).T

        def store(d, k, block):
            scatter_block(keep, send, d + k, block.T)

        grad_terms(left, zm, lambda i, j: (i, j), store)

    terms = terms_shape(channels)
    return call(
        kernel,
        (jax.ShapeDtypeStruct(shape, BF16), terms, terms, *side_shapes(shape)),
        (hidden, slope, zm, zu, taps, grad),
        [],
        scratch=[pltpu.VMEM(grad.shape, F32)],
        flops=2 * 27 * size_x * rows * channels * channels,
        nbytes=8 * MIB,
        vmem=24 * MIB,
    )


def add_convolution(mask, own, field, f, halos, w, lay):
    size_x, size_y, size_z, channels = own.shape
    rows = size_y * size_z

    def kernel(mask, own, field, xa, xb, ya, yb, w, out, zc, taps):
        for x in range(size_x):
            store_shifts(zc, x + 1, (1, size_y + 1), field[x].reshape(rows, channels))
        fill_sides(zc, f, xa, xb)
        fill_columns(zc, f, ya, yb)
        lay_weights(taps, lay(w))

        def emit(x, term):
            near = own[x].reshape(rows, channels).astype(F32)
            out[x] = (mask[x // BLOCK] * (near + term)).astype(BF16).reshape(size_y, size_z, channels)

        convolve(zc, taps, emit)

    return call(
        kernel,
        jax.ShapeDtypeStruct(own.shape, BF16),
        (mask, own, field, *halos, w),
        [],
        scratch=[pltpu.VMEM(field_shape(own.shape), BF16), pltpu.VMEM(taps_shape(channels), BF16)],
        flops=2 * 27 * size_x * rows * channels * channels,
        nbytes=3 * MIB,
        vmem=24 * MIB,
    )


def after(values, *others):
    return lax.optimization_barrier((values, others))[0]


def swap(value, axis, bit, travel):
    pairs = [(i, i ^ bit) for i in range(lax.axis_size(axis))]
    return lax.ppermute(value.astype(travel), axis, pairs)


def first_sums(keeps, cames):
    places, taps, share, channels = keeps[0].shape
    rows = taps * share

    def kernel(keep_a, keep_b, came_a, came_b, stays, *leaves):
        for g, (keep, came) in enumerate(((keep_a, came_a), (keep_b, came_b))):
            for p in range(places):
                value = (keep[p] + came[p]).reshape(rows, channels)
                if p == 0:
                    stays[g] = value
                else:
                    leaves[p - 1][g] = value.astype(BF16)

    stay = jax.ShapeDtypeStruct((2, rows, channels), F32)
    leave = jax.ShapeDtypeStruct((2, rows, channels), BF16)
    return call(kernel, (stay,) + (leave,) * (places - 1), (*keeps, *cames), [], nbytes=4 * MIB, vmem=8 * MIB)


def body(features, w_first, w_second, occ, cotangent):
    count_x, count_y = lax.axis_size("gx"), lax.axis_size("gy")
    shape = features.shape
    mask, xa, xb, ya, yb = pack_sides(features, cotangent, occ)
    xa, xb = swap_sides(xa, xb)
    zm, first_taps, pre = own_terms(mask, features, w_first, straight)
    xa, xb = after((xa, xb), pre)
    ya, yb = finish_columns(xa, xb, ya, yb)
    behind = after(mask, ya)
    ya, yb = swap_columns(ya, yb)
    zu, second_taps, grad = own_terms(behind, cotangent, w_second, turned)
    halos = after((xa, xb, ya, yb), grad)
    zm, zu, hidden, slope, keep_second, send = hidden_and_terms(mask, halos, zm, zu, first_taps, pre, shape)
    came_second = swap(send, "gy", 1, F32)
    pre_grad, keep_first, send, xa, xb, ya, yb = pre_grad_and_terms(hidden, slope, zm, zu, second_taps, grad)
    came_first = swap(send, "gy", 1, F32)
    xa, xb = swap_sides(xa, xb)

    stays, *leaves = first_sums((keep_second, keep_first), (came_second, came_first))
    came = [swap(value, "gy", 2 * (p + 1), BF16) for p, value in enumerate(leaves)]
    xa, xb = after((xa, xb), stays)
    ya, yb = finish_columns(xa, xb, ya, yb)
    came = after(came, ya)
    ya, yb = swap_columns(ya, yb)
    for value in came:
        stays = stays + value.astype(F32)
    odd = lax.axis_index("gx") % 2 == 1
    leaves = jnp.where(odd, stays[0], stays[1])
    stays = jnp.where(odd, stays[1], stays[0])
    came = swap(leaves, "gx", 1, F32)
    halos = after((xa, xb, ya, yb), leaves)
    output = add_convolution(mask, features, hidden, 0, halos, w_second, straight)
    stays = stays + after(came, output)
    bit = 2
    while bit < count_x:
        came = swap(stays, "gx", bit, F32)
        if bit == 2:
            halos = after((xa, xb, ya, yb), stays)
            grad_features = add_convolution(mask, cotangent, pre_grad, 1, halos, w_first, turned)
            came = after(came, grad_features)
        stays = stays + came
        bit *= 2
    came = swap(stays, "gx", 1, F32)
    factor = 1.0 / math.sqrt(count_x * count_y * shape[0] * shape[1] * shape[2])
    total_second = jnp.where(odd, came, stays) * factor
    total_first = jnp.where(odd, stays, came) * factor
    kernel_shape = (27, -1, shape[3])
    return output, grad_features, total_first.reshape(kernel_shape), total_second.reshape(kernel_shape)


def solution(mesh):
    in_specs = (P("gx", "gy", None, None), P(), P(), P("gx", "gy", None), P("gx", "gy", None, None))
    out_specs = (
        P("gx", "gy", None, None),
        P("gx", "gy", None, None),
        P(None, "gy", None),
        P(None, "gy", None),
    )
    return jax.shard_map(body, mesh=mesh, in_specs=in_specs, out_specs=out_specs, check_vma=False)
```

profile of v0, /device:TPU:0, one launch (start us, length us, event | category | flops | bytes accessed | tf_op | source)
XLA Modules:
  0.0 75.3 jit_solution(4531887904582376159)
XLA Ops:
  0.6 1.1 %shard_map.84 = (f32[1,256,128]{2,1,0:T(8,128)S(1)}, bf16[2,16,16,128]{3,2,1,0:T(8,128)(2,1)S(1)}, bf16[2,16,16,128]{3,2,1,0:T(8,128)(2,1)S(1)}, bf16[2,8,16,128...) custom-call(s32[1,2,2]{2,1,0:T(2,128)} %occ_hbm.1, bf16[8,16,16,128]{3,2,1,0:T(8,128)(2,1)} %own.2, ...), custom_call_target="tpu_custom_call" | custom-call | bytes 1048576 | tf_op jit(solution)/shard_map/pallas_call | solution.py:19
  1.8 3.1 %collective-permute-start = (bf16[2,16,16,128]{3,2,1,0:T(8,128)(2,1)S(1)}, bf16[2,16,16,128]{3,2,1,0:T(8,128)(2,1)S(1)}, u32[]{:S(2)}, u32[]{:S(2)}) collective-permute-start(bf16[2,16,16,128]{3,2,1,0:T(8,128)(2,1)S(1)} %get-tuple-element.59), channel_id=1, source_target_pairs={{0,8},{8,0},{16,24},{24,16},{1,9},{9,1},{17,25},{25,17},{2,10},{10... | collective-permute-start | bytes 393224 | tf_op jit(solution)/shard_map/ppermute | solution.py:136
  4.9 0.7 collective-permute-start.1
  5.5 0.0 copy-start
  5.5 1.0 %copy-done = bf16[8,16,16,128]{3,2,1,0:T(8,128)(2,1)S(1)} copy-done((bf16[8,16,16,128]{3,2,1,0:T(8,128)(2,1)S(1)}, bf16[8,16,16,128]{3,2,1,0:T(8,128)(2,1)}, u32[]{:S(2)}) %copy-start) | copy-done | bytes 524312
  6.6 0.0 copy-start.4
  6.6 1.2 %copy-done.4 = bf16[27,128,128]{2,1,0:T(8,128)(2,1)S(1)} copy-done((bf16[27,128,128]{2,1,0:T(8,128)(2,1)S(1)}, bf16[27,128,128]{2,1,0:T(8,128)(2,1)}, u32[]{:S(2)}) %copy-start.4) | copy-done | bytes 884760
  7.7 0.0 copy-start.2
  7.7 0.0 copy-start.3
  7.7 2.8 %shard_map.85 = (bf16[10,18,16,384]{3,2,1,0:T(8,128)(2,1)S(1)}, bf16[12,384,256]{2,1,0:T(8,128)(2,1)S(1)}, f32[8,256,128]{2,1,0:T(8,128)S(1)}) custom-call(f32[1,256,128]{2,1,0:T(8,128)S(1)} %get-tuple-element.68.mask, bf16[8,16,16,128]{3,2,1,0:T(8,128)(2,1)S(1)} %copy-done, bf16[27,128,128]{2,1,0:T(8,128)(2,1)S(1)} %copy-done.4), custom_call_target="tpu_custom_call" | custom-call | flops 1811939328 | bytes 4194304 | tf_op jit(solution)/shard_map/pallas_call | solution.py:19
  10.6 0.0 collective-permute-done.xa
  10.6 0.0 collective-permute-done.1.xb
  10.6 0.1 collective-permute-start.2
  10.7 0.7 collective-permute-start.3
  11.4 0.0 copy-done.2
  11.4 0.0 copy-done.3
  11.4 2.8 %shard_map.87 = (bf16[10,18,16,384]{3,2,1,0:T(8,128)(2,1)S(1)}, bf16[12,384,256]{2,1,0:T(8,128)(2,1)S(1)}, f32[8,256,128]{2,1,0:T(8,128)S(1)}) custom-call(f32[1,256,128]{2,1,0:T(8,128)S(1)} %get-tuple-element.68.mask, bf16[8,16,16,128]{3,2,1,0:T(8,128)(2,1)S(1)} %copy-done.2, bf16[27,128,128]{2,1,0:T(8,128)(2,1)S(1)} %copy-done.3), custom_call_target="tpu_custom_call" | custom-call | flops 1811939328 | bytes 4194304 | tf_op jit(solution)/shard_map/pallas_call | solution.py:19
  14.2 0.0 collective-permute-done.2.ya
  14.3 0.0 collective-permute-done.3.yb
  14.3 2.9 %shard_map.88 = (bf16[10,18,16,384]{3,2,1,0:T(8,128)(2,1)S(1)}, bf16[10,18,16,384]{3,2,1,0:T(8,128)(2,1)S(1)}, bf16[8,16,16,128]{3,2,1,0:T(8,128)(2,1)S(1)}, f32...) custom-call(f32[1,256,128]{2,1,0:T(8,128)S(1)} %get-tuple-element.68, ...), custom_call_target="tpu_custom_call", output_to_operand_aliasing={{0}: (7, {}), {1}: (8, {})} | custom-call | flops 1811939328 | bytes 8388608 | tf_op jit(solution)/shard_map/pallas_call | solution.py:19
  17.2 3.5 %shard_map.89 = (bf16[8,16,16,128]{3,2,1,0:T(8,128)(2,1)S(1)}, f32[4,27,16,128]{3,2,1,0:T(8,128)S(1)}, f32[4,27,16,128]{3,2,1,0:T(8,128)S(1)}, bf16[2,16,16,128]...) custom-call(bf16[8,16,16,128]{3,2,1,0:T(8,128)(2,1)S(1)} %get-tuple-, ...), custom_call_target="tpu_custom_call" | custom-call | flops 1811939328 | bytes 8388608 | tf_op jit(solution)/shard_map/pallas_call | solution.py:19
  20.7 0.0 copy-start.6
  20.7 0.8 %copy-done.6 = bf16[8,16,16,128]{3,2,1,0:T(8,128)(2,1)} copy-done((bf16[8,16,16,128]{3,2,1,0:T(8,128)(2,1)}, bf16[8,16,16,128]{3,2,1,0:T(8,128)(2,1)S(1)}, u32[]{:S(2)}) %copy-start.6) | copy-done | bytes 524312
  21.5 3.3 %collective-permute-start.7 = (f32[4,27,16,128]{3,2,1,0:T(8,128)S(1)}, f32[4,27,16,128]{3,2,1,0:T(8,128)S(1)}, u32[]{:S(2)}, u32[]{:S(2)}) collective-permute-start(f32[4,27,16,128]{3,2,1,0:T(8,128)S(1)} %get-tuple-element.87), channel_id=1, source_target_pairs={{0,1},{1,0},{2,3},{3,2},{4,5},{5,4},{6,7},{7,6},{8,9},{9,8},{10,11... | collective-permute-start | bytes 2654216 | tf_op jit(solution)/shard_map/ppermute | solution.py:444
  24.7 0.0 collective-permute-start.6
  24.7 2.0 %collective-permute-done.7.came_b = f32[4,27,16,128]{3,2,1,0:T(8,128)S(1)} collective-permute-done((f32[4,27,16,128]{3,2,1,0:T(8,128)S(1)}, f32[4,27,16,128]{3,2,1,0:T(8,128)S(1)}, u32[]{:S(2)}, u32[]{:S(2)}) %collective-permute-start.7) | collective-permute-done | bytes 884768 | tf_op jit(solution)/shard_map/ppermute | solution.py:444
  26.8 1.3 %collective-permute-done.6.came_a = f32[4,27,16,128]{3,2,1,0:T(8,128)S(1)} collective-permute-done((f32[4,27,16,128]{3,2,1,0:T(8,128)S(1)}, f32[4,27,16,128]{3,2,1,0:T(8,128)S(1)}, u32[]{:S(2)}, u32[]{:S(2)}) %collective-permute-start.6) | collective-permute-done | bytes 884768 | tf_op jit(solution)/shard_map/ppermute | solution.py:444
  28.1 0.9 %shard_map.90 = (f32[2,432,128]{2,1,0:T(8,128)S(1)}, bf16[2,432,128]{2,1,0:T(8,128)(2,1)}, bf16[2,432,128]{2,1,0:T(8,128)(2,1)}, bf16[2,432,128]{2,1,0:T(8,128)(2,1)}) custom-call(f32[4,27,16,128]{3,2,1,0:T(8,128)S(1)} %get-tuple-element.84.keep_a, f32[4,27,16,128]{3,2,1,0:T(8,128)S(1)} %get-tuple-element.85.keep_b, ...), custom_call_target="tpu_custom_call" | custom-call | bytes 4194304 | tf_op jit(solution)/shard_map/pallas_call | solution.py:19
  29.0 0.0 copy-start.1
  29.0 2.1 %collective-permute-start.10 = (bf16[2,432,128]{2,1,0:T(8,128)(2,1)}, bf16[2,432,128]{2,1,0:T(8,128)(2,1)}, u32[]{:S(2)}, u32[]{:S(2)}) collective-permute-start(bf16[2,432,128]{2,1,0:T(8,128)(2,1)} %get-tuple-element.95), channel_id=1, source_target_pairs={{0,2},{1,3},{2,0},{3,1},{4,6},{5,7},{6,4},{7,5},{8,10},{9,11},{10,... | collective-permute-start | bytes 663560 | tf_op jit(solution)/shard_map/ppermute | solution.py:444
  31.1 0.6 collective-permute-start.11
  31.7 1.1 %collective-permute-start.12 = (bf16[2,432,128]{2,1,0:T(8,128)(2,1)}, bf16[2,432,128]{2,1,0:T(8,128)(2,1)}, u32[]{:S(2)}, u32[]{:S(2)}) collective-permute-start(bf16[2,432,128]{2,1,0:T(8,128)(2,1)} %get-tuple-element.97), channel_id=1, source_target_pairs={{0,6},{1,7},{2,4},{3,5},{4,2},{5,3},{6,0},{7,1},{8,14},{9,15},{10,... | collective-permute-start | bytes 663560 | tf_op jit(solution)/shard_map/ppermute | solution.py:444
  32.8 4.4 %collective-permute-start.4 = (bf16[2,16,16,128]{3,2,1,0:T(8,128)(2,1)}, bf16[2,16,16,128]{3,2,1,0:T(8,128)(2,1)S(1)}, u32[]{:S(2)}, u32[]{:S(2)}) collective-permute-start(bf16[2,16,16,128]{3,2,1,0:T(8,128)(2,1)} %get-tuple-element.82), channel_id=1, source_target_pairs={{0,8},{8,0},{16,24},{24,16},{1,9},{9,1},{17,25},{25,17},{2,10},{10... | collective-permute-start | bytes 393224 | tf_op jit(solution)/shard_map/ppermute | solution.py:136
  37.2 0.7 collective-permute-start.5
  37.9 2.8 %collective-permute-done.4.xa = bf16[2,16,16,128]{3,2,1,0:T(8,128)(2,1)S(1)} collective-permute-done((bf16[2,16,16,128]{3,2,1,0:T(8,128)(2,1)}, bf16[2,16,16,128]{3,2,1,0:T(8,128)(2,1)S(1)}, u32[]{:S(2)}, u32[]{:S(2)}) %collective-permute-start.4) | collective-permute-done | bytes 131104 | tf_op jit(solution)/shard_map/ppermute | solution.py:136
  40.6 0.0 collective-permute-done.5.xb
  40.7 0.1 collective-permute-start.8
  40.7 0.8 %collective-permute-start.9 = (bf16[2,10,16,128]{3,2,1,0:T(8,128)(2,1)S(1)}, bf16[2,10,16,128]{3,2,1,0:T(8,128)(2,1)S(1)}, u32[]{:S(2)}, u32[]{:S(2)}) collective-permute-start(bf16[2,10,16,128]{3,2,1,0:T(8,128)(2,1)S(1)} %get-tuple-element.94), channel_id=1, source_target_pairs={{0,0},{7,7},{1,2},{3,4},{5,6},{2,1},{4,3},{6,5},{8,8},{15,15},{9,1... | collective-permute-start | bytes 245768 | tf_op jit(solution)/shard_map/ppermute | solution.py:141
  41.6 0.0 collective-permute-done.10
  41.6 2.0 %collective-permute-done.11 = bf16[2,432,128]{2,1,0:T(8,128)(2,1)} collective-permute-done((bf16[2,432,128]{2,1,0:T(8,128)(2,1)}, bf16[2,432,128]{2,1,0:T(8,128)(2,1)}, u32[]{:S(2)}, u32[]{:S(2)}) %collective-permute-start.11) | collective-permute-done | bytes 221216 | tf_op jit(solution)/shard_map/ppermute | solution.py:444
  43.6 0.0 collective-permute-done.12
  43.6 1.2 %convert_add_fusion = f32[2,432,128]{2,1,0:T(8,128)S(1)} fusion(bf16[2,432,128]{2,1,0:T(8,128)(2,1)} %collective-permute-done.12, bf16[2,432,128]{2,1,0:T(8,128)(2,1)} %collective-permute-done.11, f32[2,432,128]{2,1,0:T(8,128)S(1)} %get-tuple-element.88, bf16[2,432,128]{2,1,0:T(8,128)(2,1)} %collective-permute-done.10), kind=kLoop, calls=%fused_computation | loop fusion | flops 663552 | bytes 1548288 | tf_op jit(solution)/shard_map/add | solution.py:490
  44.8 0.0 copy-start.5
  44.9 0.0 copy-start.7
  44.9 4.5 %collective-permute-start.13 = (f32[432,128]{1,0:T(8,128)S(1)}, f32[432,128]{1,0:T(8,128)S(1)}, u32[]{:S(2)}, u32[]{:S(2)}) collective-permute-start(f32[432,128]{1,0:T(8,128)S(1)} %select_bitcast_fusion), channel_id=1, source_target_pairs={{0,8},{8,0},{16,24},{24,16},{1,9},{9,1},{17,25},{25,17},{2,10},{10... | collective-permute-start | bytes 663560 | tf_op jit(solution)/shard_map/ppermute | solution.py:444
  49.3 0.0 collective-permute-done.8.ya
  49.3 0.0 collective-permute-done.9.yb
  49.3 0.0 copy-done.1
  49.3 3.6 %shard_map.92 = bf16[8,16,16,128]{3,2,1,0:T(8,128)(2,1)} custom-call(f32[1,256,128]{2,1,0:T(8,128)S(1)} %get-tuple-element.68.mask, bf16[8,16,16,128]{3,2,1,0:T(8,128)(2,1)S(1)} %copy-done.1, bf16[8,16,16,128]{3,2,1,0:T(8,128)(2,1)S(1)} %get-tuple-element.77.hidden.field, bf16[2,16,16,128]{3,2,1,0:T(8,128)(2,1)S(1)} %collective-permute-done.4.xa, ...), custom_call_target="tpu_custom_call" | custom-call | flops 1811939328 | bytes 3145728 | tf_op jit(solution)/shard_map/pallas_call | solution.py:19
  53.0 2.2 %collective-permute-done.13 = f32[432,128]{1,0:T(8,128)S(1)} collective-permute-done((f32[432,128]{1,0:T(8,128)S(1)}, f32[432,128]{1,0:T(8,128)S(1)}, u32[]{:S(2)}, u32[]{:S(2)}) %collective-permute-start.13) | collective-permute-done | bytes 221216 | tf_op jit(solution)/shard_map/ppermute | solution.py:444
  55.2 1.5 %collective-permute-start.14 = (f32[432,128]{1,0:T(8,128)S(1)}, f32[432,128]{1,0:T(8,128)S(1)}, u32[]{:S(2)}, u32[]{:S(2)}) collective-permute-start(f32[432,128]{1,0:T(8,128)S(1)} %bitcast_add_fusion), channel_id=1, source_target_pairs={{0,16},{8,24},{16,0},{24,8},{1,17},{9,25},{17,1},{25,9},{2,18},{10... | collective-permute-start | bytes 663560 | tf_op jit(solution)/shard_map/ppermute | solution.py:444
  56.7 0.0 copy-done.5
  56.7 0.0 copy-done.7
  56.7 3.6 %shard_map.93 = bf16[8,16,16,128]{3,2,1,0:T(8,128)(2,1)} custom-call(f32[1,256,128]{2,1,0:T(8,128)S(1)} %get-tuple-element.68.mask, bf16[8,16,16,128]{3,2,1,0:T(8,128)(2,1)S(1)} %copy-done.2, bf16[8,16,16,128]{3,2,1,0:T(8,128)(2,1)S(1)} %copy-done.7, bf16[2,16,16,128]{3,2,1,0:T(8,128)(2,1)S(1)} %collective-permute-done.4.xa, ...), custom_call_target="tpu_custom_call" | custom-call | flops 1811939328 | bytes 3145728 | tf_op jit(solution)/shard_map/pallas_call | solution.py:19
  60.3 7.7 %collective-permute-done.14 = f32[432,128]{1,0:T(8,128)S(1)} collective-permute-done((f32[432,128]{1,0:T(8,128)S(1)}, f32[432,128]{1,0:T(8,128)S(1)}, u32[]{:S(2)}, u32[]{:S(2)}) %collective-permute-start.14) | collective-permute-done | bytes 221216 | tf_op jit(solution)/shard_map/ppermute | solution.py:444
  68.0 0.1 collective-permute-start.15
  68.1 6.4 %collective-permute-done.15 = f32[432,128]{1,0:T(8,128)S(1)} collective-permute-done((f32[432,128]{1,0:T(8,128)S(1)}, f32[432,128]{1,0:T(8,128)S(1)}, u32[]{:S(2)}, u32[]{:S(2)}) %collective-permute-start.15) | collective-permute-done | bytes 221216 | tf_op jit(solution)/shard_map/ppermute | solution.py:444
  74.5 0.8 %select_multiply_fusion = (f32[432,128]{1,0:T(8,128)}, f32[432,128]{1,0:T(8,128)}) fusion(f32[432,128]{1,0:T(8,128)S(1)} %collective-permute-done.15, f32[432,128]{1,0:T(8,128)S(1)} %add.24, pred[]{:T(512)S(6)} %eq.5), kind=kLoop, calls=%fused_computation.2 | loop fusion | flops 221184 | bytes 884737 | tf_op jit(solution)/shard_map/mul | solution.py:509
  (5 shorter events, 0.2 us)
Async XLA Ops:
  1.8 8.8 %collective-permute-start = (bf16[2,16,16,128]{3,2,1,0:T(8,128)(2,1)S(1)}, bf16[2,16,16,128]{3,2,1,0:T(8,128)(2,1)S(1)}, u32[]{:S(2)}, u32[]{:S(2)}) collective-permute-start(bf16[2,16,16,128]{3,2,1,0:T(8,128)(2,1)S(1)} %get-tuple-element.59), channel_id=1, source_target_pairs={{0,8},{8,0},{16,24},{24,16},{1,9},{9,1},{17,25},{25,17},{2,10},{10... | collective-permute-start | bytes 393224 | tf_op jit(solution)/shard_map/ppermute | solution.py:136
  4.9 5.7 %collective-permute-start.1 = (bf16[2,16,16,128]{3,2,1,0:T(8,128)(2,1)S(1)}, bf16[2,16,16,128]{3,2,1,0:T(8,128)(2,1)S(1)}, u32[]{:S(2)}, u32[]{:S(2)}) collective-permute-start(bf16[2,16,16,128]{3,2,1,0:T(8,128)(2,1)S(1)} %get-tuple-element.60), channel_id=1, source_target_pairs={{0,0},{24,24},{8,16},{16,8},{1,1},{25,25},{9,17},{17,9},{2,2},{26,... | collective-permute-start | bytes 393224 | tf_op jit(solution)/shard_map/ppermute | solution.py:136
  5.5 1.0 %copy-start = (bf16[8,16,16,128]{3,2,1,0:T(8,128)(2,1)S(1)}, bf16[8,16,16,128]{3,2,1,0:T(8,128)(2,1)}, u32[]{:S(2)}) copy-start(bf16[8,16,16,128]{3,2,1,0:T(8,128)(2,1)} %own.2) | copy-start | bytes 1572868
  6.6 1.2 %copy-start.4 = (bf16[27,128,128]{2,1,0:T(8,128)(2,1)S(1)}, bf16[27,128,128]{2,1,0:T(8,128)(2,1)}, u32[]{:S(2)}) copy-start(bf16[27,128,128]{2,1,0:T(8,128)(2,1)} %w.7) | copy-start | bytes 2654212
  7.7 3.7 %copy-start.2 = (bf16[8,16,16,128]{3,2,1,0:T(8,128)(2,1)S(1)}, bf16[8,16,16,128]{3,2,1,0:T(8,128)(2,1)}, u32[]{:S(2)}) copy-start(bf16[8,16,16,128]{3,2,1,0:T(8,128)(2,1)} %own.3) | copy-start | bytes 1572868
  7.7 3.7 %copy-start.3 = (bf16[27,128,128]{2,1,0:T(8,128)(2,1)S(1)}, bf16[27,128,128]{2,1,0:T(8,128)(2,1)}, u32[]{:S(2)}) copy-start(bf16[27,128,128]{2,1,0:T(8,128)(2,1)} %w.6) | copy-start | bytes 2654212
  10.6 3.6 %collective-permute-start.2 = (bf16[2,10,16,128]{3,2,1,0:T(8,128)(2,1)S(1)}, bf16[2,10,16,128]{3,2,1,0:T(8,128)(2,1)S(1)}, u32[]{:S(2)}, u32[]{:S(2)}) collective-permute-start(bf16[2,10,16,128]{3,2,1,0:T(8,128)(2,1)S(1)} %get-tuple-element.66), channel_id=1, source_target_pairs={{0,1},{1,0},{2,3},{3,2},{4,5},{5,4},{6,7},{7,6},{8,9},{9,8},{10,11... | collective-permute-start | bytes 245768 | tf_op jit(solution)/shard_map/ppermute | solution.py:141
  10.7 3.5 %collective-permute-start.3 = (bf16[2,10,16,128]{3,2,1,0:T(8,128)(2,1)S(1)}, bf16[2,10,16,128]{3,2,1,0:T(8,128)(2,1)S(1)}, u32[]{:S(2)}, u32[]{:S(2)}) collective-permute-start(bf16[2,10,16,128]{3,2,1,0:T(8,128)(2,1)S(1)} %get-tuple-element.67), channel_id=1, source_target_pairs={{0,0},{7,7},{1,2},{3,4},{5,6},{2,1},{4,3},{6,5},{8,8},{15,15},{9,1... | collective-permute-start | bytes 245768 | tf_op jit(solution)/shard_map/ppermute | solution.py:141
  20.7 0.8 %copy-start.6 = (bf16[8,16,16,128]{3,2,1,0:T(8,128)(2,1)}, bf16[8,16,16,128]{3,2,1,0:T(8,128)(2,1)S(1)}, u32[]{:S(2)}) copy-start(bf16[8,16,16,128]{3,2,1,0:T(8,128)(2,1)S(1)} %get-tuple-element.105.field) | copy-start | bytes 1572868
  21.5 5.3 %collective-permute-start.7 = (f32[4,27,16,128]{3,2,1,0:T(8,128)S(1)}, f32[4,27,16,128]{3,2,1,0:T(8,128)S(1)}, u32[]{:S(2)}, u32[]{:S(2)}) collective-permute-start(f32[4,27,16,128]{3,2,1,0:T(8,128)S(1)} %get-tuple-element.87), channel_id=1, source_target_pairs={{0,1},{1,0},{2,3},{3,2},{4,5},{5,4},{6,7},{7,6},{8,9},{9,8},{10,11... | collective-permute-start | bytes 2654216 | tf_op jit(solution)/shard_map/ppermute | solution.py:444
  24.7 3.3 %collective-permute-start.6 = (f32[4,27,16,128]{3,2,1,0:T(8,128)S(1)}, f32[4,27,16,128]{3,2,1,0:T(8,128)S(1)}, u32[]{:S(2)}, u32[]{:S(2)}) collective-permute-start(f32[4,27,16,128]{3,2,1,0:T(8,128)S(1)} %get-tuple-element.86), channel_id=1, source_target_pairs={{0,1},{1,0},{2,3},{3,2},{4,5},{5,4},{6,7},{7,6},{8,9},{9,8},{10,11... | collective-permute-start | bytes 2654216 | tf_op jit(solution)/shard_map/ppermute | solution.py:444
  29.0 20.3 %copy-start.1 = (bf16[8,16,16,128]{3,2,1,0:T(8,128)(2,1)S(1)}, bf16[8,16,16,128]{3,2,1,0:T(8,128)(2,1)}, u32[]{:S(2)}) copy-start(bf16[8,16,16,128]{3,2,1,0:T(8,128)(2,1)} %own.2) | copy-start | bytes 1572868
  29.0 12.6 %collective-permute-start.10 = (bf16[2,432,128]{2,1,0:T(8,128)(2,1)}, bf16[2,432,128]{2,1,0:T(8,128)(2,1)}, u32[]{:S(2)}, u32[]{:S(2)}) collective-permute-start(bf16[2,432,128]{2,1,0:T(8,128)(2,1)} %get-tuple-element.95), channel_id=1, source_target_pairs={{0,2},{1,3},{2,0},{3,1},{4,6},{5,7},{6,4},{7,5},{8,10},{9,11},{10,... | collective-permute-start | bytes 663560 | tf_op jit(solution)/shard_map/ppermute | solution.py:444
  31.1 12.5 %collective-permute-start.11 = (bf16[2,432,128]{2,1,0:T(8,128)(2,1)}, bf16[2,432,128]{2,1,0:T(8,128)(2,1)}, u32[]{:S(2)}, u32[]{:S(2)}) collective-permute-start(bf16[2,432,128]{2,1,0:T(8,128)(2,1)} %get-tuple-element.96), channel_id=1, source_target_pairs={{0,4},{1,5},{2,6},{3,7},{4,0},{5,1},{6,2},{7,3},{8,12},{9,13},{10,... | collective-permute-start | bytes 663560 | tf_op jit(solution)/shard_map/ppermute | solution.py:444
  31.7 11.9 %collective-permute-start.12 = (bf16[2,432,128]{2,1,0:T(8,128)(2,1)}, bf16[2,432,128]{2,1,0:T(8,128)(2,1)}, u32[]{:S(2)}, u32[]{:S(2)}) collective-permute-start(bf16[2,432,128]{2,1,0:T(8,128)(2,1)} %get-tuple-element.97), channel_id=1, source_target_pairs={{0,6},{1,7},{2,4},{3,5},{4,2},{5,3},{6,0},{7,1},{8,14},{9,15},{10,... | collective-permute-start | bytes 663560 | tf_op jit(solution)/shard_map/ppermute | solution.py:444
  32.8 7.8 %collective-permute-start.4 = (bf16[2,16,16,128]{3,2,1,0:T(8,128)(2,1)}, bf16[2,16,16,128]{3,2,1,0:T(8,128)(2,1)S(1)}, u32[]{:S(2)}, u32[]{:S(2)}) collective-permute-start(bf16[2,16,16,128]{3,2,1,0:T(8,128)(2,1)} %get-tuple-element.82), channel_id=1, source_target_pairs={{0,8},{8,0},{16,24},{24,16},{1,9},{9,1},{17,25},{25,17},{2,10},{10... | collective-permute-start | bytes 393224 | tf_op jit(solution)/shard_map/ppermute | solution.py:136
  37.2 3.4 %collective-permute-start.5 = (bf16[2,16,16,128]{3,2,1,0:T(8,128)(2,1)S(1)}, bf16[2,16,16,128]{3,2,1,0:T(8,128)(2,1)S(1)}, u32[]{:S(2)}, u32[]{:S(2)}) collective-permute-start(bf16[2,16,16,128]{3,2,1,0:T(8,128)(2,1)S(1)} %get-tuple-element.83), channel_id=1, source_target_pairs={{0,0},{24,24},{8,16},{16,8},{1,1},{25,25},{9,17},{17,9},{2,2},{26,... | collective-permute-start | bytes 393224 | tf_op jit(solution)/shard_map/ppermute | solution.py:136
  40.7 8.7 %collective-permute-start.8 = (bf16[2,10,16,128]{3,2,1,0:T(8,128)(2,1)S(1)}, bf16[2,10,16,128]{3,2,1,0:T(8,128)(2,1)S(1)}, u32[]{:S(2)}, u32[]{:S(2)}) collective-permute-start(bf16[2,10,16,128]{3,2,1,0:T(8,128)(2,1)S(1)} %get-tuple-element.93), channel_id=1, source_target_pairs={{0,1},{1,0},{2,3},{3,2},{4,5},{5,4},{6,7},{7,6},{8,9},{9,8},{10,11... | collective-permute-start | bytes 245768 | tf_op jit(solution)/shard_map/ppermute | solution.py:141
  40.7 8.6 %collective-permute-start.9 = (bf16[2,10,16,128]{3,2,1,0:T(8,128)(2,1)S(1)}, bf16[2,10,16,128]{3,2,1,0:T(8,128)(2,1)S(1)}, u32[]{:S(2)}, u32[]{:S(2)}) collective-permute-start(bf16[2,10,16,128]{3,2,1,0:T(8,128)(2,1)S(1)} %get-tuple-element.94), channel_id=1, source_target_pairs={{0,0},{7,7},{1,2},{3,4},{5,6},{2,1},{4,3},{6,5},{8,8},{15,15},{9,1... | collective-permute-start | bytes 245768 | tf_op jit(solution)/shard_map/ppermute | solution.py:141
  44.8 11.8 %copy-start.5 = (bf16[27,128,128]{2,1,0:T(8,128)(2,1)S(1)}, bf16[27,128,128]{2,1,0:T(8,128)(2,1)}, u32[]{:S(2)}) copy-start(bf16[27,128,128]{2,1,0:T(8,128)(2,1)} %w.7) | copy-start | bytes 2654212
  44.9 11.8 %copy-start.7 = (bf16[8,16,16,128]{3,2,1,0:T(8,128)(2,1)S(1)}, bf16[8,16,16,128]{3,2,1,0:T(8,128)(2,1)}, u32[]{:S(2)}) copy-start(bf16[8,16,16,128]{3,2,1,0:T(8,128)(2,1)} %copy-done.6) | copy-start | bytes 1572868
  44.9 10.3 %collective-permute-start.13 = (f32[432,128]{1,0:T(8,128)S(1)}, f32[432,128]{1,0:T(8,128)S(1)}, u32[]{:S(2)}, u32[]{:S(2)}) collective-permute-start(f32[432,128]{1,0:T(8,128)S(1)} %select_bitcast_fusion), channel_id=1, source_target_pairs={{0,8},{8,0},{16,24},{24,16},{1,9},{9,1},{17,25},{25,17},{2,10},{10... | collective-permute-start | bytes 663560 | tf_op jit(solution)/shard_map/ppermute | solution.py:444
  55.2 12.8 %collective-permute-start.14 = (f32[432,128]{1,0:T(8,128)S(1)}, f32[432,128]{1,0:T(8,128)S(1)}, u32[]{:S(2)}, u32[]{:S(2)}) collective-permute-start(f32[432,128]{1,0:T(8,128)S(1)} %bitcast_add_fusion), channel_id=1, source_target_pairs={{0,16},{8,24},{16,0},{24,8},{1,17},{9,25},{17,1},{25,9},{2,18},{10... | collective-permute-start | bytes 663560 | tf_op jit(solution)/shard_map/ppermute | solution.py:444
  68.0 6.5 %collective-permute-start.15 = (f32[432,128]{1,0:T(8,128)S(1)}, f32[432,128]{1,0:T(8,128)S(1)}, u32[]{:S(2)}, u32[]{:S(2)}) collective-permute-start(f32[432,128]{1,0:T(8,128)S(1)} %add.24), channel_id=1, source_target_pairs={{0,8},{8,0},{16,24},{24,16},{1,9},{9,1},{17,25},{25,17},{2,10},{10... | collective-permute-start | bytes 663560 | tf_op jit(solution)/shard_map/ppermute | solution.py:444
where the time goes:
time: 75.7 us; the launch traced here: 75.3 us
  waiting for transfers between devices  24.4 us (32%)
  starting transfers between devices  23.5 us (31%)
  Pallas kernels  21.4 us (28%)
  local copies, waits for them, and re-layouts  3.02 us (4%)
  other arithmetic  2.13 us (3%)
  between operations  0.85 us (1%)
    ppermute x8, waiting for transfers between devices, swap(): return lax.ppermute(value.astype(travel), axis, pairs)  21.6 us
    pallas_call x10, Pallas kernels, call(): pl.pallas_call(kernel, out_shape=out_shapes, in_specs=list(spaces) + [VME...  21.4 us
    ppermute x8, starting transfers between devices, swap(): return lax.ppermute(value.astype(travel), axis, pairs)  13.1 us
    ppermute x4, starting transfers between devices, swap_sides(): return (lax.ppermute(xa, 'gx', even), lax.ppermute(xb, 'gx', odd))  8.8 us
    unnamed x16, local copies, waits for them, and re-layouts  3.02 us
    ppermute x4, waiting for transfers between devices, swap_sides(): return (lax.ppermute(xa, 'gx', even), lax.ppermute(xb, 'gx', odd))  2.78 us
    ppermute x4, starting transfers between devices, swap_columns(): return (lax.ppermute(ya, 'gy', even), lax.ppermute(yb, 'gy', odd))  1.65 us
  transfers between devices with their start and end apart: 16, of which 7 were waited for; matrix products, arithmetic and copies ran while one was open for 2% of the time, Pallas kernels for 17%

commit v1 on v0

--- a/solution.py
+++ b/solution.py
@@ -61,52 +61,66 @@
     return index % 2, one_if(index > 0), one_if(index < lax.axis_size(axis) - 1)
 
 
-def pack_sides(features, cotangent, occ):
+def pack_sides(features, cotangent, occ, w):
     size_x, size_y, size_z, channels = features.shape
     rows = size_y * size_z
 
-    def kernel(occ_hbm, first, second, mask, xa, xb, ya, yb, occ_ref, sem, occ_sem):
+    def kernel(occ_hbm, first, second, w_hbm, mask, xa, xb, ya, yb, own, weights, occ_ref, sem, occ_sem, own_sem, w_sem):
         odd_x, odd_y = lax.axis_index("gx") % 2, lax.axis_index("gy") % 2
         first_x = pick(odd_x, size_x - 1, 0)
         first_y = pick(odd_y, size_y - 1, 0)
         sides = ((xa, first_x), (xb, size_x - 1 - first_x))
         columns = ((ya, first_y), (yb, size_y - 1 - first_y))
         occ_copy = pltpu.make_async_copy(occ_hbm, occ_ref, occ_sem)
-        occ_copy.start()
+        own_copy = pltpu.make_async_copy(first, own, own_sem)
+        w_copy = pltpu.make_async_copy(w_hbm, weights, w_sem)
         copies = []
-        for f, ref in enumerate((first, second)):
-            for n, (out, x) in enumerate(sides):
-                copies.append(pltpu.make_async_copy(ref.at[x], out.at[f], sem.at[f, n]))
-            for n, (out, y) in enumerate(columns):
-                copies.append(pltpu.make_async_copy(ref.at[:, y], out.at[f], sem.at[f, 2 + n]))
-        for copy in copies:
+        for n, (out, x) in enumerate(sides):
+            copies.append(pltpu.make_async_copy(second.at[x], out.at[1], sem.at[n]))
+        for n, (out, y) in enumerate(columns):
+            copies.append(pltpu.make_async_copy(second.at[:, y], out.at[1], sem.at[2 + n]))
+        for copy in [occ_copy, own_copy, *copies, w_copy]:
             copy.start()
         occ_copy.wait()
         for n in range(size_x // BLOCK):
             mask[n] = plane_mask(occ_ref, n, size_y, size_z)
+        own_copy.wait()
+        for out, x in sides:
+            out[0] = own[x] * mask[x // BLOCK].astype(BF16).reshape(size_y, size_z, channels)
+        for out, y in columns:
+            at = pl.ds(pl.multiple_of(y * size_z, size_z), size_z)
+            for x in range(size_x):
+                out[0, x] = own[x, y] * mask[x // BLOCK, at, :].astype(BF16)
         for copy in copies:
             copy.wait()
         for out, x in sides:
-            here = mask[x // BLOCK].astype(BF16).reshape(size_y, size_z, channels)
-            for f in range(2):
-                out[f] = out[f] * here
+            out[1] = out[1] * mask[x // BLOCK].astype(BF16).reshape(size_y, size_z, channels)
         for out, y in columns:
             at = pl.ds(pl.multiple_of(y * size_z, size_z), size_z)
             for x in range(size_x):
-                here = mask[x // BLOCK, at, :].astype(BF16)
-                for f in range(2):
-                    out[f, x] = out[f, x] * here
+                out[1, x] = out[1, x] * mask[x // BLOCK, at, :].astype(BF16)
+        w_copy.wait()
 
     side = pltpu.VMEM((2, size_y, size_z, channels), BF16)
     column = pltpu.VMEM((2, size_x, size_z, channels), BF16)
     return call(
         kernel,
-        (pltpu.VMEM((size_x // BLOCK, rows, channels), F32), side, side, column, column),
-        [pltpu.with_memory_space_constraint(value, pltpu.HBM) for value in (occ, features, cotangent)],
-        [HBM] * 3,
+        (
+            pltpu.VMEM((size_x // BLOCK, rows, channels), F32),
+            side,
+            side,
+            column,
+            column,
+            pltpu.VMEM(features.shape, BF16),
+            pltpu.VMEM(w.shape, BF16),
+        ),
+        [pltpu.with_memory_space_constraint(value, pltpu.HBM) for value in (occ, features, cotangent, w)],
+        [HBM] * 4,
         scratch=[
             pltpu.SMEM(occ.shape, jnp.int32),
-            pltpu.SemaphoreType.DMA((2, 4)),
+            pltpu.SemaphoreType.DMA((4,)),
+            pltpu.SemaphoreType.DMA(()),
+            pltpu.SemaphoreType.DMA(()),
             pltpu.SemaphoreType.DMA(()),
         ],
         nbytes=MIB,
@@ -273,15 +287,15 @@
     return call(
         kernel,
         (
-            jax.ShapeDtypeStruct(field_shape(field.shape), BF16),
-            jax.ShapeDtypeStruct(taps_shape(channels), BF16),
-            jax.ShapeDtypeStruct((size_x, rows, channels), F32),
+            pltpu.VMEM(field_shape(field.shape), BF16),
+            pltpu.VMEM(taps_shape(channels), BF16),
+            pltpu.VMEM((size_x, rows, channels), F32),
         ),
         (mask, field, w),
         [],
         flops=2 * 27 * size_x * rows * channels * channels,
         nbytes=4 * MIB,
-        vmem=24 * MIB,
+        vmem=14 * MIB,
     )
 
 
@@ -369,7 +383,7 @@
         [],
         flops=2 * 27 * size_x * rows * channels * channels,
         nbytes=8 * MIB,
-        vmem=24 * MIB,
+        vmem=14 * MIB,
         aliases={7: 0, 8: 1},
     )
 
@@ -402,7 +416,7 @@
         scratch=[pltpu.VMEM(grad.shape, F32)],
         flops=2 * 27 * size_x * rows * channels * channels,
         nbytes=8 * MIB,
-        vmem=24 * MIB,
+        vmem=14 * MIB,
     )
 
 
@@ -431,7 +445,7 @@
         scratch=[pltpu.VMEM(field_shape(own.shape), BF16), pltpu.VMEM(taps_shape(channels), BF16)],
         flops=2 * 27 * size_x * rows * channels * channels,
         nbytes=3 * MIB,
-        vmem=24 * MIB,
+        vmem=14 * MIB,
     )
 
 
@@ -444,30 +458,54 @@
     return lax.ppermute(value.astype(travel), axis, pairs)
 
 
-def first_sums(keeps, cames):
-    places, taps, share, channels = keeps[0].shape
+def first_sum(g, keep, came, earlier):
+    places, taps, share, channels = keep.shape
     rows = taps * share
 
-    def kernel(keep_a, keep_b, came_a, came_b, stays, *leaves):
-        for g, (keep, came) in enumerate(((keep_a, came_a), (keep_b, came_b))):
-            for p in range(places):
-                value = (keep[p] + came[p]).reshape(rows, channels)
-                if p == 0:
-                    stays[g] = value
-                else:
-                    leaves[p - 1][g] = value.astype(BF16)
-
-    stay = jax.ShapeDtypeStruct((2, rows, channels), F32)
-    leave = jax.ShapeDtypeStruct((2, rows, channels), BF16)
-    return call(kernel, (stay,) + (leave,) * (places - 1), (*keeps, *cames), [], nbytes=4 * MIB, vmem=8 * MIB)
+    def kernel(keep, came, *refs):
+        stays, *leaves = refs[-places:]
+        for p in range(places):
+            value = (keep[p] + came[p]).reshape(rows, channels)
+            if p == 0:
+                stays[g] = value
+            else:
+                leaves[p - 1][g] = value.astype(BF16)
+
+    stay = pltpu.VMEM((2, rows, channels), F32)
+    leave = pltpu.VMEM((2, rows, channels), BF16)
+    return call(
+        kernel,
+        (stay,) + (leave,) * (places - 1),
+        (keep, came, *earlier),
+        [],
+        nbytes=2 * MIB,
+        vmem=4 * MIB,
+        aliases={2 + n: n for n in range(len(earlier))},
+    )
+
+
+def second_sum(stays, came):
+    _, rows, channels = stays.shape
+
+    def kernel(stays, *refs):
+        came, (stay, leave) = refs[:-2], refs[-2:]
+        odd = lax.axis_index("gx") % 2
+        for out, g in ((stay, odd), (leave, 1 - odd)):
+            value = stays[g]
+            for ref in came:
+                value += ref[g].astype(F32)
+            out[...] = value
+
+    shape = pltpu.VMEM((rows, channels), F32)
+    return call(kernel, (shape, shape), (stays, *came), [], nbytes=2 * MIB, vmem=4 * MIB)
 
 
 def body(features, w_first, w_second, occ, cotangent):
     count_x, count_y = lax.axis_size("gx"), lax.axis_size("gy")
     shape = features.shape
-    mask, xa, xb, ya, yb = pack_sides(features, cotangent, occ)
+    mask, xa, xb, ya, yb, own, weights = pack_sides(features, cotangent, occ, w_first)
     xa, xb = swap_sides(xa, xb)
-    zm, first_taps, pre = own_terms(mask, features, w_first, straight)
+    zm, first_taps, pre = own_terms(mask, own, weights, straight)
     xa, xb = after((xa, xb), pre)
     ya, yb = finish_columns(xa, xb, ya, yb)
     behind = after(mask, ya)
@@ -475,36 +513,44 @@
     zu, second_taps, grad = own_terms(behind, cotangent, w_second, turned)
     halos = after((xa, xb, ya, yb), grad)
     zm, zu, hidden, slope, keep_second, send = hidden_and_terms(mask, halos, zm, zu, first_taps, pre, shape)
-    came_second = swap(send, "gy", 1, F32)
+    came = swap(send, "gy", 1, F32)
     pre_grad, keep_first, send, xa, xb, ya, yb = pre_grad_and_terms(hidden, slope, zm, zu, second_taps, grad)
-    came_first = swap(send, "gy", 1, F32)
+
+    sums = first_sum(0, keep_second, after(came, pre_grad), ())
+    came = swap(send, "gy", 1, F32)
     xa, xb = swap_sides(xa, xb)
-
-    stays, *leaves = first_sums((keep_second, keep_first), (came_second, came_first))
+    stays, *leaves = first_sum(1, keep_first, after(came, sums[0]), sums)
     came = [swap(value, "gy", 2 * (p + 1), BF16) for p, value in enumerate(leaves)]
-    xa, xb = after((xa, xb), stays)
+    stays, leaves = second_sum(stays, after(came, xa, xb))
+    xa, xb = after((xa, xb), leaves)
+    came = swap(leaves, "gx", 1, F32)
     ya, yb = finish_columns(xa, xb, ya, yb)
     came = after(came, ya)
     ya, yb = swap_columns(ya, yb)
-    for value in came:
-        stays = stays + value.astype(F32)
-    odd = lax.axis_index("gx") % 2 == 1
-    leaves = jnp.where(odd, stays[0], stays[1])
-    stays = jnp.where(odd, stays[1], stays[0])
-    came = swap(leaves, "gx", 1, F32)
-    halos = after((xa, xb, ya, yb), leaves)
-    output = add_convolution(mask, features, hidden, 0, halos, w_second, straight)
-    stays = stays + after(came, output)
+    stays = stays + came
+    convolutions = [
+        (mask, features, hidden, 0, w_second, straight),
+        (mask, cotangent, pre_grad, 1, w_first, turned),
+    ]
+    results = []
+
+    def convolve_beside(came, behind):
+        if len(results) == len(convolutions):
+            return came
+        mask, own, field, f, w, lay = convolutions[len(results)]
+        halos = after((xa, xb, ya, yb), behind)
+        results.append(add_convolution(mask, own, field, f, halos, w, lay))
+        return after(came, results[-1])
+
     bit = 2
     while bit < count_x:
-        came = swap(stays, "gx", bit, F32)
-        if bit == 2:
-            halos = after((xa, xb, ya, yb), stays)
-            grad_features = add_convolution(mask, cotangent, pre_grad, 1, halos, w_first, turned)
-            came = after(came, grad_features)
-        stays = stays + came
+        own = stays.astype(BF16)
+        came = convolve_beside(swap(own, "gx", bit, BF16), own)
+        stays = own.astype(F32) + came.astype(F32)
         bit *= 2
-    came = swap(stays, "gx", 1, F32)
+    came = convolve_beside(swap(stays, "gx", 1, F32), stays)
+    output, grad_features = results
+    odd = lax.axis_index("gx") % 2 == 1
     factor = 1.0 / math.sqrt(count_x * count_y * shape[0] * shape[1] * shape[2])
     total_second = jnp.where(odd, came, stays) * factor
     total_first = jnp.where(odd, stays, came) * factor

time: 75.7 us -> 62.6 us (0.83)
  waiting for transfers between devices: 24.4 us -> 14.3 us
  local copies, waits for them, and re-layouts: 3.02 us -> 0.02 us
  starting transfers between devices: 23.5 us -> 25.9 us
  other arithmetic: 2.13 us -> 0.88 us
  Pallas kernels: 21.4 us -> 20.5 us
    ppermute x8, waiting for transfers between devices: 21.6 us -> 11.5 us  [swap(): return lax.ppermute(value.astype(travel), axis, pairs)]
    unnamed x16 -> x8, local copies, waits for them, and re-layouts: 3.02 us -> 0.02 us
    ppermute x8, starting transfers between devices: 13.1 us -> 15.2 us  [swap(): return lax.ppermute(value.astype(travel), axis, pairs)]
    add x3 -> x1, other arithmetic: 1.32 us -> 0.02 us  [body(): stays = own.astype(F32) + came.astype(F32)]
    pallas_call x10 -> x12, Pallas kernels: 21.4 us -> 20.5 us  [call(): pl.pallas_call(kernel, out_shape=out_shapes, in_specs=list(spaces) + [VME...]
  transfers between devices with their start and end apart: 16 -> 16, of which waited for: 7 -> 6; matrix products, arithmetic and copies ran while one was open for 2% -> 0% of each run, Pallas kernels for 17% -> 25%
where the time goes in v1:
time: 62.6 us; the launch traced here: 62.4 us
  starting transfers between devices  25.9 us (41%)
  Pallas kernels  20.5 us (33%)
  waiting for transfers between devices  14.3 us (23%)
  other arithmetic  0.88 us (1%)
  between operations  0.84 us (1%)
    pallas_call x12, Pallas kernels, call(): pl.pallas_call(kernel, out_shape=out_shapes, in_specs=list(spaces) + [VME...  20.5 us
    ppermute x8, starting transfers between devices, swap(): return lax.ppermute(value.astype(travel), axis, pairs)  15.2 us
    ppermute x8, waiting for transfers between devices, swap(): return lax.ppermute(value.astype(travel), axis, pairs)  11.5 us
    ppermute x4, starting transfers between devices, swap_sides(): return (lax.ppermute(xa, 'gx', even), lax.ppermute(xb, 'gx', odd))  9.01 us
    ppermute x4, waiting for transfers between devices, swap_sides(): return (lax.ppermute(xa, 'gx', even), lax.ppermute(xb, 'gx', odd))  2.8 us
    ppermute x4, starting transfers between devices, swap_columns(): return (lax.ppermute(ya, 'gy', even), lax.ppermute(yb, 'gy', odd))  1.65 us
  transfers between devices with their start and end apart: 16, of which 6 were waited for; matrix products, arithmetic and copies ran while one was open for 0% of the time, Pallas kernels for 25%

profile of v1, /device:TPU:0, one launch (start us, length us, event | category | flops | bytes accessed | tf_op | source)
XLA Modules:
  0.0 62.4 jit_solution(8177297159724660720)
XLA Ops:
  0.6 1.5 %shard_map.84 = (f32[1,256,128]{2,1,0:T(8,128)S(1)}, bf16[2,16,16,128]{3,2,1,0:T(8,128)(2,1)S(1)}, bf16[2,16,16,128]{3,2,1,0:T(8,128)(2,1)S(1)}, bf16[2,8,16,128...) custom-call(s32[1,2,2]{2,1,0:T(2,128)} %occ_hbm.1, ...), custom_call_target="tpu_custom_call" | custom-call | bytes 1048576 | tf_op jit(solution)/shard_map/pallas_call | solution.py:19
  2.2 3.1 %collective-permute-start = (bf16[2,16,16,128]{3,2,1,0:T(8,128)(2,1)S(1)}, bf16[2,16,16,128]{3,2,1,0:T(8,128)(2,1)S(1)}, u32[]{:S(2)}, u32[]{:S(2)}) collective-permute-start(bf16[2,16,16,128]{3,2,1,0:T(8,128)(2,1)S(1)} %get-tuple-element.70), channel_id=1, source_target_pairs={{0,8},{8,0},{16,24},{24,16},{1,9},{9,1},{17,25},{25,17},{2,10},{10... | collective-permute-start | bytes 393224 | tf_op jit(solution)/shard_map/ppermute | solution.py:150
  5.2 0.7 %collective-permute-start.1 = (bf16[2,16,16,128]{3,2,1,0:T(8,128)(2,1)S(1)}, bf16[2,16,16,128]{3,2,1,0:T(8,128)(2,1)S(1)}, u32[]{:S(2)}, u32[]{:S(2)}) collective-permute-start(bf16[2,16,16,128]{3,2,1,0:T(8,128)(2,1)S(1)} %get-tuple-element.71), channel_id=1, source_target_pairs={{0,0},{24,24},{8,16},{16,8},{1,1},{25,25},{9,17},{17,9},{2,2},{26,... | collective-permute-start | bytes 393224 | tf_op jit(solution)/shard_map/ppermute | solution.py:150
  5.9 0.0 copy-start.2
  5.9 0.0 copy-start.3
  5.9 2.8 %shard_map.85 = (bf16[10,18,16,384]{3,2,1,0:T(8,128)(2,1)S(1)}, bf16[12,384,256]{2,1,0:T(8,128)(2,1)S(1)}, f32[8,256,128]{2,1,0:T(8,128)S(1)}) custom-call(f32[1,256,128]{2,1,0:T(8,128)S(1)} %get-tuple-element.81.mask, bf16[8,16,16,128]{3,2,1,0:T(8,128)(2,1)S(1)} %get-tuple-element.72.field, bf16[27,128,128]{2,1,0:T(8,128)(2,1)S(1)} %get-tuple-element.73.w), custom_call_target="tpu_custom_call" | custom-call | flops 1811939328 | bytes 4194304 | tf_op jit(solution)/shard_map/pallas_call | solution.py:19
  8.8 0.0 collective-permute-done.xa
  8.8 0.0 collective-permute-done.1.xb
  8.8 0.1 collective-permute-start.2
  8.9 0.7 %collective-permute-start.3 = (bf16[2,10,16,128]{3,2,1,0:T(8,128)(2,1)S(1)}, bf16[2,10,16,128]{3,2,1,0:T(8,128)(2,1)S(1)}, u32[]{:S(2)}, u32[]{:S(2)}) collective-permute-start(bf16[2,10,16,128]{3,2,1,0:T(8,128)(2,1)S(1)} %get-tuple-element.80), channel_id=1, source_target_pairs={{0,0},{7,7},{1,2},{3,4},{5,6},{2,1},{4,3},{6,5},{8,8},{15,15},{9,1... | collective-permute-start | bytes 245768 | tf_op jit(solution)/shard_map/ppermute | solution.py:155
  9.6 0.0 copy-done.2
  9.6 0.0 copy-done.3
  9.6 2.8 %shard_map.87 = (bf16[10,18,16,384]{3,2,1,0:T(8,128)(2,1)S(1)}, bf16[12,384,256]{2,1,0:T(8,128)(2,1)S(1)}, f32[8,256,128]{2,1,0:T(8,128)S(1)}) custom-call(f32[1,256,128]{2,1,0:T(8,128)S(1)} %get-tuple-element.81.mask, bf16[8,16,16,128]{3,2,1,0:T(8,128)(2,1)S(1)} %copy-done.2, bf16[27,128,128]{2,1,0:T(8,128)(2,1)S(1)} %copy-done.3), custom_call_target="tpu_custom_call" | custom-call | flops 1811939328 | bytes 4194304 | tf_op jit(solution)/shard_map/pallas_call | solution.py:19
  12.4 0.0 collective-permute-done.2.ya
  12.5 0.0 collective-permute-done.3.yb
  12.5 2.9 %shard_map.88 = (bf16[10,18,16,384]{3,2,1,0:T(8,128)(2,1)S(1)}, bf16[10,18,16,384]{3,2,1,0:T(8,128)(2,1)S(1)}, bf16[8,16,16,128]{3,2,1,0:T(8,128)(2,1)S(1)}, f32...) custom-call(f32[1,256,128]{2,1,0:T(8,128)S(1)} %get-tuple-element.81, ...), custom_call_target="tpu_custom_call", output_to_operand_aliasing={{0}: (7, {}), {1}: (8, {})} | custom-call | flops 1811939328 | bytes 8388608 | tf_op jit(solution)/shard_map/pallas_call | solution.py:19
  15.4 3.3 %collective-permute-start.7 = (f32[4,27,16,128]{3,2,1,0:T(8,128)S(1)}, f32[4,27,16,128]{3,2,1,0:T(8,128)S(1)}, u32[]{:S(2)}, u32[]{:S(2)}) collective-permute-start(f32[4,27,16,128]{3,2,1,0:T(8,128)S(1)} %get-tuple-element.100), channel_id=1, source_target_pairs={{0,1},{1,0},{2,3},{3,2},{4,5},{5,4},{6,7},{7,6},{8,9},{9,8},{10,11... | collective-permute-start | bytes 2654216 | tf_op jit(solution)/shard_map/ppermute | solution.py:458
  18.7 2.9 %shard_map.89 = (bf16[8,16,16,128]{3,2,1,0:T(8,128)(2,1)S(1)}, f32[4,27,16,128]{3,2,1,0:T(8,128)S(1)}, f32[4,27,16,128]{3,2,1,0:T(8,128)S(1)}, bf16[2,16,16,128]...) custom-call(bf16[8,16,16,128]{3,2,1,0:T(8,128)(2,1)S(1)} %get-tuple-, ...), custom_call_target="tpu_custom_call" | custom-call | flops 1811939328 | bytes 8388608 | tf_op jit(solution)/shard_map/pallas_call | solution.py:19
  21.6 0.1 collective-permute-start.6
  21.7 0.0 collective-permute-done.7.came
  21.7 0.1 shard_map.90
  21.8 2.3 %collective-permute-done.6.came = f32[4,27,16,128]{3,2,1,0:T(8,128)S(1)} collective-permute-done((f32[4,27,16,128]{3,2,1,0:T(8,128)S(1)}, f32[4,27,16,128]{3,2,1,0:T(8,128)S(1)}, u32[]{:S(2)}, u32[]{:S(2)}) %collective-permute-start.6) | collective-permute-done | bytes 884768 | tf_op jit(solution)/shard_map/ppermute | solution.py:458
  24.1 0.0 copy-start.1
  24.1 0.1 shard_map.91
  24.2 2.0 %collective-permute-start.10 = (bf16[2,432,128]{2,1,0:T(8,128)(2,1)S(1)}, bf16[2,432,128]{2,1,0:T(8,128)(2,1)S(1)}, u32[]{:S(2)}, u32[]{:S(2)}) collective-permute-start(bf16[2,432,128]{2,1,0:T(8,128)(2,1)S(1)} %get-tuple-element.111), channel_id=1, source_target_pairs={{0,6},{1,7},{2,4},{3,5},{4,2},{5,3},{6,0},{7,1},{8,14},{9,15},{10,... | collective-permute-start | bytes 663560 | tf_op jit(solution)/shard_map/ppermute | solution.py:458
  26.2 1.6 %collective-permute-start.8 = (bf16[2,432,128]{2,1,0:T(8,128)(2,1)S(1)}, bf16[2,432,128]{2,1,0:T(8,128)(2,1)S(1)}, u32[]{:S(2)}, u32[]{:S(2)}) collective-permute-start(bf16[2,432,128]{2,1,0:T(8,128)(2,1)S(1)} %get-tuple-element.109), channel_id=1, source_target_pairs={{0,2},{1,3},{2,0},{3,1},{4,6},{5,7},{6,4},{7,5},{8,10},{9,11},{10,... | collective-permute-start | bytes 663560 | tf_op jit(solution)/shard_map/ppermute | solution.py:458
  27.8 0.1 collective-permute-start.9
  27.9 4.6 %collective-permute-start.4 = (bf16[2,16,16,128]{3,2,1,0:T(8,128)(2,1)S(1)}, bf16[2,16,16,128]{3,2,1,0:T(8,128)(2,1)S(1)}, u32[]{:S(2)}, u32[]{:S(2)}) collective-permute-start(bf16[2,16,16,128]{3,2,1,0:T(8,128)(2,1)S(1)} %get-tuple-element.95), channel_id=1, source_target_pairs={{0,8},{8,0},{16,24},{24,16},{1,9},{9,1},{17,25},{25,17},{2,10},{10... | collective-permute-start | bytes 393224 | tf_op jit(solution)/shard_map/ppermute | solution.py:150
  32.5 0.7 %collective-permute-start.5 = (bf16[2,16,16,128]{3,2,1,0:T(8,128)(2,1)S(1)}, bf16[2,16,16,128]{3,2,1,0:T(8,128)(2,1)S(1)}, u32[]{:S(2)}, u32[]{:S(2)}) collective-permute-start(bf16[2,16,16,128]{3,2,1,0:T(8,128)(2,1)S(1)} %get-tuple-element.96), channel_id=1, source_target_pairs={{0,0},{24,24},{8,16},{16,8},{1,1},{25,25},{9,17},{17,9},{2,2},{26,... | collective-permute-start | bytes 393224 | tf_op jit(solution)/shard_map/ppermute | solution.py:150
  33.2 2.8 %collective-permute-done.4.xa = bf16[2,16,16,128]{3,2,1,0:T(8,128)(2,1)S(1)} collective-permute-done((bf16[2,16,16,128]{3,2,1,0:T(8,128)(2,1)S(1)}, bf16[2,16,16,128]{3,2,1,0:T(8,128)(2,1)S(1)}, u32[]{:S(2)}, u32[]{:S(2)}) %collective-permute-start.4) | collective-permute-done | bytes 131104 | tf_op jit(solution)/shard_map/ppermute | solution.py:150
  36.0 0.0 collective-permute-done.5.xb
  36.0 0.0 collective-permute-done.10.refs_2_
  36.0 2.3 %collective-permute-done.8.refs_0_ = bf16[2,432,128]{2,1,0:T(8,128)(2,1)S(1)} collective-permute-done((bf16[2,432,128]{2,1,0:T(8,128)(2,1)S(1)}, bf16[2,432,128]{2,1,0:T(8,128)(2,1)S(1)}, u32[]{:S(2)}, u32[]{:S(2)}) %collective-permute-start.8) | collective-permute-done | bytes 221216 | tf_op jit(solution)/shard_map/ppermute | solution.py:458
  38.3 0.0 collective-permute-done.9.refs_1_
  38.3 0.1 shard_map.92
  38.4 4.8 %collective-permute-start.13 = (f32[432,128]{1,0:T(8,128)S(1)}, f32[432,128]{1,0:T(8,128)S(1)}, u32[]{:S(2)}, u32[]{:S(2)}) collective-permute-start(f32[432,128]{1,0:T(8,128)S(1)} %get-tuple-element.115), channel_id=1, source_target_pairs={{0,8},{8,0},{16,24},{24,16},{1,9},{9,1},{17,25},{25,17},{2,10},{10... | collective-permute-start | bytes 663560 | tf_op jit(solution)/shard_map/ppermute | solution.py:458
  43.2 0.1 collective-permute-start.11
  43.2 0.8 %collective-permute-start.12 = (bf16[2,10,16,128]{3,2,1,0:T(8,128)(2,1)S(1)}, bf16[2,10,16,128]{3,2,1,0:T(8,128)(2,1)S(1)}, u32[]{:S(2)}, u32[]{:S(2)}) collective-permute-start(bf16[2,10,16,128]{3,2,1,0:T(8,128)(2,1)S(1)} %get-tuple-element.121), channel_id=1, source_target_pairs={{0,0},{7,7},{1,2},{3,4},{5,6},{2,1},{4,3},{6,5},{8,8},{15,15},{9,1... | collective-permute-start | bytes 245768 | tf_op jit(solution)/shard_map/ppermute | solution.py:155
  44.1 4.2 %collective-permute-done.13 = f32[432,128]{1,0:T(8,128)S(1)} collective-permute-done((f32[432,128]{1,0:T(8,128)S(1)}, f32[432,128]{1,0:T(8,128)S(1)}, u32[]{:S(2)}, u32[]{:S(2)}) %collective-permute-start.13) | collective-permute-done | bytes 221216 | tf_op jit(solution)/shard_map/ppermute | solution.py:458
  48.3 0.0 copy-start
  48.3 3.0 %collective-permute-start.14 = (bf16[432,128]{1,0:T(8,128)(2,1)S(1)}, bf16[432,128]{1,0:T(8,128)(2,1)S(1)}, u32[]{:S(2)}, u32[]{:S(2)}) collective-permute-start(bf16[432,128]{1,0:T(8,128)(2,1)S(1)} %add_convert_fusion), channel_id=1, source_target_pairs={{0,16},{8,24},{16,0},{24,8},{1,17},{9,25},{17,1},{25,9},{2,18},{10... | collective-permute-start | bytes 331784 | tf_op jit(solution)/shard_map/ppermute | solution.py:458
  51.3 0.0 collective-permute-done.11.ya
  51.3 0.0 collective-permute-done.12.yb
  51.3 0.0 copy-done.1
  51.3 3.6 %shard_map.94 = bf16[8,16,16,128]{3,2,1,0:T(8,128)(2,1)} custom-call(f32[1,256,128]{2,1,0:T(8,128)S(1)} %get-tuple-element.81.mask, bf16[8,16,16,128]{3,2,1,0:T(8,128)(2,1)S(1)} %copy-done.1, bf16[8,16,16,128]{3,2,1,0:T(8,128)(2,1)S(1)} %get-tuple-element.90.hidden.field, bf16[2,16,16,128]{3,2,1,0:T(8,128)(2,1)S(1)} %collective-permute-done.4.xa, ...), custom_call_target="tpu_custom_call" | custom-call | flops 1811939328 | bytes 3145728 | tf_op jit(solution)/shard_map/pallas_call | solution.py:19
  54.9 0.6 %collective-permute-done.14 = bf16[432,128]{1,0:T(8,128)(2,1)S(1)} collective-permute-done((bf16[432,128]{1,0:T(8,128)(2,1)S(1)}, bf16[432,128]{1,0:T(8,128)(2,1)S(1)}, u32[]{:S(2)}, u32[]{:S(2)}) %collective-permute-start.14) | collective-permute-done | bytes 110624 | tf_op jit(solution)/shard_map/ppermute | solution.py:458
  55.6 0.4 collective-permute-start.15
  56.0 0.0 copy-done
  56.0 3.6 %shard_map.95 = bf16[8,16,16,128]{3,2,1,0:T(8,128)(2,1)} custom-call(f32[1,256,128]{2,1,0:T(8,128)S(1)} %get-tuple-element.81.mask, bf16[8,16,16,128]{3,2,1,0:T(8,128)(2,1)S(1)} %copy-done.2, bf16[8,16,16,128]{3,2,1,0:T(8,128)(2,1)S(1)} %get-tuple-element.101.field, bf16[2,16,16,128]{3,2,1,0:T(8,128)(2,1)S(1)} %collective-permute-done.4.xa, ...), custom_call_target="tpu_custom_call" | custom-call | flops 1811939328 | bytes 3145728 | tf_op jit(solution)/shard_map/pallas_call | solution.py:19
  59.6 2.0 %collective-permute-done.15 = f32[432,128]{1,0:T(8,128)S(1)} collective-permute-done((f32[432,128]{1,0:T(8,128)S(1)}, f32[432,128]{1,0:T(8,128)S(1)}, u32[]{:S(2)}, u32[]{:S(2)}) %collective-permute-start.15) | collective-permute-done | bytes 221216 | tf_op jit(solution)/shard_map/ppermute | solution.py:458
  61.6 0.8 %select_multiply_fusion = (f32[432,128]{1,0:T(8,128)}, f32[432,128]{1,0:T(8,128)}) fusion(f32[432,128]{1,0:T(8,128)S(1)} %collective-permute-done.15, pred[]{:T(512)S(6)} %eq.5, bf16[432,128]{1,0:T(8,128)(2,1)S(1)} %collective-permute-done.14, bf16[432,128]{1,0:T(8,128)(2,1)S(1)} %add_convert_fusion), kind=kLoop, calls=%fused_computation | loop fusion | flops 387072 | bytes 884737 | tf_op jit(solution)/shard_map/mul | solution.py:555
  (4 shorter events, 0.1 us)
Async XLA Ops:
  2.2 6.6 %collective-permute-start = (bf16[2,16,16,128]{3,2,1,0:T(8,128)(2,1)S(1)}, bf16[2,16,16,128]{3,2,1,0:T(8,128)(2,1)S(1)}, u32[]{:S(2)}, u32[]{:S(2)}) collective-permute-start(bf16[2,16,16,128]{3,2,1,0:T(8,128)(2,1)S(1)} %get-tuple-element.70), channel_id=1, source_target_pairs={{0,8},{8,0},{16,24},{24,16},{1,9},{9,1},{17,25},{25,17},{2,10},{10... | collective-permute-start | bytes 393224 | tf_op jit(solution)/shard_map/ppermute | solution.py:150
  5.2 3.6 %collective-permute-start.1 = (bf16[2,16,16,128]{3,2,1,0:T(8,128)(2,1)S(1)}, bf16[2,16,16,128]{3,2,1,0:T(8,128)(2,1)S(1)}, u32[]{:S(2)}, u32[]{:S(2)}) collective-permute-start(bf16[2,16,16,128]{3,2,1,0:T(8,128)(2,1)S(1)} %get-tuple-element.71), channel_id=1, source_target_pairs={{0,0},{24,24},{8,16},{16,8},{1,1},{25,25},{9,17},{17,9},{2,2},{26,... | collective-permute-start | bytes 393224 | tf_op jit(solution)/shard_map/ppermute | solution.py:150
  5.9 3.7 %copy-start.2 = (bf16[8,16,16,128]{3,2,1,0:T(8,128)(2,1)S(1)}, bf16[8,16,16,128]{3,2,1,0:T(8,128)(2,1)}, u32[]{:S(2)}) copy-start(bf16[8,16,16,128]{3,2,1,0:T(8,128)(2,1)} %own.3) | copy-start | bytes 1572868
  5.9 3.7 %copy-start.3 = (bf16[27,128,128]{2,1,0:T(8,128)(2,1)S(1)}, bf16[27,128,128]{2,1,0:T(8,128)(2,1)}, u32[]{:S(2)}) copy-start(bf16[27,128,128]{2,1,0:T(8,128)(2,1)} %w.4) | copy-start | bytes 2654212
  8.8 3.6 %collective-permute-start.2 = (bf16[2,10,16,128]{3,2,1,0:T(8,128)(2,1)S(1)}, bf16[2,10,16,128]{3,2,1,0:T(8,128)(2,1)S(1)}, u32[]{:S(2)}, u32[]{:S(2)}) collective-permute-start(bf16[2,10,16,128]{3,2,1,0:T(8,128)(2,1)S(1)} %get-tuple-element.79), channel_id=1, source_target_pairs={{0,1},{1,0},{2,3},{3,2},{4,5},{5,4},{6,7},{7,6},{8,9},{9,8},{10,11... | collective-permute-start | bytes 245768 | tf_op jit(solution)/shard_map/ppermute | solution.py:155
  8.9 3.5 %collective-permute-start.3 = (bf16[2,10,16,128]{3,2,1,0:T(8,128)(2,1)S(1)}, bf16[2,10,16,128]{3,2,1,0:T(8,128)(2,1)S(1)}, u32[]{:S(2)}, u32[]{:S(2)}) collective-permute-start(bf16[2,10,16,128]{3,2,1,0:T(8,128)(2,1)S(1)} %get-tuple-element.80), channel_id=1, source_target_pairs={{0,0},{7,7},{1,2},{3,4},{5,6},{2,1},{4,3},{6,5},{8,8},{15,15},{9,1... | collective-permute-start | bytes 245768 | tf_op jit(solution)/shard_map/ppermute | solution.py:155
  15.4 6.3 %collective-permute-start.7 = (f32[4,27,16,128]{3,2,1,0:T(8,128)S(1)}, f32[4,27,16,128]{3,2,1,0:T(8,128)S(1)}, u32[]{:S(2)}, u32[]{:S(2)}) collective-permute-start(f32[4,27,16,128]{3,2,1,0:T(8,128)S(1)} %get-tuple-element.100), channel_id=1, source_target_pairs={{0,1},{1,0},{2,3},{3,2},{4,5},{5,4},{6,7},{7,6},{8,9},{9,8},{10,11... | collective-permute-start | bytes 2654216 | tf_op jit(solution)/shard_map/ppermute | solution.py:458
  21.6 2.5 %collective-permute-start.6 = (f32[4,27,16,128]{3,2,1,0:T(8,128)S(1)}, f32[4,27,16,128]{3,2,1,0:T(8,128)S(1)}, u32[]{:S(2)}, u32[]{:S(2)}) collective-permute-start(f32[4,27,16,128]{3,2,1,0:T(8,128)S(1)} %get-tuple-element.98), channel_id=1, source_target_pairs={{0,1},{1,0},{2,3},{3,2},{4,5},{5,4},{6,7},{7,6},{8,9},{9,8},{10,11... | collective-permute-start | bytes 2654216 | tf_op jit(solution)/shard_map/ppermute | solution.py:458
  24.1 27.2 %copy-start.1 = (bf16[8,16,16,128]{3,2,1,0:T(8,128)(2,1)S(1)}, bf16[8,16,16,128]{3,2,1,0:T(8,128)(2,1)}, u32[]{:S(2)}) copy-start(bf16[8,16,16,128]{3,2,1,0:T(8,128)(2,1)} %own.2) | copy-start | bytes 1572868
  24.2 11.8 %collective-permute-start.10 = (bf16[2,432,128]{2,1,0:T(8,128)(2,1)S(1)}, bf16[2,432,128]{2,1,0:T(8,128)(2,1)S(1)}, u32[]{:S(2)}, u32[]{:S(2)}) collective-permute-start(bf16[2,432,128]{2,1,0:T(8,128)(2,1)S(1)} %get-tuple-element.111), channel_id=1, source_target_pairs={{0,6},{1,7},{2,4},{3,5},{4,2},{5,3},{6,0},{7,1},{8,14},{9,15},{10,... | collective-permute-start | bytes 663560 | tf_op jit(solution)/shard_map/ppermute | solution.py:458
  26.2 12.0 %collective-permute-start.8 = (bf16[2,432,128]{2,1,0:T(8,128)(2,1)S(1)}, bf16[2,432,128]{2,1,0:T(8,128)(2,1)S(1)}, u32[]{:S(2)}, u32[]{:S(2)}) collective-permute-start(bf16[2,432,128]{2,1,0:T(8,128)(2,1)S(1)} %get-tuple-element.109), channel_id=1, source_target_pairs={{0,2},{1,3},{2,0},{3,1},{4,6},{5,7},{6,4},{7,5},{8,10},{9,11},{10,... | collective-permute-start | bytes 663560 | tf_op jit(solution)/shard_map/ppermute | solution.py:458
  27.8 10.5 %collective-permute-start.9 = (bf16[2,432,128]{2,1,0:T(8,128)(2,1)S(1)}, bf16[2,432,128]{2,1,0:T(8,128)(2,1)S(1)}, u32[]{:S(2)}, u32[]{:S(2)}) collective-permute-start(bf16[2,432,128]{2,1,0:T(8,128)(2,1)S(1)} %get-tuple-element.110), channel_id=1, source_target_pairs={{0,4},{1,5},{2,6},{3,7},{4,0},{5,1},{6,2},{7,3},{8,12},{9,13},{10,... | collective-permute-start | bytes 663560 | tf_op jit(solution)/shard_map/ppermute | solution.py:458
  27.9 8.1 %collective-permute-start.4 = (bf16[2,16,16,128]{3,2,1,0:T(8,128)(2,1)S(1)}, bf16[2,16,16,128]{3,2,1,0:T(8,128)(2,1)S(1)}, u32[]{:S(2)}, u32[]{:S(2)}) collective-permute-start(bf16[2,16,16,128]{3,2,1,0:T(8,128)(2,1)S(1)} %get-tuple-element.95), channel_id=1, source_target_pairs={{0,8},{8,0},{16,24},{24,16},{1,9},{9,1},{17,25},{25,17},{2,10},{10... | collective-permute-start | bytes 393224 | tf_op jit(solution)/shard_map/ppermute | solution.py:150
  32.5 3.5 %collective-permute-start.5 = (bf16[2,16,16,128]{3,2,1,0:T(8,128)(2,1)S(1)}, bf16[2,16,16,128]{3,2,1,0:T(8,128)(2,1)S(1)}, u32[]{:S(2)}, u32[]{:S(2)}) collective-permute-start(bf16[2,16,16,128]{3,2,1,0:T(8,128)(2,1)S(1)} %get-tuple-element.96), channel_id=1, source_target_pairs={{0,0},{24,24},{8,16},{16,8},{1,1},{25,25},{9,17},{17,9},{2,2},{26,... | collective-permute-start | bytes 393224 | tf_op jit(solution)/shard_map/ppermute | solution.py:150
  38.4 9.9 %collective-permute-start.13 = (f32[432,128]{1,0:T(8,128)S(1)}, f32[432,128]{1,0:T(8,128)S(1)}, u32[]{:S(2)}, u32[]{:S(2)}) collective-permute-start(f32[432,128]{1,0:T(8,128)S(1)} %get-tuple-element.115), channel_id=1, source_target_pairs={{0,8},{8,0},{16,24},{24,16},{1,9},{9,1},{17,25},{25,17},{2,10},{10... | collective-permute-start | bytes 663560 | tf_op jit(solution)/shard_map/ppermute | solution.py:458
  43.2 8.1 %collective-permute-start.11 = (bf16[2,10,16,128]{3,2,1,0:T(8,128)(2,1)S(1)}, bf16[2,10,16,128]{3,2,1,0:T(8,128)(2,1)S(1)}, u32[]{:S(2)}, u32[]{:S(2)}) collective-permute-start(bf16[2,10,16,128]{3,2,1,0:T(8,128)(2,1)S(1)} %get-tuple-element.120), channel_id=1, source_target_pairs={{0,1},{1,0},{2,3},{3,2},{4,5},{5,4},{6,7},{7,6},{8,9},{9,8},{10,11... | collective-permute-start | bytes 245768 | tf_op jit(solution)/shard_map/ppermute | solution.py:155
  43.2 8.1 %collective-permute-start.12 = (bf16[2,10,16,128]{3,2,1,0:T(8,128)(2,1)S(1)}, bf16[2,10,16,128]{3,2,1,0:T(8,128)(2,1)S(1)}, u32[]{:S(2)}, u32[]{:S(2)}) collective-permute-start(bf16[2,10,16,128]{3,2,1,0:T(8,128)(2,1)S(1)} %get-tuple-element.121), channel_id=1, source_target_pairs={{0,0},{7,7},{1,2},{3,4},{5,6},{2,1},{4,3},{6,5},{8,8},{15,15},{9,1... | collective-permute-start | bytes 245768 | tf_op jit(solution)/shard_map/ppermute | solution.py:155
  48.3 7.7 %copy-start = (bf16[27,128,128]{2,1,0:T(8,128)(2,1)S(1)}, bf16[27,128,128]{2,1,0:T(8,128)(2,1)}, u32[]{:S(2)}) copy-start(bf16[27,128,128]{2,1,0:T(8,128)(2,1)} %w.5) | copy-start | bytes 2654212
  48.3 7.3 %collective-permute-start.14 = (bf16[432,128]{1,0:T(8,128)(2,1)S(1)}, bf16[432,128]{1,0:T(8,128)(2,1)S(1)}, u32[]{:S(2)}, u32[]{:S(2)}) collective-permute-start(bf16[432,128]{1,0:T(8,128)(2,1)S(1)} %add_convert_fusion), channel_id=1, source_target_pairs={{0,16},{8,24},{16,0},{24,8},{1,17},{9,25},{17,1},{25,9},{2,18},{10... | collective-permute-start | bytes 331784 | tf_op jit(solution)/shard_map/ppermute | solution.py:458
  55.6 6.0 %collective-permute-start.15 = (f32[432,128]{1,0:T(8,128)S(1)}, f32[432,128]{1,0:T(8,128)S(1)}, u32[]{:S(2)}, u32[]{:S(2)}) collective-permute-start(f32[432,128]{1,0:T(8,128)S(1)} %convert_add_fusion), channel_id=1, source_target_pairs={{0,8},{8,0},{16,24},{24,16},{1,9},{9,1},{17,25},{25,17},{2,10},{10... | collective-permute-start | bytes 663560 | tf_op jit(solution)/shard_map/ppermute | solution.py:458

commit v2 on v1

--- a/solution.py
+++ b/solution.py
@@ -28,12 +28,19 @@
     )(*args)
 
 
-def swap_pairs(count, odd):
-    if not odd:
-        return [(i, i ^ 1) for i in range(count)]
-    ends = [(0, 0), (count - 1, count - 1)]
-    inner = [(i, i + 1) for i in range(1, count - 1, 2)]
-    return ends + inner + [(b, a) for a, b in inner]
+def swap_pairs(axis, odd):
+    count_x, count_y = lax.axis_size("gx"), lax.axis_size("gy")
+    pairs = []
+    for x in range(count_x):
+        for y in range(count_y):
+            at, count = (x, count_x) if axis == "gx" else (y, count_y)
+            to = at - 1 if (at % 2 == 0) == odd else at + 1
+            if not 0 <= to < count:
+                other = (x, y ^ 1) if axis == "gx" else (x ^ 1, y)
+            else:
+                other = (to, y) if axis == "gx" else (x, to)
+            pairs.append((x * count_y + y, other[0] * count_y + other[1]))
+    return pairs
 
 
 def plane_mask(occ, block_x, size_y, size_z):
@@ -145,14 +152,10 @@
     return call(kernel, (shape, shape), (got_xa, got_xb, ya, yb), [], nbytes=MIB, vmem=4 * MIB)
 
 
-def swap_sides(xa, xb):
-    even, odd = (swap_pairs(lax.axis_size("gx"), which) for which in (False, True))
-    return lax.ppermute(xa, "gx", even), lax.ppermute(xb, "gx", odd)
-
-
-def swap_columns(ya, yb):
-    even, odd = (swap_pairs(lax.axis_size("gy"), which) for which in (False, True))
-    return lax.ppermute(ya, "gy", even), lax.ppermute(yb, "gy", odd)
+def swap_neighbours(axis, first, second):
+    return tuple(
+        lax.ppermute(value, ("gx", "gy"), swap_pairs(axis, odd)) for value, odd in ((first, False), (second, True))
+    )
 
 
 def store_shifts(zc, x, ys, rows):
@@ -453,9 +456,8 @@
     return lax.optimization_barrier((values, others))[0]
 
 
-def swap(value, axis, bit, travel):
-    pairs = [(i, i ^ bit) for i in range(lax.axis_size(axis))]
-    return lax.ppermute(value.astype(travel), axis, pairs)
+def swap(value, axis, bit):
+    return lax.ppermute(value, axis, [(i, i ^ bit) for i in range(lax.axis_size(axis))])
 
 
 def first_sum(g, keep, came, earlier):
@@ -484,50 +486,100 @@
     )
 
 
-def second_sum(stays, came):
+CODE_ROWS = 16
+CODE_TOP = 32000.0
+
+
+def encode(value, out):
+    most = jnp.max(jnp.max(jnp.abs(value), axis=0, keepdims=True), axis=1, keepdims=True)
+    power = jnp.ceil(jnp.log2(jnp.clip(most, 2.0**-100, 2.0**100)))
+    power = jnp.broadcast_to(power, (1, value.shape[1]))
+    head = jnp.broadcast_to(power, (CODE_ROWS, value.shape[1]))
+    out[:CODE_ROWS] = head.astype(jnp.int32).astype(jnp.int16)
+    scaled = value * (CODE_TOP * jnp.exp2(-power))
+    out[CODE_ROWS:] = jnp.round(scaled).astype(jnp.int32).astype(jnp.int16)
+
+
+def decode(ref):
+    power = ref[:CODE_ROWS].astype(jnp.int32).astype(F32)[:1]
+    return ref[CODE_ROWS:].astype(jnp.int32).astype(F32) * (jnp.exp2(power) * (1.0 / CODE_TOP))
+
+
+def coded_shape(rows, channels):
+    return pltpu.VMEM((CODE_ROWS + rows, channels), jnp.int16)
+
+
+def second_sums(stays, came):
     _, rows, channels = stays.shape
 
     def kernel(stays, *refs):
         came, (stay, leave) = refs[:-2], refs[-2:]
         odd = lax.axis_index("gx") % 2
-        for out, g in ((stay, odd), (leave, 1 - odd)):
+
+        def total(g):
             value = stays[g]
             for ref in came:
                 value += ref[g].astype(F32)
-            out[...] = value
-
-    shape = pltpu.VMEM((rows, channels), F32)
-    return call(kernel, (shape, shape), (stays, *came), [], nbytes=2 * MIB, vmem=4 * MIB)
+            return value
+
+        stay[...] = total(odd)
+        encode(total(1 - odd), leave)
+
+    outs = (pltpu.VMEM((rows, channels), F32), coded_shape(rows, channels))
+    return call(kernel, outs, (stays, *came), [], nbytes=2 * MIB, vmem=4 * MIB)
+
+
+def next_sum(own, came):
+    rows, channels = came.shape[0] - CODE_ROWS, came.shape[1]
+    coded = own.dtype != F32
+
+    def kernel(own, came, out):
+        encode((decode(own) if coded else own[...]) + decode(came), out)
+
+    return call(kernel, coded_shape(rows, channels), (own, came), [], nbytes=MIB, vmem=4 * MIB)
+
+
+def final_grads(own, came, taps, factor):
+    rows, channels = came.shape[0] - CODE_ROWS, came.shape[1]
+
+    def kernel(own, came, second, first):
+        odd = lax.axis_index("gx") % 2
+        mine, other = decode(own) * factor, decode(came) * factor
+        second[...] = pick(odd, mine, other).reshape(second.shape)
+        first[...] = pick(odd, other, mine).reshape(first.shape)
+
+    shape = jax.ShapeDtypeStruct((taps, rows // taps, channels), F32)
+    return call(kernel, (shape, shape), (own, came), [], nbytes=MIB, vmem=4 * MIB)
 
 
 def body(features, w_first, w_second, occ, cotangent):
     count_x, count_y = lax.axis_size("gx"), lax.axis_size("gy")
     shape = features.shape
     mask, xa, xb, ya, yb, own, weights = pack_sides(features, cotangent, occ, w_first)
-    xa, xb = swap_sides(xa, xb)
+    xa, xb = swap_neighbours("gx", xa, xb)
     zm, first_taps, pre = own_terms(mask, own, weights, straight)
     xa, xb = after((xa, xb), pre)
     ya, yb = finish_columns(xa, xb, ya, yb)
     behind = after(mask, ya)
-    ya, yb = swap_columns(ya, yb)
+    ya, yb = swap_neighbours("gy", ya, yb)
     zu, second_taps, grad = own_terms(behind, cotangent, w_second, turned)
     halos = after((xa, xb, ya, yb), grad)
     zm, zu, hidden, slope, keep_second, send = hidden_and_terms(mask, halos, zm, zu, first_taps, pre, shape)
-    came = swap(send, "gy", 1, F32)
+    came = swap(send, "gy", 1)
     pre_grad, keep_first, send, xa, xb, ya, yb = pre_grad_and_terms(hidden, slope, zm, zu, second_taps, grad)
 
     sums = first_sum(0, keep_second, after(came, pre_grad), ())
-    came = swap(send, "gy", 1, F32)
-    xa, xb = swap_sides(xa, xb)
+    came = swap(send, "gy", 1)
+    xa, xb = swap_neighbours("gx", xa, xb)
     stays, *leaves = first_sum(1, keep_first, after(came, sums[0]), sums)
-    came = [swap(value, "gy", 2 * (p + 1), BF16) for p, value in enumerate(leaves)]
-    stays, leaves = second_sum(stays, after(came, xa, xb))
+    came = [swap(value, "gy", 2 * (p + 1)) for p, value in enumerate(leaves)]
+    stays, leaves = second_sums(stays, after(came, xa, xb))
     xa, xb = after((xa, xb), leaves)
-    came = swap(leaves, "gx", 1, F32)
+    came = swap(leaves, "gx", 1)
     ya, yb = finish_columns(xa, xb, ya, yb)
     came = after(came, ya)
-    ya, yb = swap_columns(ya, yb)
-    stays = stays + came
+    ya, yb = swap_neighbours("gy", ya, yb)
+    stays = next_sum(stays, came)
     convolutions = [
         (mask, features, hidden, 0, w_second, straight),
         (mask, cotangent, pre_grad, 1, w_first, turned),
@@ -544,18 +596,13 @@
 
     bit = 2
     while bit < count_x:
-        own = stays.astype(BF16)
-        came = convolve_beside(swap(own, "gx", bit, BF16), own)
-        stays = own.astype(F32) + came.astype(F32)
+        stays = next_sum(stays, convolve_beside(swap(stays, "gx", bit), stays))
         bit *= 2
-    came = convolve_beside(swap(stays, "gx", 1, F32), stays)
+    came = convolve_beside(swap(stays, "gx", 1), stays)
+    factor = 1.0 / math.sqrt(count_x * count_y * shape[0] * shape[1] * shape[2])
+    grad_second, grad_first = final_grads(stays, came, w_first.shape[0], factor)
     output, grad_features = results
-    odd = lax.axis_index("gx") % 2 == 1
-    factor = 1.0 / math.sqrt(count_x * count_y * shape[0] * shape[1] * shape[2])
-    total_second = jnp.where(odd, came, stays) * factor
-    total_first = jnp.where(odd, stays, came) * factor
-    kernel_shape = (27, -1, shape[3])
-    return output, grad_features, total_first.reshape(kernel_shape), total_second.reshape(kernel_shape)
+    return output, grad_features, grad_first, grad_second
 
 
 def solution(mesh):

time: 62.6 us -> 55.9 us (0.89)
  starting transfers between devices: 25.9 us -> 19.6 us
  Pallas kernels: 20.5 us -> 22 us
  waiting for transfers between devices: 14.3 us -> 13.4 us
  other arithmetic: 0.88 us -> 0 us
    ppermute x16, starting transfers between devices: 25.9 us -> 19.6 us  [the longest x8 10.7 us: swap(): lax.ppermute(value, axis, [(i, i ^ bit) for i in range(lax.axis_size(axis...]
    pallas_call x12 -> x15, Pallas kernels: 20.5 us -> 22 us  [call(): pl.pallas_call(kernel, out_shape=out_shapes, in_specs=list(spaces) + [VME...]
    ppermute x16, waiting for transfers between devices: 14.3 us -> 13.4 us  [the longest x8 9.45 us: swap(): lax.ppermute(value, axis, [(i, i ^ bit) for i in range(lax.axis_size(axis...]
    mul x1 -> x0, other arithmetic: 0.82 us -> none  [body(): total_second = jnp.where(odd, came, stays) * factor]
  transfers between devices with their start and end apart: 16 -> 16, of which waited for: 6 -> 7; matrix products, arithmetic and copies ran while one was open for 0% -> 0% of each run, Pallas kernels for 25% -> 29%
where the time goes in v2:
time: 55.9 us; the launch traced here: 55.8 us
  Pallas kernels  22 us (39%)
  starting transfers between devices  19.6 us (35%)
  waiting for transfers between devices  13.4 us (24%)
  between operations  0.77 us (1%)
    pallas_call x15, Pallas kernels, call(): pl.pallas_call(kernel, out_shape=out_shapes, in_specs=list(spaces) + [VME...  22 us
    ppermute x8, starting transfers between devices, swap(): lax.ppermute(value, axis, [(i, i ^ bit) for i in range(lax.axis_size(axis...  10.7 us
    ppermute x8, waiting for transfers between devices, swap(): lax.ppermute(value, axis, [(i, i ^ bit) for i in range(lax.axis_size(axis...  9.45 us
    ppermute x8, starting transfers between devices, swap_neighbours(): lax.ppermute(value, ('gx', 'gy'), swap_pairs(axis, odd))  8.81 us
    ppermute x8, waiting for transfers between devices, swap_neighbours(): lax.ppermute(value, ('gx', 'gy'), swap_pairs(axis, odd))  3.99 us
  transfers between devices with their start and end apart: 16, of which 7 were waited for; matrix products, arithmetic and copies ran while one was open for 0% of the time, Pallas kernels for 29%

profile of v2, /device:TPU:0, one launch (start us, length us, event | category | flops | bytes accessed | tf_op | source)
XLA Modules:
  0.0 55.8 jit_solution(17777466544014094075)
XLA Ops:
  0.6 1.5 %shard_map.84 = (f32[1,256,128]{2,1,0:T(8,128)S(1)}, bf16[2,16,16,128]{3,2,1,0:T(8,128)(2,1)S(1)}, bf16[2,16,16,128]{3,2,1,0:T(8,128)(2,1)S(1)}, bf16[2,8,16,128...) custom-call(s32[1,2,2]{2,1,0:T(2,128)} %occ_hbm.1, ...), custom_call_target="tpu_custom_call" | custom-call | bytes 1048576 | tf_op jit(solution)/shard_map/pallas_call | solution.py:19
  2.2 3.1 %collective-permute-start = (bf16[2,16,16,128]{3,2,1,0:T(8,128)(2,1)S(1)}, bf16[2,16,16,128]{3,2,1,0:T(8,128)(2,1)S(1)}, u32[]{:S(2)}, u32[]{:S(2)}) collective-permute-start(bf16[2,16,16,128]{3,2,1,0:T(8,128)(2,1)S(1)} %get-tuple-element.72), channel_id=1, source_target_pairs={{0,8},{1,9},{2,10},{3,11},{4,12},{5,13},{6,14},{7,15},{8,0},{9,1},... | collective-permute-start | bytes 393224 | tf_op jit(solution)/shard_map/ppermute | solution.py:157
  5.2 0.0 collective-permute-start.1
  5.2 0.0 copy-start.2
  5.3 0.0 copy-start.3
  5.3 2.8 %shard_map.85 = (bf16[10,18,16,384]{3,2,1,0:T(8,128)(2,1)S(1)}, bf16[12,384,256]{2,1,0:T(8,128)(2,1)S(1)}, f32[8,256,128]{2,1,0:T(8,128)S(1)}) custom-call(f32[1,256,128]{2,1,0:T(8,128)S(1)} %get-tuple-element.83.mask, bf16[8,16,16,128]{3,2,1,0:T(8,128)(2,1)S(1)} %get-tuple-element.74.field, bf16[27,128,128]{2,1,0:T(8,128)(2,1)S(1)} %get-tuple-element.75.w), custom_call_target="tpu_custom_call" | custom-call | flops 1811939328 | bytes 4194304 | tf_op jit(solution)/shard_map/pallas_call | solution.py:19
  8.1 0.6 %collective-permute-done.xa = bf16[2,16,16,128]{3,2,1,0:T(8,128)(2,1)S(1)} collective-permute-done((bf16[2,16,16,128]{3,2,1,0:T(8,128)(2,1)S(1)}, bf16[2,16,16,128]{3,2,1,0:T(8,128)(2,1)S(1)}, u32[]{:S(2)}, u32[]{:S(2)}) %collective-permute-start) | collective-permute-done | bytes 131104 | tf_op jit(solution)/shard_map/ppermute | solution.py:157
  8.7 0.0 collective-permute-done.1.xb
  8.8 0.1 collective-permute-start.2
  8.9 2.9 %collective-permute-start.3 = (bf16[2,10,16,128]{3,2,1,0:T(8,128)(2,1)S(1)}, bf16[2,10,16,128]{3,2,1,0:T(8,128)(2,1)S(1)}, u32[]{:S(2)}, u32[]{:S(2)}) collective-permute-start(bf16[2,10,16,128]{3,2,1,0:T(8,128)(2,1)S(1)} %get-tuple-element.82), channel_id=1, source_target_pairs={{0,8},{1,2},{2,1},{3,4},{4,3},{5,6},{6,5},{7,15},{8,0},{9,10},{10,... | collective-permute-start | bytes 245768 | tf_op jit(solution)/shard_map/ppermute | solution.py:157
  11.8 0.0 copy-done.2
  11.8 0.0 copy-done.3
  11.8 2.8 %shard_map.87 = (bf16[10,18,16,384]{3,2,1,0:T(8,128)(2,1)S(1)}, bf16[12,384,256]{2,1,0:T(8,128)(2,1)S(1)}, f32[8,256,128]{2,1,0:T(8,128)S(1)}) custom-call(f32[1,256,128]{2,1,0:T(8,128)S(1)} %get-tuple-element.83.mask, bf16[8,16,16,128]{3,2,1,0:T(8,128)(2,1)S(1)} %copy-done.2, bf16[27,128,128]{2,1,0:T(8,128)(2,1)S(1)} %copy-done.3), custom_call_target="tpu_custom_call" | custom-call | flops 1811939328 | bytes 4194304 | tf_op jit(solution)/shard_map/pallas_call | solution.py:19
  14.6 0.0 collective-permute-done.3.yb
  14.6 0.0 collective-permute-done.2.ya
  14.6 2.9 %shard_map.88 = (bf16[10,18,16,384]{3,2,1,0:T(8,128)(2,1)S(1)}, bf16[10,18,16,384]{3,2,1,0:T(8,128)(2,1)S(1)}, bf16[8,16,16,128]{3,2,1,0:T(8,128)(2,1)S(1)}, f32...) custom-call(f32[1,256,128]{2,1,0:T(8,128)S(1)} %get-tuple-element.83, ...), custom_call_target="tpu_custom_call", output_to_operand_aliasing={{0}: (7, {}), {1}: (8, {})} | custom-call | flops 1811939328 | bytes 8388608 | tf_op jit(solution)/shard_map/pallas_call | solution.py:19
  17.6 0.1 collective-permute-start.7
  17.6 2.9 %shard_map.89 = (bf16[8,16,16,128]{3,2,1,0:T(8,128)(2,1)S(1)}, f32[4,27,16,128]{3,2,1,0:T(8,128)S(1)}, f32[4,27,16,128]{3,2,1,0:T(8,128)S(1)}, bf16[2,16,16,128]...) custom-call(bf16[8,16,16,128]{3,2,1,0:T(8,128)(2,1)S(1)} %get-tuple-, ...), custom_call_target="tpu_custom_call" | custom-call | flops 1811939328 | bytes 8388608 | tf_op jit(solution)/shard_map/pallas_call | solution.py:19
  20.5 0.6 collective-permute-start.6
  21.1 0.0 collective-permute-done.7.came
  21.1 0.1 shard_map.90
  21.2 2.0 %collective-permute-done.6.came = f32[4,27,16,128]{3,2,1,0:T(8,128)S(1)} collective-permute-done((f32[4,27,16,128]{3,2,1,0:T(8,128)S(1)}, f32[4,27,16,128]{3,2,1,0:T(8,128)S(1)}, u32[]{:S(2)}, u32[]{:S(2)}) %collective-permute-start.6) | collective-permute-done | bytes 884768 | tf_op jit(solution)/shard_map/ppermute | solution.py:460
  23.1 0.0 copy-start.1
  23.1 0.1 shard_map.91
  23.2 1.4 %collective-permute-start.8 = (bf16[2,432,128]{2,1,0:T(8,128)(2,1)S(1)}, bf16[2,432,128]{2,1,0:T(8,128)(2,1)S(1)}, u32[]{:S(2)}, u32[]{:S(2)}) collective-permute-start(bf16[2,432,128]{2,1,0:T(8,128)(2,1)S(1)} %get-tuple-element.111), channel_id=1, source_target_pairs={{0,2},{1,3},{2,0},{3,1},{4,6},{5,7},{6,4},{7,5},{8,10},{9,11},{10,... | collective-permute-start | bytes 663560 | tf_op jit(solution)/shard_map/ppermute | solution.py:460
  24.6 1.7 %collective-permute-start.9 = (bf16[2,432,128]{2,1,0:T(8,128)(2,1)S(1)}, bf16[2,432,128]{2,1,0:T(8,128)(2,1)S(1)}, u32[]{:S(2)}, u32[]{:S(2)}) collective-permute-start(bf16[2,432,128]{2,1,0:T(8,128)(2,1)S(1)} %get-tuple-element.112), channel_id=1, source_target_pairs={{0,4},{1,5},{2,6},{3,7},{4,0},{5,1},{6,2},{7,3},{8,12},{9,13},{10,... | collective-permute-start | bytes 663560 | tf_op jit(solution)/shard_map/ppermute | solution.py:460
  26.3 0.5 collective-permute-start.10
  26.8 2.1 %collective-permute-start.4 = (bf16[2,16,16,128]{3,2,1,0:T(8,128)(2,1)S(1)}, bf16[2,16,16,128]{3,2,1,0:T(8,128)(2,1)S(1)}, u32[]{:S(2)}, u32[]{:S(2)}) collective-permute-start(bf16[2,16,16,128]{3,2,1,0:T(8,128)(2,1)S(1)} %get-tuple-element.97), channel_id=1, source_target_pairs={{0,8},{1,9},{2,10},{3,11},{4,12},{5,13},{6,14},{7,15},{8,0},{9,1},... | collective-permute-start | bytes 393224 | tf_op jit(solution)/shard_map/ppermute | solution.py:157
  28.9 0.0 collective-permute-start.5
  28.9 3.3 %collective-permute-done.4.xa = bf16[2,16,16,128]{3,2,1,0:T(8,128)(2,1)S(1)} collective-permute-done((bf16[2,16,16,128]{3,2,1,0:T(8,128)(2,1)S(1)}, bf16[2,16,16,128]{3,2,1,0:T(8,128)(2,1)S(1)}, u32[]{:S(2)}, u32[]{:S(2)}) %collective-permute-start.4) | collective-permute-done | bytes 131104 | tf_op jit(solution)/shard_map/ppermute | solution.py:157
  32.2 0.0 collective-permute-done.5.xb
  32.2 0.0 collective-permute-done.8.refs_0_
  32.2 4.3 %collective-permute-done.9.refs_1_ = bf16[2,432,128]{2,1,0:T(8,128)(2,1)S(1)} collective-permute-done((bf16[2,432,128]{2,1,0:T(8,128)(2,1)S(1)}, bf16[2,432,128]{2,1,0:T(8,128)(2,1)S(1)}, u32[]{:S(2)}, u32[]{:S(2)}) %collective-permute-start.9) | collective-permute-done | bytes 221216 | tf_op jit(solution)/shard_map/ppermute | solution.py:460
  36.5 0.0 collective-permute-done.10.refs_2_
  36.5 0.2 shard_map.92
  36.8 2.8 %collective-permute-start.13 = (s16[448,128]{1,0:T(8,128)(2,1)S(1)}, s16[448,128]{1,0:T(8,128)(2,1)S(1)}, u32[]{:S(2)}, u32[]{:S(2)}) collective-permute-start(s16[448,128]{1,0:T(8,128)(2,1)S(1)} %get-tuple-element.117), channel_id=1, source_target_pairs={{0,8},{8,0},{16,24},{24,16},{1,9},{9,1},{17,25},{25,17},{2,10},{10... | collective-permute-start | bytes 344072 | tf_op jit(solution)/shard_map/ppermute | solution.py:460
  39.6 0.1 collective-permute-start.12
  39.7 0.6 %collective-permute-start.11 = (bf16[2,10,16,128]{3,2,1,0:T(8,128)(2,1)S(1)}, bf16[2,10,16,128]{3,2,1,0:T(8,128)(2,1)S(1)}, u32[]{:S(2)}, u32[]{:S(2)}) collective-permute-start(bf16[2,10,16,128]{3,2,1,0:T(8,128)(2,1)S(1)} %get-tuple-element.122), channel_id=1, source_target_pairs={{0,1},{1,0},{2,3},{3,2},{4,5},{5,4},{6,7},{7,6},{8,9},{9,8},{10,11... | collective-permute-start | bytes 245768 | tf_op jit(solution)/shard_map/ppermute | solution.py:157
  40.2 2.1 %collective-permute-done.13.came = s16[448,128]{1,0:T(8,128)(2,1)S(1)} collective-permute-done((s16[448,128]{1,0:T(8,128)(2,1)S(1)}, s16[448,128]{1,0:T(8,128)(2,1)S(1)}, u32[]{:S(2)}, u32[]{:S(2)}) %collective-permute-start.13) | collective-permute-done | bytes 114720 | tf_op jit(solution)/shard_map/ppermute | solution.py:460
  42.3 0.2 shard_map.94.own
  42.5 0.0 copy-start
  42.5 3.2 %collective-permute-start.14 = (s16[448,128]{1,0:T(8,128)(2,1)S(1)}, s16[448,128]{1,0:T(8,128)(2,1)S(1)}, u32[]{:S(2)}, u32[]{:S(2)}) collective-permute-start(s16[448,128]{1,0:T(8,128)(2,1)S(1)} %shard_map.94.own), channel_id=1, source_target_pairs={{0,16},{8,24},{16,0},{24,8},{1,17},{9,25},{17,1},{25,9},{2,18},{10... | collective-permute-start | bytes 344072 | tf_op jit(solution)/shard_map/ppermute | solution.py:460
  45.8 0.0 collective-permute-done.12.yb
  45.8 0.0 collective-permute-done.11.ya
  45.8 0.0 copy-done.1
  45.8 3.8 %shard_map.95 = bf16[8,16,16,128]{3,2,1,0:T(8,128)(2,1)} custom-call(f32[1,256,128]{2,1,0:T(8,128)S(1)} %get-tuple-element.83.mask, bf16[8,16,16,128]{3,2,1,0:T(8,128)(2,1)S(1)} %copy-done.1, bf16[8,16,16,128]{3,2,1,0:T(8,128)(2,1)S(1)} %get-tuple-element.92.hidden.field, bf16[2,16,16,128]{3,2,1,0:T(8,128)(2,1)S(1)} %collective-permute-done.4.xa, ...), custom_call_target="tpu_custom_call" | custom-call | flops 1811939328 | bytes 3145728 | tf_op jit(solution)/shard_map/pallas_call | solution.py:19
  49.6 0.3 collective-permute-done.14.came
  49.9 0.2 shard_map.96.own
  50.1 0.5 collective-permute-start.15
  50.6 0.0 copy-done
  50.6 3.6 %shard_map.97 = bf16[8,16,16,128]{3,2,1,0:T(8,128)(2,1)} custom-call(f32[1,256,128]{2,1,0:T(8,128)S(1)} %get-tuple-element.83.mask, bf16[8,16,16,128]{3,2,1,0:T(8,128)(2,1)S(1)} %copy-done.2, bf16[8,16,16,128]{3,2,1,0:T(8,128)(2,1)S(1)} %get-tuple-element.103.field, bf16[2,16,16,128]{3,2,1,0:T(8,128)(2,1)S(1)} %collective-permute-done.4.xa, ...), custom_call_target="tpu_custom_call" | custom-call | flops 1811939328 | bytes 3145728 | tf_op jit(solution)/shard_map/pallas_call | solution.py:19
  54.2 0.7 %collective-permute-done.15.came = s16[448,128]{1,0:T(8,128)(2,1)S(1)} collective-permute-done((s16[448,128]{1,0:T(8,128)(2,1)S(1)}, s16[448,128]{1,0:T(8,128)(2,1)S(1)}, u32[]{:S(2)}, u32[]{:S(2)}) %collective-permute-start.15) | collective-permute-done | bytes 114720 | tf_op jit(solution)/shard_map/ppermute | solution.py:460
  54.9 0.8 %shard_map.98 = (f32[27,16,128]{2,1,0:T(8,128)}, f32[27,16,128]{2,1,0:T(8,128)}) custom-call(s16[448,128]{1,0:T(8,128)(2,1)S(1)} %shard_map.96.own, s16[448,128]{1,0:T(8,128)(2,1)S(1)} %collective-permute-done.15.came), custom_call_target="tpu_custom_call" | custom-call | bytes 1048576 | tf_op jit(solution)/shard_map/pallas_call | solution.py:19
  (2 shorter events, 0.1 us)
Async XLA Ops:
  2.2 6.6 %collective-permute-start = (bf16[2,16,16,128]{3,2,1,0:T(8,128)(2,1)S(1)}, bf16[2,16,16,128]{3,2,1,0:T(8,128)(2,1)S(1)}, u32[]{:S(2)}, u32[]{:S(2)}) collective-permute-start(bf16[2,16,16,128]{3,2,1,0:T(8,128)(2,1)S(1)} %get-tuple-element.72), channel_id=1, source_target_pairs={{0,8},{1,9},{2,10},{3,11},{4,12},{5,13},{6,14},{7,15},{8,0},{9,1},... | collective-permute-start | bytes 393224 | tf_op jit(solution)/shard_map/ppermute | solution.py:157
  5.2 3.5 %collective-permute-start.1 = (bf16[2,16,16,128]{3,2,1,0:T(8,128)(2,1)S(1)}, bf16[2,16,16,128]{3,2,1,0:T(8,128)(2,1)S(1)}, u32[]{:S(2)}, u32[]{:S(2)}) collective-permute-start(bf16[2,16,16,128]{3,2,1,0:T(8,128)(2,1)S(1)} %get-tuple-element.73), channel_id=1, source_target_pairs={{0,1},{1,0},{2,3},{3,2},{4,5},{5,4},{6,7},{7,6},{8,16},{9,17},{10,... | collective-permute-start | bytes 393224 | tf_op jit(solution)/shard_map/ppermute | solution.py:157
  5.2 6.5 %copy-start.2 = (bf16[8,16,16,128]{3,2,1,0:T(8,128)(2,1)S(1)}, bf16[8,16,16,128]{3,2,1,0:T(8,128)(2,1)}, u32[]{:S(2)}) copy-start(bf16[8,16,16,128]{3,2,1,0:T(8,128)(2,1)} %own.3) | copy-start | bytes 1572868
  5.3 6.5 %copy-start.3 = (bf16[27,128,128]{2,1,0:T(8,128)(2,1)S(1)}, bf16[27,128,128]{2,1,0:T(8,128)(2,1)}, u32[]{:S(2)}) copy-start(bf16[27,128,128]{2,1,0:T(8,128)(2,1)} %w.4) | copy-start | bytes 2654212
  8.8 5.8 %collective-permute-start.2 = (bf16[2,10,16,128]{3,2,1,0:T(8,128)(2,1)S(1)}, bf16[2,10,16,128]{3,2,1,0:T(8,128)(2,1)S(1)}, u32[]{:S(2)}, u32[]{:S(2)}) collective-permute-start(bf16[2,10,16,128]{3,2,1,0:T(8,128)(2,1)S(1)} %get-tuple-element.81), channel_id=1, source_target_pairs={{0,1},{1,0},{2,3},{3,2},{4,5},{5,4},{6,7},{7,6},{8,9},{9,8},{10,11... | collective-permute-start | bytes 245768 | tf_op jit(solution)/shard_map/ppermute | solution.py:157
  8.9 5.8 %collective-permute-start.3 = (bf16[2,10,16,128]{3,2,1,0:T(8,128)(2,1)S(1)}, bf16[2,10,16,128]{3,2,1,0:T(8,128)(2,1)S(1)}, u32[]{:S(2)}, u32[]{:S(2)}) collective-permute-start(bf16[2,10,16,128]{3,2,1,0:T(8,128)(2,1)S(1)} %get-tuple-element.82), channel_id=1, source_target_pairs={{0,8},{1,2},{2,1},{3,4},{4,3},{5,6},{6,5},{7,15},{8,0},{9,10},{10,... | collective-permute-start | bytes 245768 | tf_op jit(solution)/shard_map/ppermute | solution.py:157
  17.6 3.5 %collective-permute-start.7 = (f32[4,27,16,128]{3,2,1,0:T(8,128)S(1)}, f32[4,27,16,128]{3,2,1,0:T(8,128)S(1)}, u32[]{:S(2)}, u32[]{:S(2)}) collective-permute-start(f32[4,27,16,128]{3,2,1,0:T(8,128)S(1)} %get-tuple-element.102), channel_id=1, source_target_pairs={{0,1},{1,0},{2,3},{3,2},{4,5},{5,4},{6,7},{7,6},{8,9},{9,8},{10,11... | collective-permute-start | bytes 2654216 | tf_op jit(solution)/shard_map/ppermute | solution.py:460
  20.5 2.6 %collective-permute-start.6 = (f32[4,27,16,128]{3,2,1,0:T(8,128)S(1)}, f32[4,27,16,128]{3,2,1,0:T(8,128)S(1)}, u32[]{:S(2)}, u32[]{:S(2)}) collective-permute-start(f32[4,27,16,128]{3,2,1,0:T(8,128)S(1)} %get-tuple-element.100), channel_id=1, source_target_pairs={{0,1},{1,0},{2,3},{3,2},{4,5},{5,4},{6,7},{7,6},{8,9},{9,8},{10,11... | collective-permute-start | bytes 2654216 | tf_op jit(solution)/shard_map/ppermute | solution.py:460
  23.1 22.7 %copy-start.1 = (bf16[8,16,16,128]{3,2,1,0:T(8,128)(2,1)S(1)}, bf16[8,16,16,128]{3,2,1,0:T(8,128)(2,1)}, u32[]{:S(2)}) copy-start(bf16[8,16,16,128]{3,2,1,0:T(8,128)(2,1)} %own.2) | copy-start | bytes 1572868
  23.2 9.0 %collective-permute-start.8 = (bf16[2,432,128]{2,1,0:T(8,128)(2,1)S(1)}, bf16[2,432,128]{2,1,0:T(8,128)(2,1)S(1)}, u32[]{:S(2)}, u32[]{:S(2)}) collective-permute-start(bf16[2,432,128]{2,1,0:T(8,128)(2,1)S(1)} %get-tuple-element.111), channel_id=1, source_target_pairs={{0,2},{1,3},{2,0},{3,1},{4,6},{5,7},{6,4},{7,5},{8,10},{9,11},{10,... | collective-permute-start | bytes 663560 | tf_op jit(solution)/shard_map/ppermute | solution.py:460
  24.6 11.9 %collective-permute-start.9 = (bf16[2,432,128]{2,1,0:T(8,128)(2,1)S(1)}, bf16[2,432,128]{2,1,0:T(8,128)(2,1)S(1)}, u32[]{:S(2)}, u32[]{:S(2)}) collective-permute-start(bf16[2,432,128]{2,1,0:T(8,128)(2,1)S(1)} %get-tuple-element.112), channel_id=1, source_target_pairs={{0,4},{1,5},{2,6},{3,7},{4,0},{5,1},{6,2},{7,3},{8,12},{9,13},{10,... | collective-permute-start | bytes 663560 | tf_op jit(solution)/shard_map/ppermute | solution.py:460
  26.3 10.2 %collective-permute-start.10 = (bf16[2,432,128]{2,1,0:T(8,128)(2,1)S(1)}, bf16[2,432,128]{2,1,0:T(8,128)(2,1)S(1)}, u32[]{:S(2)}, u32[]{:S(2)}) collective-permute-start(bf16[2,432,128]{2,1,0:T(8,128)(2,1)S(1)} %get-tuple-element.113), channel_id=1, source_target_pairs={{0,6},{1,7},{2,4},{3,5},{4,2},{5,3},{6,0},{7,1},{8,14},{9,15},{10,... | collective-permute-start | bytes 663560 | tf_op jit(solution)/shard_map/ppermute | solution.py:460
  26.8 5.4 %collective-permute-start.4 = (bf16[2,16,16,128]{3,2,1,0:T(8,128)(2,1)S(1)}, bf16[2,16,16,128]{3,2,1,0:T(8,128)(2,1)S(1)}, u32[]{:S(2)}, u32[]{:S(2)}) collective-permute-start(bf16[2,16,16,128]{3,2,1,0:T(8,128)(2,1)S(1)} %get-tuple-element.97), channel_id=1, source_target_pairs={{0,8},{1,9},{2,10},{3,11},{4,12},{5,13},{6,14},{7,15},{8,0},{9,1},... | collective-permute-start | bytes 393224 | tf_op jit(solution)/shard_map/ppermute | solution.py:157
  28.9 3.3 %collective-permute-start.5 = (bf16[2,16,16,128]{3,2,1,0:T(8,128)(2,1)S(1)}, bf16[2,16,16,128]{3,2,1,0:T(8,128)(2,1)S(1)}, u32[]{:S(2)}, u32[]{:S(2)}) collective-permute-start(bf16[2,16,16,128]{3,2,1,0:T(8,128)(2,1)S(1)} %get-tuple-element.98), channel_id=1, source_target_pairs={{0,1},{1,0},{2,3},{3,2},{4,5},{5,4},{6,7},{7,6},{8,16},{9,17},{10,... | collective-permute-start | bytes 393224 | tf_op jit(solution)/shard_map/ppermute | solution.py:157
  36.8 5.6 %collective-permute-start.13 = (s16[448,128]{1,0:T(8,128)(2,1)S(1)}, s16[448,128]{1,0:T(8,128)(2,1)S(1)}, u32[]{:S(2)}, u32[]{:S(2)}) collective-permute-start(s16[448,128]{1,0:T(8,128)(2,1)S(1)} %get-tuple-element.117), channel_id=1, source_target_pairs={{0,8},{8,0},{16,24},{24,16},{1,9},{9,1},{17,25},{25,17},{2,10},{10... | collective-permute-start | bytes 344072 | tf_op jit(solution)/shard_map/ppermute | solution.py:460
  39.6 6.2 %collective-permute-start.12 = (bf16[2,10,16,128]{3,2,1,0:T(8,128)(2,1)S(1)}, bf16[2,10,16,128]{3,2,1,0:T(8,128)(2,1)S(1)}, u32[]{:S(2)}, u32[]{:S(2)}) collective-permute-start(bf16[2,10,16,128]{3,2,1,0:T(8,128)(2,1)S(1)} %get-tuple-element.123), channel_id=1, source_target_pairs={{0,8},{1,2},{2,1},{3,4},{4,3},{5,6},{6,5},{7,15},{8,0},{9,10},{10,... | collective-permute-start | bytes 245768 | tf_op jit(solution)/shard_map/ppermute | solution.py:157
  39.7 6.1 %collective-permute-start.11 = (bf16[2,10,16,128]{3,2,1,0:T(8,128)(2,1)S(1)}, bf16[2,10,16,128]{3,2,1,0:T(8,128)(2,1)S(1)}, u32[]{:S(2)}, u32[]{:S(2)}) collective-permute-start(bf16[2,10,16,128]{3,2,1,0:T(8,128)(2,1)S(1)} %get-tuple-element.122), channel_id=1, source_target_pairs={{0,1},{1,0},{2,3},{3,2},{4,5},{5,4},{6,7},{7,6},{8,9},{9,8},{10,11... | collective-permute-start | bytes 245768 | tf_op jit(solution)/shard_map/ppermute | solution.py:157
  42.5 8.1 %copy-start = (bf16[27,128,128]{2,1,0:T(8,128)(2,1)S(1)}, bf16[27,128,128]{2,1,0:T(8,128)(2,1)}, u32[]{:S(2)}) copy-start(bf16[27,128,128]{2,1,0:T(8,128)(2,1)} %w.5) | copy-start | bytes 2654212
  42.5 7.4 %collective-permute-start.14 = (s16[448,128]{1,0:T(8,128)(2,1)S(1)}, s16[448,128]{1,0:T(8,128)(2,1)S(1)}, u32[]{:S(2)}, u32[]{:S(2)}) collective-permute-start(s16[448,128]{1,0:T(8,128)(2,1)S(1)} %shard_map.94.own), channel_id=1, source_target_pairs={{0,16},{8,24},{16,0},{24,8},{1,17},{9,25},{17,1},{25,9},{2,18},{10... | collective-permute-start | bytes 344072 | tf_op jit(solution)/shard_map/ppermute | solution.py:460
  50.1 4.9 %collective-permute-start.15 = (s16[448,128]{1,0:T(8,128)(2,1)S(1)}, s16[448,128]{1,0:T(8,128)(2,1)S(1)}, u32[]{:S(2)}, u32[]{:S(2)}) collective-permute-start(s16[448,128]{1,0:T(8,128)(2,1)S(1)} %shard_map.96.own), channel_id=1, source_target_pairs={{0,8},{8,0},{16,24},{24,16},{1,9},{9,1},{17,25},{25,17},{2,10},{10... | collective-permute-start | bytes 344072 | tf_op jit(solution)/shard_map/ppermute | solution.py:460

commit v3 on v2

--- a/solution.py
+++ b/solution.py
@@ -460,30 +460,41 @@
     return lax.ppermute(value, axis, [(i, i ^ bit) for i in range(lax.axis_size(axis))])
 
 
+def is_far(place):
+    return place & (place - 1) != 0
+
+
 def first_sum(g, keep, came, earlier):
     places, taps, share, channels = keep.shape
     rows = taps * share
+    far = [p for p in range(places) if is_far(p)]
+    near = [p for p in range(1, places) if not is_far(p)]
 
     def kernel(keep, came, *refs):
-        stays, *leaves = refs[-places:]
+        outs = refs[-places:]
         for p in range(places):
             value = (keep[p] + came[p]).reshape(rows, channels)
             if p == 0:
-                stays[g] = value
+                outs[0][g] = value
+            elif p in near:
+                outs[1 + near.index(p)][g] = value.astype(BF16)
             else:
-                leaves[p - 1][g] = value.astype(BF16)
+                outs[1 + len(near) + far.index(p)][...] = value.astype(BF16)
 
     stay = pltpu.VMEM((2, rows, channels), F32)
-    leave = pltpu.VMEM((2, rows, channels), BF16)
-    return call(
+    both = pltpu.VMEM((2, rows, channels), BF16)
+    one = pltpu.VMEM((rows, channels), BF16)
+    outs = call(
         kernel,
-        (stay,) + (leave,) * (places - 1),
+        (stay,) + (both,) * len(near) + (one,) * len(far),
         (keep, came, *earlier),
         [],
         nbytes=2 * MIB,
         vmem=4 * MIB,
         aliases={2 + n: n for n in range(len(earlier))},
     )
+    count = 1 + len(near)
+    return outs[:count], outs[count:]
 
 
 CODE_ROWS = 16
@@ -509,24 +520,28 @@
     return pltpu.VMEM((CODE_ROWS + rows, channels), jnp.int16)
 
 
-def second_sums(stays, came):
+def second_sums(stays, near, far):
     _, rows, channels = stays.shape
+    count = len(near)
 
     def kernel(stays, *refs):
-        came, (stay, leave) = refs[:-2], refs[-2:]
+        near, (stay, leave) = refs[:count], refs[-2:]
+        far = (refs[count : count + len(far_second)], refs[count + len(far_second) : -2])
         odd = lax.axis_index("gx") % 2
-
-        def total(g):
+        totals = []
+        for g in range(2):
             value = stays[g]
-            for ref in came:
+            for ref in near:
                 value += ref[g].astype(F32)
-            return value
-
-        stay[...] = total(odd)
-        encode(total(1 - odd), leave)
-
+            for ref in far[g]:
+                value += ref[...].astype(F32)
+            totals.append(value)
+        stay[...] = pick(odd, totals[0], totals[1])
+        encode(pick(odd, totals[1], totals[0]), leave)
+
+    far_second, far_first = far
     outs = (pltpu.VMEM((rows, channels), F32), coded_shape(rows, channels))
-    return call(kernel, outs, (stays, *came), [], nbytes=2 * MIB, vmem=4 * MIB)
+    return call(kernel, outs, (stays, *near, *far_second, *far_first), [], nbytes=2 * MIB, vmem=4 * MIB)
 
 
 def next_sum(own, came):
@@ -568,12 +583,15 @@
     came = swap(send, "gy", 1)
     pre_grad, keep_first, send, xa, xb, ya, yb = pre_grad_and_terms(hidden, slope, zm, zu, second_taps, grad)
 
-    sums = first_sum(0, keep_second, after(came, pre_grad), ())
+    places = range(1, keep_first.shape[0])
+    sums, leaves = first_sum(0, keep_second, after(came, pre_grad), ())
+    far_second = [swap(value, "gy", 2 * p) for value, p in zip(leaves, filter(is_far, places))]
     came = swap(send, "gy", 1)
-    xa, xb = swap_neighbours("gx", xa, xb)
-    stays, *leaves = first_sum(1, keep_first, after(came, sums[0]), sums)
-    came = [swap(value, "gy", 2 * (p + 1)) for p, value in enumerate(leaves)]
-    stays, leaves = second_sums(stays, after(came, xa, xb))
+    (stays, *near), leaves = first_sum(1, keep_first, after(came, sums[0]), sums)
+    near = [swap(value, "gy", 2 * p) for value, p in zip(near, (p for p in places if not is_far(p)))]
+    far_first = [swap(value, "gy", 2 * p) for value, p in zip(leaves, filter(is_far, places))]
+    xa, xb = swap_neighbours("gx", *after((xa, xb), far_second, stays))
+    stays, leaves = second_sums(stays, *after((near, (far_second, far_first)), xa, xb))
     xa, xb = after((xa, xb), leaves)
     came = swap(leaves, "gx", 1)
     ya, yb = finish_columns(xa, xb, ya, yb)

time: 55.9 us -> 54.6 us (0.977)
  waiting for transfers between devices: 13.4 us -> 9.41 us
  starting transfers between devices: 19.6 us -> 22.2 us
    ppermute x8, waiting for transfers between devices: 3.99 us -> 0.66 us  [swap_neighbours(): lax.ppermute(value, ('gx', 'gy'), swap_pairs(axis, odd))]
    ppermute x8, starting transfers between devices: 8.81 us -> 10.4 us  [swap_neighbours(): lax.ppermute(value, ('gx', 'gy'), swap_pairs(axis, odd))]
    ppermute x8 -> x9, starting transfers between devices: 10.7 us -> 11.8 us  [swap(): lax.ppermute(value, axis, [(i, i ^ bit) for i in range(lax.axis_size(axis...]
    ppermute x8 -> x9, waiting for transfers between devices: 9.45 us -> 8.76 us  [swap(): lax.ppermute(value, axis, [(i, i ^ bit) for i in range(lax.axis_size(axis...]
  transfers between devices with their start and end apart: 16 -> 17, of which waited for: 7 -> 6; matrix products, arithmetic and copies ran while one was open for 0% -> 0% of each run, Pallas kernels for 29% -> 30%
where the time goes in v3:
time: 54.6 us; the launch traced here: 54.4 us
  starting transfers between devices  22.2 us (41%)
  Pallas kernels  22 us (40%)
  waiting for transfers between devices  9.41 us (17%)
  between operations  0.8 us (1%)
    pallas_call x15, Pallas kernels, call(): pl.pallas_call(kernel, out_shape=out_shapes, in_specs=list(spaces) + [VME...  22 us
    ppermute x9, starting transfers between devices, swap(): lax.ppermute(value, axis, [(i, i ^ bit) for i in range(lax.axis_size(axis...  11.8 us
    ppermute x8, starting transfers between devices, swap_neighbours(): lax.ppermute(value, ('gx', 'gy'), swap_pairs(axis, odd))  10.4 us
    ppermute x9, waiting for transfers between devices, swap(): lax.ppermute(value, axis, [(i, i ^ bit) for i in range(lax.axis_size(axis...  8.76 us
  transfers between devices with their start and end apart: 17, of which 6 were waited for; matrix products, arithmetic and copies ran while one was open for 0% of the time, Pallas kernels for 30%

profile of v3, /device:TPU:0, one launch (start us, length us, event | category | flops | bytes accessed | tf_op | source)
XLA Modules:
  0.0 54.4 jit_solution(6027019246503134018)
XLA Ops:
  0.6 1.5 %shard_map.84 = (f32[1,256,128]{2,1,0:T(8,128)S(1)}, bf16[2,16,16,128]{3,2,1,0:T(8,128)(2,1)S(1)}, bf16[2,16,16,128]{3,2,1,0:T(8,128)(2,1)S(1)}, bf16[2,8,16,128...) custom-call(s32[1,2,2]{2,1,0:T(2,128)} %occ_hbm.1, ...), custom_call_target="tpu_custom_call" | custom-call | bytes 1048576 | tf_op jit(solution)/shard_map/pallas_call | solution.py:19
  2.2 3.1 %collective-permute-start = (bf16[2,16,16,128]{3,2,1,0:T(8,128)(2,1)S(1)}, bf16[2,16,16,128]{3,2,1,0:T(8,128)(2,1)S(1)}, u32[]{:S(2)}, u32[]{:S(2)}) collective-permute-start(bf16[2,16,16,128]{3,2,1,0:T(8,128)(2,1)S(1)} %get-tuple-element.75), channel_id=1, source_target_pairs={{0,8},{1,9},{2,10},{3,11},{4,12},{5,13},{6,14},{7,15},{8,0},{9,1},... | collective-permute-start | bytes 393224 | tf_op jit(solution)/shard_map/ppermute | solution.py:157
  5.2 0.0 collective-permute-start.1
  5.2 0.0 copy-start.2
  5.3 0.0 copy-start.3
  5.3 2.8 %shard_map.85 = (bf16[10,18,16,384]{3,2,1,0:T(8,128)(2,1)S(1)}, bf16[12,384,256]{2,1,0:T(8,128)(2,1)S(1)}, f32[8,256,128]{2,1,0:T(8,128)S(1)}) custom-call(f32[1,256,128]{2,1,0:T(8,128)S(1)} %get-tuple-element.86.mask, bf16[8,16,16,128]{3,2,1,0:T(8,128)(2,1)S(1)} %get-tuple-element.77.field, bf16[27,128,128]{2,1,0:T(8,128)(2,1)S(1)} %get-tuple-element.78.w), custom_call_target="tpu_custom_call" | custom-call | flops 1811939328 | bytes 4194304 | tf_op jit(solution)/shard_map/pallas_call | solution.py:19
  8.1 0.6 %collective-permute-done.xa = bf16[2,16,16,128]{3,2,1,0:T(8,128)(2,1)S(1)} collective-permute-done((bf16[2,16,16,128]{3,2,1,0:T(8,128)(2,1)S(1)}, bf16[2,16,16,128]{3,2,1,0:T(8,128)(2,1)S(1)}, u32[]{:S(2)}, u32[]{:S(2)}) %collective-permute-start) | collective-permute-done | bytes 131104 | tf_op jit(solution)/shard_map/ppermute | solution.py:157
  8.7 0.0 collective-permute-done.1.xb
  8.8 0.1 collective-permute-start.2
  8.9 2.9 %collective-permute-start.3 = (bf16[2,10,16,128]{3,2,1,0:T(8,128)(2,1)S(1)}, bf16[2,10,16,128]{3,2,1,0:T(8,128)(2,1)S(1)}, u32[]{:S(2)}, u32[]{:S(2)}) collective-permute-start(bf16[2,10,16,128]{3,2,1,0:T(8,128)(2,1)S(1)} %get-tuple-element.85), channel_id=1, source_target_pairs={{0,8},{1,2},{2,1},{3,4},{4,3},{5,6},{6,5},{7,15},{8,0},{9,10},{10,... | collective-permute-start | bytes 245768 | tf_op jit(solution)/shard_map/ppermute | solution.py:157
  11.8 0.0 copy-done.2
  11.8 0.0 copy-done.3
  11.8 2.8 %shard_map.87 = (bf16[10,18,16,384]{3,2,1,0:T(8,128)(2,1)S(1)}, bf16[12,384,256]{2,1,0:T(8,128)(2,1)S(1)}, f32[8,256,128]{2,1,0:T(8,128)S(1)}) custom-call(f32[1,256,128]{2,1,0:T(8,128)S(1)} %get-tuple-element.86.mask, bf16[8,16,16,128]{3,2,1,0:T(8,128)(2,1)S(1)} %copy-done.2, bf16[27,128,128]{2,1,0:T(8,128)(2,1)S(1)} %copy-done.3), custom_call_target="tpu_custom_call" | custom-call | flops 1811939328 | bytes 4194304 | tf_op jit(solution)/shard_map/pallas_call | solution.py:19
  14.6 0.0 collective-permute-done.3.yb
  14.6 0.0 collective-permute-done.2.ya
  14.6 2.9 %shard_map.88 = (bf16[10,18,16,384]{3,2,1,0:T(8,128)(2,1)S(1)}, bf16[10,18,16,384]{3,2,1,0:T(8,128)(2,1)S(1)}, bf16[8,16,16,128]{3,2,1,0:T(8,128)(2,1)S(1)}, f32...) custom-call(f32[1,256,128]{2,1,0:T(8,128)S(1)} %get-tuple-element.86, ...), custom_call_target="tpu_custom_call", output_to_operand_aliasing={{0}: (7, {}), {1}: (8, {})} | custom-call | flops 1811939328 | bytes 8388608 | tf_op jit(solution)/shard_map/pallas_call | solution.py:19
  17.6 0.1 collective-permute-start.4
  17.6 2.9 %shard_map.89 = (bf16[8,16,16,128]{3,2,1,0:T(8,128)(2,1)S(1)}, f32[4,27,16,128]{3,2,1,0:T(8,128)S(1)}, f32[4,27,16,128]{3,2,1,0:T(8,128)S(1)}, bf16[2,16,16,128]...) custom-call(bf16[8,16,16,128]{3,2,1,0:T(8,128)(2,1)S(1)} %get-tuple-, ...), custom_call_target="tpu_custom_call" | custom-call | flops 1811939328 | bytes 8388608 | tf_op jit(solution)/shard_map/pallas_call | solution.py:19
  20.5 0.6 %collective-permute-start.6 = (f32[4,27,16,128]{3,2,1,0:T(8,128)S(1)}, f32[4,27,16,128]{3,2,1,0:T(8,128)S(1)}, u32[]{:S(2)}, u32[]{:S(2)}) collective-permute-start(f32[4,27,16,128]{3,2,1,0:T(8,128)S(1)} %get-tuple-element.108), channel_id=1, source_target_pairs={{0,1},{1,0},{2,3},{3,2},{4,5},{5,4},{6,7},{7,6},{8,9},{9,8},{10,11... | collective-permute-start | bytes 2654216 | tf_op jit(solution)/shard_map/ppermute | solution.py:460
  21.1 0.0 collective-permute-done.4.came
  21.1 0.1 shard_map.90
  21.2 2.2 %collective-permute-start.5 = (bf16[432,128]{1,0:T(8,128)(2,1)S(1)}, bf16[432,128]{1,0:T(8,128)(2,1)S(1)}, u32[]{:S(2)}, u32[]{:S(2)}) collective-permute-start(bf16[432,128]{1,0:T(8,128)(2,1)S(1)} %get-tuple-element.106), channel_id=1, source_target_pairs={{0,6},{1,7},{2,4},{3,5},{4,2},{5,3},{6,0},{7,1},{8,14},{9,15},{10,... | collective-permute-start | bytes 331784 | tf_op jit(solution)/shard_map/ppermute | solution.py:460
  23.3 0.0 collective-permute-done.6.came
  23.3 0.0 copy-start.1
  23.4 0.1 shard_map.91
  23.4 1.2 %collective-permute-start.9 = (bf16[2,432,128]{2,1,0:T(8,128)(2,1)S(1)}, bf16[2,432,128]{2,1,0:T(8,128)(2,1)S(1)}, u32[]{:S(2)}, u32[]{:S(2)}) collective-permute-start(bf16[2,432,128]{2,1,0:T(8,128)(2,1)S(1)} %get-tuple-element.116), channel_id=1, source_target_pairs={{0,2},{1,3},{2,0},{3,1},{4,6},{5,7},{6,4},{7,5},{8,10},{9,11},{10,... | collective-permute-start | bytes 663560 | tf_op jit(solution)/shard_map/ppermute | solution.py:460
  24.6 1.7 %collective-permute-start.10 = (bf16[2,432,128]{2,1,0:T(8,128)(2,1)S(1)}, bf16[2,432,128]{2,1,0:T(8,128)(2,1)S(1)}, u32[]{:S(2)}, u32[]{:S(2)}) collective-permute-start(bf16[2,432,128]{2,1,0:T(8,128)(2,1)S(1)} %get-tuple-element.117), channel_id=1, source_target_pairs={{0,4},{1,5},{2,6},{3,7},{4,0},{5,1},{6,2},{7,3},{8,12},{9,13},{10,... | collective-permute-start | bytes 663560 | tf_op jit(solution)/shard_map/ppermute | solution.py:460
  26.3 1.1 %collective-permute-done.5.refs_2_ = bf16[432,128]{1,0:T(8,128)(2,1)S(1)} collective-permute-done((bf16[432,128]{1,0:T(8,128)(2,1)S(1)}, bf16[432,128]{1,0:T(8,128)(2,1)S(1)}, u32[]{:S(2)}, u32[]{:S(2)}) %collective-permute-start.5) | collective-permute-done | bytes 110624 | tf_op jit(solution)/shard_map/ppermute | solution.py:460
  27.4 1.6 %collective-permute-start.7 = (bf16[2,16,16,128]{3,2,1,0:T(8,128)(2,1)S(1)}, bf16[2,16,16,128]{3,2,1,0:T(8,128)(2,1)S(1)}, u32[]{:S(2)}, u32[]{:S(2)}) collective-permute-start(bf16[2,16,16,128]{3,2,1,0:T(8,128)(2,1)S(1)} %get-tuple-element.114), channel_id=1, source_target_pairs={{0,8},{1,9},{2,10},{3,11},{4,12},{5,13},{6,14},{7,15},{8,0},{9,1},... | collective-permute-start | bytes 393224 | tf_op jit(solution)/shard_map/ppermute | solution.py:157
  29.1 0.0 collective-permute-start.8
  29.1 1.9 %collective-permute-start.11 = (bf16[432,128]{1,0:T(8,128)(2,1)S(1)}, bf16[432,128]{1,0:T(8,128)(2,1)S(1)}, u32[]{:S(2)}, u32[]{:S(2)}) collective-permute-start(bf16[432,128]{1,0:T(8,128)(2,1)S(1)} %get-tuple-element.118), channel_id=1, source_target_pairs={{0,6},{1,7},{2,4},{3,5},{4,2},{5,3},{6,0},{7,1},{8,14},{9,15},{10,... | collective-permute-start | bytes 331784 | tf_op jit(solution)/shard_map/ppermute | solution.py:460
  31.0 4.5 %collective-permute-done.11.refs_3_ = bf16[432,128]{1,0:T(8,128)(2,1)S(1)} collective-permute-done((bf16[432,128]{1,0:T(8,128)(2,1)S(1)}, bf16[432,128]{1,0:T(8,128)(2,1)S(1)}, u32[]{:S(2)}, u32[]{:S(2)}) %collective-permute-start.11) | collective-permute-done | bytes 110624 | tf_op jit(solution)/shard_map/ppermute | solution.py:460
  35.5 0.0 collective-permute-done.9.refs_0_
  35.5 0.0 collective-permute-done.10.refs_1_
  35.5 0.0 collective-permute-done.7.xa
  35.5 0.0 collective-permute-done.8.xb
  35.5 0.2 shard_map.92
  35.7 1.5 %collective-permute-start.14 = (s16[448,128]{1,0:T(8,128)(2,1)S(1)}, s16[448,128]{1,0:T(8,128)(2,1)S(1)}, u32[]{:S(2)}, u32[]{:S(2)}) collective-permute-start(s16[448,128]{1,0:T(8,128)(2,1)S(1)} %get-tuple-element.123), channel_id=1, source_target_pairs={{0,8},{8,0},{16,24},{24,16},{1,9},{9,1},{17,25},{25,17},{2,10},{10... | collective-permute-start | bytes 344072 | tf_op jit(solution)/shard_map/ppermute | solution.py:460
  37.2 0.7 %collective-permute-start.13 = (bf16[2,10,16,128]{3,2,1,0:T(8,128)(2,1)S(1)}, bf16[2,10,16,128]{3,2,1,0:T(8,128)(2,1)S(1)}, u32[]{:S(2)}, u32[]{:S(2)}) collective-permute-start(bf16[2,10,16,128]{3,2,1,0:T(8,128)(2,1)S(1)} %get-tuple-element.129), channel_id=1, source_target_pairs={{0,8},{1,2},{2,1},{3,4},{4,3},{5,6},{6,5},{7,15},{8,0},{9,10},{10,... | collective-permute-start | bytes 245768 | tf_op jit(solution)/shard_map/ppermute | solution.py:157
  37.9 2.0 %collective-permute-start.12 = (bf16[2,10,16,128]{3,2,1,0:T(8,128)(2,1)S(1)}, bf16[2,10,16,128]{3,2,1,0:T(8,128)(2,1)S(1)}, u32[]{:S(2)}, u32[]{:S(2)}) collective-permute-start(bf16[2,10,16,128]{3,2,1,0:T(8,128)(2,1)S(1)} %get-tuple-element.128), channel_id=1, source_target_pairs={{0,1},{1,0},{2,3},{3,2},{4,5},{5,4},{6,7},{7,6},{8,9},{9,8},{10,11... | collective-permute-start | bytes 245768 | tf_op jit(solution)/shard_map/ppermute | solution.py:157
  39.9 0.7 %collective-permute-done.14.came = s16[448,128]{1,0:T(8,128)(2,1)S(1)} collective-permute-done((s16[448,128]{1,0:T(8,128)(2,1)S(1)}, s16[448,128]{1,0:T(8,128)(2,1)S(1)}, u32[]{:S(2)}, u32[]{:S(2)}) %collective-permute-start.14) | collective-permute-done | bytes 114720 | tf_op jit(solution)/shard_map/ppermute | solution.py:460
  40.6 0.2 shard_map.94.own
  40.8 0.0 copy-start
  40.8 2.7 %collective-permute-start.15 = (s16[448,128]{1,0:T(8,128)(2,1)S(1)}, s16[448,128]{1,0:T(8,128)(2,1)S(1)}, u32[]{:S(2)}, u32[]{:S(2)}) collective-permute-start(s16[448,128]{1,0:T(8,128)(2,1)S(1)} %shard_map.94.own), channel_id=1, source_target_pairs={{0,16},{8,24},{16,0},{24,8},{1,17},{9,25},{17,1},{25,9},{2,18},{10... | collective-permute-start | bytes 344072 | tf_op jit(solution)/shard_map/ppermute | solution.py:460
  43.4 0.0 collective-permute-done.13.yb
  43.4 0.0 collective-permute-done.12.ya
  43.4 0.0 copy-done.1
  43.5 3.8 %shard_map.95 = bf16[8,16,16,128]{3,2,1,0:T(8,128)(2,1)} custom-call(f32[1,256,128]{2,1,0:T(8,128)S(1)} %get-tuple-element.86.mask, bf16[8,16,16,128]{3,2,1,0:T(8,128)(2,1)S(1)} %copy-done.1, bf16[8,16,16,128]{3,2,1,0:T(8,128)(2,1)S(1)} %get-tuple-element.95.hidden.field, bf16[2,16,16,128]{3,2,1,0:T(8,128)(2,1)S(1)} %collective-permute-done.7.xa, ...), custom_call_target="tpu_custom_call" | custom-call | flops 1811939328 | bytes 3145728 | tf_op jit(solution)/shard_map/pallas_call | solution.py:19
  47.3 1.3 %collective-permute-done.15.came = s16[448,128]{1,0:T(8,128)(2,1)S(1)} collective-permute-done((s16[448,128]{1,0:T(8,128)(2,1)S(1)}, s16[448,128]{1,0:T(8,128)(2,1)S(1)}, u32[]{:S(2)}, u32[]{:S(2)}) %collective-permute-start.15) | collective-permute-done | bytes 114720 | tf_op jit(solution)/shard_map/ppermute | solution.py:460
  48.6 0.2 shard_map.96.own
  48.7 0.1 collective-permute-start.16
  48.8 0.0 copy-done
  48.8 3.6 %shard_map.97 = bf16[8,16,16,128]{3,2,1,0:T(8,128)(2,1)} custom-call(f32[1,256,128]{2,1,0:T(8,128)S(1)} %get-tuple-element.86.mask, bf16[8,16,16,128]{3,2,1,0:T(8,128)(2,1)S(1)} %copy-done.2, bf16[8,16,16,128]{3,2,1,0:T(8,128)(2,1)S(1)} %get-tuple-element.104.field, bf16[2,16,16,128]{3,2,1,0:T(8,128)(2,1)S(1)} %collective-permute-done.7.xa, ...), custom_call_target="tpu_custom_call" | custom-call | flops 1811939328 | bytes 3145728 | tf_op jit(solution)/shard_map/pallas_call | solution.py:19
  52.4 1.2 %collective-permute-done.16.came = s16[448,128]{1,0:T(8,128)(2,1)S(1)} collective-permute-done((s16[448,128]{1,0:T(8,128)(2,1)S(1)}, s16[448,128]{1,0:T(8,128)(2,1)S(1)}, u32[]{:S(2)}, u32[]{:S(2)}) %collective-permute-start.16) | collective-permute-done | bytes 114720 | tf_op jit(solution)/shard_map/ppermute | solution.py:460
  53.6 0.8 %shard_map.98 = (f32[27,16,128]{2,1,0:T(8,128)}, f32[27,16,128]{2,1,0:T(8,128)}) custom-call(s16[448,128]{1,0:T(8,128)(2,1)S(1)} %shard_map.96.own, s16[448,128]{1,0:T(8,128)(2,1)S(1)} %collective-permute-done.16.came), custom_call_target="tpu_custom_call" | custom-call | bytes 1048576 | tf_op jit(solution)/shard_map/pallas_call | solution.py:19
  (2 shorter events, 0.1 us)
Async XLA Ops:
  2.2 6.6 %collective-permute-start = (bf16[2,16,16,128]{3,2,1,0:T(8,128)(2,1)S(1)}, bf16[2,16,16,128]{3,2,1,0:T(8,128)(2,1)S(1)}, u32[]{:S(2)}, u32[]{:S(2)}) collective-permute-start(bf16[2,16,16,128]{3,2,1,0:T(8,128)(2,1)S(1)} %get-tuple-element.75), channel_id=1, source_target_pairs={{0,8},{1,9},{2,10},{3,11},{4,12},{5,13},{6,14},{7,15},{8,0},{9,1},... | collective-permute-start | bytes 393224 | tf_op jit(solution)/shard_map/ppermute | solution.py:157
  5.2 3.5 %collective-permute-start.1 = (bf16[2,16,16,128]{3,2,1,0:T(8,128)(2,1)S(1)}, bf16[2,16,16,128]{3,2,1,0:T(8,128)(2,1)S(1)}, u32[]{:S(2)}, u32[]{:S(2)}) collective-permute-start(bf16[2,16,16,128]{3,2,1,0:T(8,128)(2,1)S(1)} %get-tuple-element.76), channel_id=1, source_target_pairs={{0,1},{1,0},{2,3},{3,2},{4,5},{5,4},{6,7},{7,6},{8,16},{9,17},{10,... | collective-permute-start | bytes 393224 | tf_op jit(solution)/shard_map/ppermute | solution.py:157
  5.2 6.5 %copy-start.2 = (bf16[8,16,16,128]{3,2,1,0:T(8,128)(2,1)S(1)}, bf16[8,16,16,128]{3,2,1,0:T(8,128)(2,1)}, u32[]{:S(2)}) copy-start(bf16[8,16,16,128]{3,2,1,0:T(8,128)(2,1)} %own.3) | copy-start | bytes 1572868
  5.3 6.5 %copy-start.3 = (bf16[27,128,128]{2,1,0:T(8,128)(2,1)S(1)}, bf16[27,128,128]{2,1,0:T(8,128)(2,1)}, u32[]{:S(2)}) copy-start(bf16[27,128,128]{2,1,0:T(8,128)(2,1)} %w.4) | copy-start | bytes 2654212
  8.8 5.8 %collective-permute-start.2 = (bf16[2,10,16,128]{3,2,1,0:T(8,128)(2,1)S(1)}, bf16[2,10,16,128]{3,2,1,0:T(8,128)(2,1)S(1)}, u32[]{:S(2)}, u32[]{:S(2)}) collective-permute-start(bf16[2,10,16,128]{3,2,1,0:T(8,128)(2,1)S(1)} %get-tuple-element.84), channel_id=1, source_target_pairs={{0,1},{1,0},{2,3},{3,2},{4,5},{5,4},{6,7},{7,6},{8,9},{9,8},{10,11... | collective-permute-start | bytes 245768 | tf_op jit(solution)/shard_map/ppermute | solution.py:157
  8.9 5.8 %collective-permute-start.3 = (bf16[2,10,16,128]{3,2,1,0:T(8,128)(2,1)S(1)}, bf16[2,10,16,128]{3,2,1,0:T(8,128)(2,1)S(1)}, u32[]{:S(2)}, u32[]{:S(2)}) collective-permute-start(bf16[2,10,16,128]{3,2,1,0:T(8,128)(2,1)S(1)} %get-tuple-element.85), channel_id=1, source_target_pairs={{0,8},{1,2},{2,1},{3,4},{4,3},{5,6},{6,5},{7,15},{8,0},{9,10},{10,... | collective-permute-start | bytes 245768 | tf_op jit(solution)/shard_map/ppermute | solution.py:157
  17.6 3.5 %collective-permute-start.4 = (f32[4,27,16,128]{3,2,1,0:T(8,128)S(1)}, f32[4,27,16,128]{3,2,1,0:T(8,128)S(1)}, u32[]{:S(2)}, u32[]{:S(2)}) collective-permute-start(f32[4,27,16,128]{3,2,1,0:T(8,128)S(1)} %get-tuple-element.103), channel_id=1, source_target_pairs={{0,1},{1,0},{2,3},{3,2},{4,5},{5,4},{6,7},{7,6},{8,9},{9,8},{10,11... | collective-permute-start | bytes 2654216 | tf_op jit(solution)/shard_map/ppermute | solution.py:460
  20.5 2.8 %collective-permute-start.6 = (f32[4,27,16,128]{3,2,1,0:T(8,128)S(1)}, f32[4,27,16,128]{3,2,1,0:T(8,128)S(1)}, u32[]{:S(2)}, u32[]{:S(2)}) collective-permute-start(f32[4,27,16,128]{3,2,1,0:T(8,128)S(1)} %get-tuple-element.108), channel_id=1, source_target_pairs={{0,1},{1,0},{2,3},{3,2},{4,5},{5,4},{6,7},{7,6},{8,9},{9,8},{10,11... | collective-permute-start | bytes 2654216 | tf_op jit(solution)/shard_map/ppermute | solution.py:460
  21.2 6.3 %collective-permute-start.5 = (bf16[432,128]{1,0:T(8,128)(2,1)S(1)}, bf16[432,128]{1,0:T(8,128)(2,1)S(1)}, u32[]{:S(2)}, u32[]{:S(2)}) collective-permute-start(bf16[432,128]{1,0:T(8,128)(2,1)S(1)} %get-tuple-element.106), channel_id=1, source_target_pairs={{0,6},{1,7},{2,4},{3,5},{4,2},{5,3},{6,0},{7,1},{8,14},{9,15},{10,... | collective-permute-start | bytes 331784 | tf_op jit(solution)/shard_map/ppermute | solution.py:460
  23.3 20.1 %copy-start.1 = (bf16[8,16,16,128]{3,2,1,0:T(8,128)(2,1)S(1)}, bf16[8,16,16,128]{3,2,1,0:T(8,128)(2,1)}, u32[]{:S(2)}) copy-start(bf16[8,16,16,128]{3,2,1,0:T(8,128)(2,1)} %own.2) | copy-start | bytes 1572868
  23.4 12.0 %collective-permute-start.9 = (bf16[2,432,128]{2,1,0:T(8,128)(2,1)S(1)}, bf16[2,432,128]{2,1,0:T(8,128)(2,1)S(1)}, u32[]{:S(2)}, u32[]{:S(2)}) collective-permute-start(bf16[2,432,128]{2,1,0:T(8,128)(2,1)S(1)} %get-tuple-element.116), channel_id=1, source_target_pairs={{0,2},{1,3},{2,0},{3,1},{4,6},{5,7},{6,4},{7,5},{8,10},{9,11},{10,... | collective-permute-start | bytes 663560 | tf_op jit(solution)/shard_map/ppermute | solution.py:460
  24.6 10.8 %collective-permute-start.10 = (bf16[2,432,128]{2,1,0:T(8,128)(2,1)S(1)}, bf16[2,432,128]{2,1,0:T(8,128)(2,1)S(1)}, u32[]{:S(2)}, u32[]{:S(2)}) collective-permute-start(bf16[2,432,128]{2,1,0:T(8,128)(2,1)S(1)} %get-tuple-element.117), channel_id=1, source_target_pairs={{0,4},{1,5},{2,6},{3,7},{4,0},{5,1},{6,2},{7,3},{8,12},{9,13},{10,... | collective-permute-start | bytes 663560 | tf_op jit(solution)/shard_map/ppermute | solution.py:460
  27.4 8.0 %collective-permute-start.7 = (bf16[2,16,16,128]{3,2,1,0:T(8,128)(2,1)S(1)}, bf16[2,16,16,128]{3,2,1,0:T(8,128)(2,1)S(1)}, u32[]{:S(2)}, u32[]{:S(2)}) collective-permute-start(bf16[2,16,16,128]{3,2,1,0:T(8,128)(2,1)S(1)} %get-tuple-element.114), channel_id=1, source_target_pairs={{0,8},{1,9},{2,10},{3,11},{4,12},{5,13},{6,14},{7,15},{8,0},{9,1},... | collective-permute-start | bytes 393224 | tf_op jit(solution)/shard_map/ppermute | solution.py:157
  29.1 6.4 %collective-permute-start.8 = (bf16[2,16,16,128]{3,2,1,0:T(8,128)(2,1)S(1)}, bf16[2,16,16,128]{3,2,1,0:T(8,128)(2,1)S(1)}, u32[]{:S(2)}, u32[]{:S(2)}) collective-permute-start(bf16[2,16,16,128]{3,2,1,0:T(8,128)(2,1)S(1)} %get-tuple-element.115), channel_id=1, source_target_pairs={{0,1},{1,0},{2,3},{3,2},{4,5},{5,4},{6,7},{7,6},{8,16},{9,17},{10,... | collective-permute-start | bytes 393224 | tf_op jit(solution)/shard_map/ppermute | solution.py:157
  29.1 6.4 %collective-permute-start.11 = (bf16[432,128]{1,0:T(8,128)(2,1)S(1)}, bf16[432,128]{1,0:T(8,128)(2,1)S(1)}, u32[]{:S(2)}, u32[]{:S(2)}) collective-permute-start(bf16[432,128]{1,0:T(8,128)(2,1)S(1)} %get-tuple-element.118), channel_id=1, source_target_pairs={{0,6},{1,7},{2,4},{3,5},{4,2},{5,3},{6,0},{7,1},{8,14},{9,15},{10,... | collective-permute-start | bytes 331784 | tf_op jit(solution)/shard_map/ppermute | solution.py:460
  35.7 4.9 %collective-permute-start.14 = (s16[448,128]{1,0:T(8,128)(2,1)S(1)}, s16[448,128]{1,0:T(8,128)(2,1)S(1)}, u32[]{:S(2)}, u32[]{:S(2)}) collective-permute-start(s16[448,128]{1,0:T(8,128)(2,1)S(1)} %get-tuple-element.123), channel_id=1, source_target_pairs={{0,8},{8,0},{16,24},{24,16},{1,9},{9,1},{17,25},{25,17},{2,10},{10... | collective-permute-start | bytes 344072 | tf_op jit(solution)/shard_map/ppermute | solution.py:460
  37.2 6.2 %collective-permute-start.13 = (bf16[2,10,16,128]{3,2,1,0:T(8,128)(2,1)S(1)}, bf16[2,10,16,128]{3,2,1,0:T(8,128)(2,1)S(1)}, u32[]{:S(2)}, u32[]{:S(2)}) collective-permute-start(bf16[2,10,16,128]{3,2,1,0:T(8,128)(2,1)S(1)} %get-tuple-element.129), channel_id=1, source_target_pairs={{0,8},{1,2},{2,1},{3,4},{4,3},{5,6},{6,5},{7,15},{8,0},{9,10},{10,... | collective-permute-start | bytes 245768 | tf_op jit(solution)/shard_map/ppermute | solution.py:157
  37.9 5.5 %collective-permute-start.12 = (bf16[2,10,16,128]{3,2,1,0:T(8,128)(2,1)S(1)}, bf16[2,10,16,128]{3,2,1,0:T(8,128)(2,1)S(1)}, u32[]{:S(2)}, u32[]{:S(2)}) collective-permute-start(bf16[2,10,16,128]{3,2,1,0:T(8,128)(2,1)S(1)} %get-tuple-element.128), channel_id=1, source_target_pairs={{0,1},{1,0},{2,3},{3,2},{4,5},{5,4},{6,7},{7,6},{8,9},{9,8},{10,11... | collective-permute-start | bytes 245768 | tf_op jit(solution)/shard_map/ppermute | solution.py:157
  40.8 8.1 %copy-start = (bf16[27,128,128]{2,1,0:T(8,128)(2,1)S(1)}, bf16[27,128,128]{2,1,0:T(8,128)(2,1)}, u32[]{:S(2)}) copy-start(bf16[27,128,128]{2,1,0:T(8,128)(2,1)} %w.5) | copy-start | bytes 2654212
  40.8 7.8 %collective-permute-start.15 = (s16[448,128]{1,0:T(8,128)(2,1)S(1)}, s16[448,128]{1,0:T(8,128)(2,1)S(1)}, u32[]{:S(2)}, u32[]{:S(2)}) collective-permute-start(s16[448,128]{1,0:T(8,128)(2,1)S(1)} %shard_map.94.own), channel_id=1, source_target_pairs={{0,16},{8,24},{16,0},{24,8},{1,17},{9,25},{17,1},{25,9},{2,18},{10... | collective-permute-start | bytes 344072 | tf_op jit(solution)/shard_map/ppermute | solution.py:460
  48.7 4.9 %collective-permute-start.16 = (s16[448,128]{1,0:T(8,128)(2,1)S(1)}, s16[448,128]{1,0:T(8,128)(2,1)S(1)}, u32[]{:S(2)}, u32[]{:S(2)}) collective-permute-start(s16[448,128]{1,0:T(8,128)(2,1)S(1)} %shard_map.96.own), channel_id=1, source_target_pairs={{0,8},{8,0},{16,24},{24,16},{1,9},{9,1},{17,25},{25,17},{2,10},{10... | collective-permute-start | bytes 344072 | tf_op jit(solution)/shard_map/ppermute | solution.py:460

commit v4 on v3

--- a/solution.py
+++ b/solution.py
@@ -68,11 +68,11 @@
     return index % 2, one_if(index > 0), one_if(index < lax.axis_size(axis) - 1)
 
 
-def pack_sides(features, cotangent, occ, w):
+def pack_sides(features, cotangent, occ):
     size_x, size_y, size_z, channels = features.shape
     rows = size_y * size_z
 
-    def kernel(occ_hbm, first, second, w_hbm, mask, xa, xb, ya, yb, own, weights, occ_ref, sem, occ_sem, own_sem, w_sem):
+    def kernel(occ_hbm, first, second, mask, xa, xb, ya, yb, own, occ_ref, sem, occ_sem, own_sem):
         odd_x, odd_y = lax.axis_index("gx") % 2, lax.axis_index("gy") % 2
         first_x = pick(odd_x, size_x - 1, 0)
         first_y = pick(odd_y, size_y - 1, 0)
@@ -80,13 +80,12 @@
         columns = ((ya, first_y), (yb, size_y - 1 - first_y))
         occ_copy = pltpu.make_async_copy(occ_hbm, occ_ref, occ_sem)
         own_copy = pltpu.make_async_copy(first, own, own_sem)
-        w_copy = pltpu.make_async_copy(w_hbm, weights, w_sem)
         copies = []
         for n, (out, x) in enumerate(sides):
             copies.append(pltpu.make_async_copy(second.at[x], out.at[1], sem.at[n]))
         for n, (out, y) in enumerate(columns):
             copies.append(pltpu.make_async_copy(second.at[:, y], out.at[1], sem.at[2 + n]))
-        for copy in [occ_copy, own_copy, *copies, w_copy]:
+        for copy in [occ_copy, own_copy, *copies]:
             copy.start()
         occ_copy.wait()
         for n in range(size_x // BLOCK):
@@ -106,7 +105,6 @@
             at = pl.ds(pl.multiple_of(y * size_z, size_z), size_z)
             for x in range(size_x):
                 out[1, x] = out[1, x] * mask[x // BLOCK, at, :].astype(BF16)
-        w_copy.wait()
 
     side = pltpu.VMEM((2, size_y, size_z, channels), BF16)
     column = pltpu.VMEM((2, size_x, size_z, channels), BF16)
@@ -119,17 +117,16 @@
             column,
             column,
             pltpu.VMEM(features.shape, BF16),
-            pltpu.VMEM(w.shape, BF16),
         ),
-        [pltpu.with_memory_space_constraint(value, pltpu.HBM) for value in (occ, features, cotangent, w)],
-        [HBM] * 4,
+        [pltpu.with_memory_space_constraint(value, pltpu.HBM) for value in (occ, features, cotangent)],
+        [HBM] * 3,
         scratch=[
             pltpu.SMEM(occ.shape, jnp.int32),
             pltpu.SemaphoreType.DMA((4,)),
             pltpu.SemaphoreType.DMA(()),
             pltpu.SemaphoreType.DMA(()),
-            pltpu.SemaphoreType.DMA(()),
         ],
+        flops=8 << 30,
         nbytes=MIB,
         vmem=4 * MIB,
     )
@@ -153,9 +150,9 @@
 
 
 def swap_neighbours(axis, first, second):
-    return tuple(
-        lax.ppermute(value, ("gx", "gy"), swap_pairs(axis, odd)) for value, odd in ((first, False), (second, True))
-    )
+    second = lax.ppermute(second, ("gx", "gy"), swap_pairs(axis, True))
+    first = lax.ppermute(first, ("gx", "gy"), swap_pairs(axis, False))
+    return first, second
 
 
 def store_shifts(zc, x, ys, rows):
@@ -240,26 +237,29 @@
                 emit(x + 2 * h + side, both[h * rows : (h + 1) * rows, side * channels : (side + 1) * channels])
 
 
-def add_halo_terms(total, zc, taps):
+def side_weights(taps, which):
+    channels = taps.shape[2] // 2
+    return jnp.concatenate([taps[n, :, :channels] for n in which], axis=0)
+
+
+def add_side_terms(total, zc, taps):
     size_x, size_y, size_z = zc.shape[0] - 2, zc.shape[1] - 2, zc.shape[2]
     depth = zc.shape[3]
-    channels = depth // 3
     rows = size_y * size_z
-
-    def weights(which):
-        return jnp.concatenate([taps[n, :, :channels] for n in which], axis=0)
-
     for plane, x, first in ((0, 0, 0), (size_x + 1, size_x - 1, 6)):
         side = jnp.concatenate([zc[plane, j : j + size_y].reshape(rows, depth) for j in range(3)], axis=1)
-        total[x] += jnp.dot(side, weights((first, first + 1, first + 2)), preferred_element_type=F32)
-    none = jnp.zeros((size_z, depth), BF16)
+        weights = side_weights(taps, (first, first + 1, first + 2))
+        total[x] += jnp.dot(side, weights, preferred_element_type=F32)
+
+
+def add_column_terms(total, zc, taps):
+    size_x, size_y, size_z = zc.shape[0] - 2, zc.shape[1] - 2, zc.shape[2]
+    depth = zc.shape[3]
     for column, y, j in ((0, 0, 0), (size_y + 1, size_y - 1, 2)):
-        own = zc[1 : size_x + 1, column].reshape(size_x * size_z, depth)
-        below = jnp.concatenate([none, own[:-size_z]], axis=0)
-        above = jnp.concatenate([own[size_z:], none], axis=0)
-        side = jnp.concatenate([below, own, above], axis=1)
-        term = jnp.dot(side, weights((j, 3 + j, 6 + j)), preferred_element_type=F32)
-        total[:, y * size_z : (y + 1) * size_z, :] += term.reshape(size_x, size_z, channels)
+        pieces = [zc[i : i + size_x, column].reshape(size_x * size_z, depth) for i in range(3)]
+        weights = side_weights(taps, (j, 3 + j, 6 + j))
+        term = jnp.dot(jnp.concatenate(pieces, axis=1), weights, preferred_element_type=F32)
+        total[:, y * size_z : (y + 1) * size_z, :] += term.reshape(size_x, size_z, -1)
 
 
 def field_shape(shape):
@@ -271,34 +271,69 @@
     return (12, 3 * channels, 2 * channels)
 
 
+def own_shapes(shape):
+    size_x, size_y, size_z, channels = shape
+    return (
+        pltpu.VMEM(field_shape(shape), BF16),
+        pltpu.VMEM(taps_shape(channels), BF16),
+        pltpu.VMEM((size_x, size_y * size_z, channels), F32),
+    )
+
+
+def masked_plane(field, mask):
+    def plane(x):
+        value = field[x]
+        return value.reshape(-1, value.shape[2]) * mask[x // BLOCK].astype(BF16)
+
+    return plane
+
+
+def store_in(total):
+    def emit(x, value):
+        total[x] = value
+
+    return emit
+
+
 def own_terms(mask, field, w, lay):
     size_x, size_y, size_z, channels = field.shape
-    rows = size_y * size_z
 
     def kernel(mask, field, w, zc, taps, total):
-        def plane(x):
-            return field[x].reshape(rows, channels) * mask[x // BLOCK].astype(BF16)
-
-        fill_own(zc, plane)
+        fill_own(zc, masked_plane(field, mask))
         lay_weights(taps, lay(w))
-
-        def emit(x, value):
-            total[x] = value
-
-        convolve(zc, taps, emit)
+        convolve(zc, taps, store_in(total))
 
     return call(
         kernel,
-        (
-            pltpu.VMEM(field_shape(field.shape), BF16),
-            pltpu.VMEM(taps_shape(channels), BF16),
-            pltpu.VMEM((size_x, rows, channels), F32),
-        ),
+        own_shapes(field.shape),
         (mask, field, w),
         [],
-        flops=2 * 27 * size_x * rows * channels * channels,
+        flops=2 * 27 * field.size * channels,
         nbytes=4 * MIB,
         vmem=14 * MIB,
+    )
+
+
+def own_terms_and_sides(mask, field, w, zm, first_taps, pre, xa, xb):
+    channels = field.shape[3]
+
+    def kernel(mask, field, w, first_taps, xa, xb, zm_in, pre_in, zu, taps, total, zm, pre):
+        fill_own(zu, masked_plane(field, mask))
+        lay_weights(taps, turned(w))
+        convolve(zu, taps, store_in(total))
+        for f, (zc, weights, out) in enumerate(((zm, first_taps, pre), (zu, taps, total))):
+            fill_sides(zc, f, xa, xb)
+            add_side_terms(out, zc, weights)
+
+    return call(
+        kernel,
+        (*own_shapes(field.shape), pltpu.VMEM(zm.shape, BF16), pltpu.VMEM(pre.shape, F32)),
+        (mask, field, w, first_taps, xa, xb, zm, pre),
+        [],
+        flops=2 * 27 * field.size * channels,
+        nbytes=4 * MIB,
+        vmem=14 * MIB,
+        aliases={6: 3, 7: 4},
     )
 
 
@@ -344,24 +379,24 @@
         odd = block[(2 * j + 1) * share : (2 * j + 2) * share]
         at = jnp.bitwise_xor(place, j)
         keep[at, d] = pick(half, even, odd)
-        send[at, d] = pick(half, odd, even)
-
-
-def terms_shape(channels):
+        send[at, d] = pick(half, odd, even).astype(send.dtype)
+
+
+def terms_shape(channels, travel):
     count_y = lax.axis_size("gy")
-    return jax.ShapeDtypeStruct((count_y // 2, 27, channels // count_y, channels), F32)
-
-
-def hidden_and_terms(mask, halos, zm, zu, taps, pre, shape):
+    shape = (count_y // 2, 27, channels // count_y, channels)
+    return jax.ShapeDtypeStruct(shape, F32), jax.ShapeDtypeStruct(shape, travel)
+
+
+def hidden_and_terms(mask, ya, yb, zm, zu, taps, pre, shape):
     size_x, size_y, size_z, channels = shape
     rows = size_y * size_z
 
-    def kernel(mask, xa, xb, ya, yb, taps, pre, zm_in, zu_in, zm, zu, hidden, slope, keep, send):
+    def kernel(mask, ya, yb, taps, pre, zm_in, zu_in, zm, zu, hidden, slope, keep, send):
         for f, zc in enumerate((zm, zu)):
-            fill_sides(zc, f, xa, xb)
             fill_columns(zc, f, ya, yb)
         slope[...] = pre[...]
-        add_halo_terms(slope, zm, taps)
+        add_column_terms(slope, zm, taps)
         for x in range(size_x):
             here = mask[x // BLOCK]
             value = slope[x]
@@ -378,16 +413,15 @@
     field = jax.ShapeDtypeStruct(shape, BF16)
     wide = jax.ShapeDtypeStruct(pre.shape, F32)
     shifted = jax.ShapeDtypeStruct(zm.shape, BF16)
-    terms = terms_shape(channels)
     return call(
         kernel,
-        (shifted, shifted, field, wide, terms, terms),
-        (mask, *halos, taps, pre, zm, zu),
+        (shifted, shifted, field, wide, *terms_shape(channels, F32)),
+        (mask, ya, yb, taps, pre, zm, zu),
         [],
         flops=2 * 27 * size_x * rows * channels * channels,
         nbytes=8 * MIB,
         vmem=14 * MIB,
-        aliases={7: 0, 8: 1},
+        aliases={5: 0, 6: 1},
     )
 
 
@@ -398,7 +432,7 @@
 
     def kernel(hidden, slope, zm, zu, taps, grad, pre_grad, keep, send, xa, xb, ya, yb, total):
         total[...] = grad[...]
-        add_halo_terms(total, zu, taps)
+        add_column_terms(total, zu, taps)
         for x in range(size_x):
             pre_grad[x] = (total[x] * slope[x]).astype(BF16).reshape(size_y, size_z, channels)
         for f, value in enumerate((hidden, pre_grad)):
@@ -410,10 +444,9 @@
 
         grad_terms(left, zm, lambda i, j: (i, j), store)
 
-    terms = terms_shape(channels)
     return call(
         kernel,
-        (jax.ShapeDtypeStruct(shape, BF16), terms, terms, *side_shapes(shape)),
+        (jax.ShapeDtypeStruct(shape, BF16), *terms_shape(channels, BF16), *side_shapes(shape)),
         (hidden, slope, zm, zu, taps, grad),
         [],
         scratch=[pltpu.VMEM(grad.shape, F32)],
@@ -452,6 +485,33 @@
     )
 
 
+def add_halos(mask, own, zc, taps, total, f, halos):
+    size_x, size_y, size_z, channels = own.shape
+    rows = size_y * size_z
+
+    def kernel(mask, own, taps, total_in, xa, xb, ya, yb, zc_in, zc, out, total):
+        total[...] = total_in[...]
+        fill_sides(zc, f, xa, xb)
+        add_side_terms(total, zc, taps)
+        fill_columns(zc, f, ya, yb)
+        add_column_terms(total, zc, taps)
+        for x in range(size_x):
+            near = own[x].reshape(rows, channels).astype(F32)
+            value = mask[x // BLOCK] * (near + total[x])
+            out[x] = value.astype(BF16).reshape(size_y, size_z, channels)
+
+    return call(
+        kernel,
+        (pltpu.VMEM(zc.shape, BF16), jax.ShapeDtypeStruct(own.shape, BF16)),
+        (mask, own, taps, total, *halos, zc),
+        [],
+        scratch=[pltpu.VMEM(total.shape, F32)],
+        nbytes=3 * MIB,
+        vmem=14 * MIB,
+        aliases={8: 0},
+    )[1]
+
+
 def after(values, *others):
     return lax.optimization_barrier((values, others))[0]
 
@@ -473,7 +533,7 @@
     def kernel(keep, came, *refs):
         outs = refs[-places:]
         for p in range(places):
-            value = (keep[p] + came[p]).reshape(rows, channels)
+            value = (keep[p] + came[p].astype(F32)).reshape(rows, channels)
             if p == 0:
                 outs[0][g] = value
             elif p in near:
@@ -556,30 +616,53 @@
 
 def final_grads(own, came, taps, factor):
     rows, channels = came.shape[0] - CODE_ROWS, came.shape[1]
-
-    def kernel(own, came, second, first):
+    shape = (taps, rows // taps, channels)
+
+    def kernel(own, came, second, first, mine, other, sem):
         odd = lax.axis_index("gx") % 2
-        mine, other = decode(own) * factor, decode(came) * factor
-        second[...] = pick(odd, mine, other).reshape(second.shape)
-        first[...] = pick(odd, other, mine).reshape(first.shape)
-
-    shape = jax.ShapeDtypeStruct((taps, rows // taps, channels), F32)
-    return call(kernel, (shape, shape), (own, came), [], nbytes=MIB, vmem=4 * MIB)
+        mine[...] = (decode(own) * factor).reshape(shape)
+
+        def copies(value, is_odd, n):
+            return (
+                (odd == is_odd, pltpu.make_async_copy(value, second, sem.at[n])),
+                (odd != is_odd, pltpu.make_async_copy(value, first, sem.at[n])),
+            )
+
+        started = copies(mine, 0, 0)
+        for where, copy in started:
+            pl.when(where)(copy.start)
+        other[...] = (decode(came) * factor).reshape(shape)
+        later = copies(other, 1, 1)
+        for where, copy in later:
+            pl.when(where)(copy.start)
+        for where, copy in started + later:
+            pl.when(where)(copy.wait)
+
+    out = jax.ShapeDtypeStruct(shape, F32)
+    return pl.pallas_call(
+        kernel,
+        out_shape=(out, out),
+        in_specs=[VMEM, VMEM],
+        out_specs=(HBM, HBM),
+        scratch_shapes=[pltpu.VMEM(shape, F32), pltpu.VMEM(shape, F32), pltpu.SemaphoreType.DMA((2,))],
+        compiler_params=pltpu.CompilerParams(vmem_limit_bytes=4 * MIB),
+        cost_estimate=pl.CostEstimate(flops=0, bytes_accessed=MIB, transcendentals=0),
+    )(own, came)
 
 
 def body(features, w_first, w_second, occ, cotangent):
     count_x, count_y = lax.axis_size("gx"), lax.axis_size("gy")
     shape = features.shape
-    mask, xa, xb, ya, yb, own, weights = pack_sides(features, cotangent, occ, w_first)
+    mask, xa, xb, ya, yb, own = pack_sides(features, cotangent, occ)
     xa, xb = swap_neighbours("gx", xa, xb)
-    zm, first_taps, pre = own_terms(mask, own, weights, straight)
+    zm, first_taps, pre = own_terms(mask, own, w_first, straight)
     xa, xb = after((xa, xb), pre)
     ya, yb = finish_columns(xa, xb, ya, yb)
     behind = after(mask, ya)
     ya, yb = swap_neighbours("gy", ya, yb)
-    zu, second_taps, grad = own_terms(behind, cotangent, w_second, turned)
-    halos = after((xa, xb, ya, yb), grad)
-    zm, zu, hidden, slope, keep_second, send = hidden_and_terms(mask, halos, zm, zu, first_taps, pre, shape)
+    zu, second_taps, grad, zm, pre = own_terms_and_sides(behind, cotangent, w_second, zm, first_taps, pre, xa, xb)
+    ya, yb = after((ya, yb), grad)
+    zm, zu, hidden, slope, keep_second, send = hidden_and_terms(mask, ya, yb, zm, zu, first_taps, pre, shape)
     came = swap(send, "gy", 1)
     pre_grad, keep_first, send, xa, xb, ya, yb = pre_grad_and_terms(hidden, slope, zm, zu, second_taps, grad)
 
@@ -590,36 +673,30 @@
     (stays, *near), leaves = first_sum(1, keep_first, after(came, sums[0]), sums)
     near = [swap(value, "gy", 2 * p) for value, p in zip(near, (p for p in places if not is_far(p)))]
     far_first = [swap(value, "gy", 2 * p) for value, p in zip(leaves, filter(is_far, places))]
-    xa, xb = swap_neighbours("gx", *after((xa, xb), far_second, stays))
-    stays, leaves = second_sums(stays, *after((near, (far_second, far_first)), xa, xb))
+    behind = after(mask, far_second, stays)
+    zp, *own_pre = own_terms(behind, pre_grad, w_first, turned)
+    xa, xb = swap_neighbours("gx", *after((xa, xb), own_pre[1]))
+    stays, leaves = second_sums(stays, *after((near, (far_second, far_first)), own_pre[1]))
     xa, xb = after((xa, xb), leaves)
     came = swap(leaves, "gx", 1)
     ya, yb = finish_columns(xa, xb, ya, yb)
     came = after(came, ya)
     ya, yb = swap_neighbours("gy", ya, yb)
     stays = next_sum(stays, came)
-    convolutions = [
-        (mask, features, hidden, 0, w_second, straight),
-        (mask, cotangent, pre_grad, 1, w_first, turned),
-    ]
-    results = []
-
-    def convolve_beside(came, behind):
-        if len(results) == len(convolutions):
-            return came
-        mask, own, field, f, w, lay = convolutions[len(results)]
-        halos = after((xa, xb, ya, yb), behind)
-        results.append(add_convolution(mask, own, field, f, halos, w, lay))
-        return after(came, results[-1])
-
     bit = 2
     while bit < count_x:
-        stays = next_sum(stays, convolve_beside(swap(stays, "gx", bit), stays))
+        came = swap(stays, "gx", bit)
+        if bit == 2:
+            halos = after((xa, xb, ya, yb), stays)
+            output = add_convolution(mask, features, hidden, 0, halos, w_second, straight)
+            came = after(came, output)
+        stays = next_sum(stays, came)
         bit *= 2
-    came = convolve_beside(swap(stays, "gx", 1), stays)
+    came = swap(stays, "gx", 1)
+    grad_features = add_halos(mask, cotangent, zp, *own_pre, 1, after(halos, stays))
+    came = after(came, grad_features)
     factor = 1.0 / math.sqrt(count_x * count_y * shape[0] * shape[1] * shape[2])
     grad_second, grad_first = final_grads(stays, came, w_first.shape[0], factor)
-    output, grad_features = results
     return output, grad_features, grad_first, grad_second
 
 

time: 54.6 us -> 53.4 us (0.978)
  starting transfers between devices: 22.2 us -> 21.2 us
  waiting for transfers between devices: 9.41 us -> 8.68 us
    pallas_call x0 -> x1, Pallas kernels: none -> 0.81 us  [final_grads(): pl.pallas_call(kernel, out_shape=(out, out), in_specs=[VMEM, VMEM], out_s...]
    ppermute x9, waiting for transfers between devices: 8.76 us -> 8.03 us  [swap(): lax.ppermute(value, axis, [(i, i ^ bit) for i in range(lax.axis_size(axis...]
    ppermute x9, starting transfers between devices: 11.8 us -> 11.2 us  [swap(): lax.ppermute(value, axis, [(i, i ^ bit) for i in range(lax.axis_size(axis...]
  transfers between devices with their start and end apart: 17 -> 17, of which waited for: 6 -> 7; matrix products, arithmetic and copies ran while one was open for 0% -> 0% of each run, Pallas kernels for 30% -> 33%
where the time goes in v4:
time: 53.4 us; the launch traced here: 53.3 us
  Pallas kernels  22.5 us (42%)
  starting transfers between devices  21.2 us (40%)
  waiting for transfers between devices  8.68 us (16%)
  between operations  0.95 us (2%)
    pallas_call x15, Pallas kernels, call(): pl.pallas_call(kernel, out_shape=out_shapes, in_specs=list(spaces) + [VME...  21.7 us
    ppermute x9, starting transfers between devices, swap(): lax.ppermute(value, axis, [(i, i ^ bit) for i in range(lax.axis_size(axis...  11.2 us
    ppermute x9, waiting for transfers between devices, swap(): lax.ppermute(value, axis, [(i, i ^ bit) for i in range(lax.axis_size(axis...  8.03 us
    ppermute x4, starting transfers between devices, swap_neighbours(): first = lax.ppermute(first, ('gx', 'gy'), swap_pairs(axis, False))  6.16 us
    ppermute x4, starting transfers between devices, swap_neighbours(): second = lax.ppermute(second, ('gx', 'gy'), swap_pairs(axis, True))  3.76 us
  transfers between devices with their start and end apart: 17, of which 7 were waited for; matrix products, arithmetic and copies ran while one was open for 0% of the time, Pallas kernels for 33%

profile of v4, /device:TPU:0, one launch (start us, length us, event | category | flops | bytes accessed | tf_op | source)
XLA Modules:
  0.0 53.3 jit_solution(15241390169762539365)
XLA Ops:
  0.6 0.0 copy-start.2
  0.6 1.3 %shard_map.84 = (f32[1,256,128]{2,1,0:T(8,128)S(1)}, bf16[2,16,16,128]{3,2,1,0:T(8,128)(2,1)S(1)}, bf16[2,16,16,128]{3,2,1,0:T(8,128)(2,1)S(1)}, bf16[2,8,16,128...) custom-call(s32[1,2,2]{2,1,0:T(2,128)} %occ_hbm.1, ...), custom_call_target="tpu_custom_call" | custom-call | flops 8589934592 | bytes 1048576 | tf_op jit(solution)/shard_map/pallas_call | solution.py:19
  1.9 3.1 %collective-permute-start = (bf16[2,16,16,128]{3,2,1,0:T(8,128)(2,1)S(1)}, bf16[2,16,16,128]{3,2,1,0:T(8,128)(2,1)S(1)}, u32[]{:S(2)}, u32[]{:S(2)}) collective-permute-start(bf16[2,16,16,128]{3,2,1,0:T(8,128)(2,1)S(1)} %get-tuple-element.79), channel_id=1, source_target_pairs={{0,8},{1,9},{2,10},{3,11},{4,12},{5,13},{6,14},{7,15},{8,0},{9,1},... | collective-permute-start | bytes 393224 | tf_op jit(solution)/shard_map/ppermute | solution.py:154
  5.0 0.0 collective-permute-start.1
  5.0 0.0 copy-done.2
  5.0 0.0 copy-start
  5.0 0.0 copy-start.1
  5.0 2.8 %shard_map.85 = (bf16[10,18,16,384]{3,2,1,0:T(8,128)(2,1)S(1)}, bf16[12,384,256]{2,1,0:T(8,128)(2,1)S(1)}, f32[8,256,128]{2,1,0:T(8,128)S(1)}) custom-call(f32[1,256,128]{2,1,0:T(8,128)S(1)} %get-tuple-element.117.mask, bf16[8,16,16,128]{3,2,1,0:T(8,128)(2,1)S(1)} %get-tuple-element.81.field, bf16[27,128,128]{2,1,0:T(8,128)(2,1)S(1)} %copy-done.2), custom_call_target="tpu_custom_call" | custom-call | flops 1811939328 | bytes 4194304 | tf_op jit(solution)/shard_map/pallas_call | solution.py:19
  7.9 0.6 %collective-permute-done.xa = bf16[2,16,16,128]{3,2,1,0:T(8,128)(2,1)S(1)} collective-permute-done((bf16[2,16,16,128]{3,2,1,0:T(8,128)(2,1)S(1)}, bf16[2,16,16,128]{3,2,1,0:T(8,128)(2,1)S(1)}, u32[]{:S(2)}, u32[]{:S(2)}) %collective-permute-start) | collective-permute-done | bytes 131104 | tf_op jit(solution)/shard_map/ppermute | solution.py:154
  8.5 0.0 collective-permute-done.1.xb
  8.5 0.1 collective-permute-start.2
  8.6 2.9 %collective-permute-start.3 = (bf16[2,10,16,128]{3,2,1,0:T(8,128)(2,1)S(1)}, bf16[2,10,16,128]{3,2,1,0:T(8,128)(2,1)S(1)}, u32[]{:S(2)}, u32[]{:S(2)}) collective-permute-start(bf16[2,10,16,128]{3,2,1,0:T(8,128)(2,1)S(1)} %get-tuple-element.88), channel_id=1, source_target_pairs={{0,8},{1,2},{2,1},{3,4},{4,3},{5,6},{6,5},{7,15},{8,0},{9,10},{10,... | collective-permute-start | bytes 245768 | tf_op jit(solution)/shard_map/ppermute | solution.py:153
  11.5 0.0 copy-done
  11.5 0.0 copy-done.1
  11.5 3.4 %shard_map.87 = (bf16[10,18,16,384]{3,2,1,0:T(8,128)(2,1)S(1)}, bf16[12,384,256]{2,1,0:T(8,128)(2,1)S(1)}, f32[8,256,128]{2,1,0:T(8,128)S(1)}, bf16[10,18,16,384]{3,2,1,0:T(8,128)(2,1)S(1)}, f32[8,256,128]{2,1,0:T(8,128)S(1)}) custom-call(f32[1,256,128]{2,1,0:T(8,128)S(1)} %get-tuple-element.117.mask, ...), custom_call_target="tpu_custom_call", output_to_operand_aliasing={{3}: (6, {}), {4}: (7, {})} | custom-call | flops 1811939328 | bytes 4194304 | tf_op jit(solution)/shard_map/pallas_call | solution.py:19
  15.0 0.0 collective-permute-done.3.yb
  15.0 0.0 collective-permute-done.2.ya
  15.0 2.6 %shard_map.88 = (bf16[10,18,16,384]{3,2,1,0:T(8,128)(2,1)S(1)}, bf16[10,18,16,384]{3,2,1,0:T(8,128)(2,1)S(1)}, bf16[8,16,16,128]{3,2,1,0:T(8,128)(2,1)S(1)}, f32...) custom-call(f32[1,256,128]{2,1,0:T(8,128)S(1)} %get-tuple-element.11, ...), custom_call_target="tpu_custom_call", output_to_operand_aliasing={{0}: (5, {}), {1}: (6, {})} | custom-call | flops 1811939328 | bytes 8388608 | tf_op jit(solution)/shard_map/pallas_call | solution.py:19
  17.6 0.1 collective-permute-start.4
  17.7 2.6 %shard_map.89 = (bf16[8,16,16,128]{3,2,1,0:T(8,128)(2,1)S(1)}, f32[4,27,16,128]{3,2,1,0:T(8,128)S(1)}, bf16[4,27,16,128]{3,2,1,0:T(8,128)(2,1)S(1)}, bf16[2,16,1...) custom-call(bf16[8,16,16,128]{3,2,1,0:T(8,128)(2,1)S(1)} %get-tuple-, ...), custom_call_target="tpu_custom_call" | custom-call | flops 1811939328 | bytes 8388608 | tf_op jit(solution)/shard_map/pallas_call | solution.py:19
  20.3 0.6 %collective-permute-start.6 = (bf16[4,27,16,128]{3,2,1,0:T(8,128)(2,1)S(1)}, bf16[4,27,16,128]{3,2,1,0:T(8,128)(2,1)S(1)}, u32[]{:S(2)}, u32[]{:S(2)}) collective-permute-start(bf16[4,27,16,128]{3,2,1,0:T(8,128)(2,1)S(1)} %get-tuple-element.111), channel_id=1, source_target_pairs={{0,1},{1,0},{2,3},{3,2},{4,5},{5,4},{6,7},{7,6},{8,9},{9,8},{10,11... | collective-permute-start | bytes 1327112 | tf_op jit(solution)/shard_map/ppermute | solution.py:520
  20.8 0.0 collective-permute-done.4.came
  20.8 0.1 shard_map.90
  20.9 2.2 %collective-permute-start.5 = (bf16[432,128]{1,0:T(8,128)(2,1)S(1)}, bf16[432,128]{1,0:T(8,128)(2,1)S(1)}, u32[]{:S(2)}, u32[]{:S(2)}) collective-permute-start(bf16[432,128]{1,0:T(8,128)(2,1)S(1)} %get-tuple-element.109), channel_id=1, source_target_pairs={{0,6},{1,7},{2,4},{3,5},{4,2},{5,3},{6,0},{7,1},{8,14},{9,15},{10,... | collective-permute-start | bytes 331784 | tf_op jit(solution)/shard_map/ppermute | solution.py:520
  23.1 0.0 collective-permute-done.6.came
  23.1 0.1 shard_map.91
  23.2 1.7 %collective-permute-start.11 = (bf16[432,128]{1,0:T(8,128)(2,1)S(1)}, bf16[432,128]{1,0:T(8,128)(2,1)S(1)}, u32[]{:S(2)}, u32[]{:S(2)}) collective-permute-start(bf16[432,128]{1,0:T(8,128)(2,1)S(1)} %get-tuple-element.123), channel_id=1, source_target_pairs={{0,6},{1,7},{2,4},{3,5},{4,2},{5,3},{6,0},{7,1},{8,14},{9,15},{10,... | collective-permute-start | bytes 331784 | tf_op jit(solution)/shard_map/ppermute | solution.py:520
  24.9 0.0 collective-permute-start.9
  24.9 1.9 %collective-permute-start.10 = (bf16[2,432,128]{2,1,0:T(8,128)(2,1)S(1)}, bf16[2,432,128]{2,1,0:T(8,128)(2,1)S(1)}, u32[]{:S(2)}, u32[]{:S(2)}) collective-permute-start(bf16[2,432,128]{2,1,0:T(8,128)(2,1)S(1)} %get-tuple-element.122), channel_id=1, source_target_pairs={{0,4},{1,5},{2,6},{3,7},{4,0},{5,1},{6,2},{7,3},{8,12},{9,13},{10,... | collective-permute-start | bytes 663560 | tf_op jit(solution)/shard_map/ppermute | solution.py:520
  26.7 0.1 collective-permute-done.5.refs_2_
  26.9 0.0 copy-start.3
  26.9 3.0 %shard_map.92 = (bf16[10,18,16,384]{3,2,1,0:T(8,128)(2,1)S(1)}, bf16[12,384,256]{2,1,0:T(8,128)(2,1)S(1)}, f32[8,256,128]{2,1,0:T(8,128)S(1)}) custom-call(f32[1,256,128]{2,1,0:T(8,128)S(1)} %get-tuple-element.117.mask, bf16[8,16,16,128]{3,2,1,0:T(8,128)(2,1)S(1)} %get-tuple-element.107.field, bf16[27,128,128]{2,1,0:T(8,128)(2,1)S(1)} %copy-done.2), custom_call_target="tpu_custom_call" | custom-call | flops 1811939328 | bytes 4194304 | tf_op jit(solution)/shard_map/pallas_call | solution.py:19
  29.9 2.1 %collective-permute-start.7 = (bf16[2,16,16,128]{3,2,1,0:T(8,128)(2,1)S(1)}, bf16[2,16,16,128]{3,2,1,0:T(8,128)(2,1)S(1)}, u32[]{:S(2)}, u32[]{:S(2)}) collective-permute-start(bf16[2,16,16,128]{3,2,1,0:T(8,128)(2,1)S(1)} %get-tuple-element.119), channel_id=1, source_target_pairs={{0,8},{1,9},{2,10},{3,11},{4,12},{5,13},{6,14},{7,15},{8,0},{9,1},... | collective-permute-start | bytes 393224 | tf_op jit(solution)/shard_map/ppermute | solution.py:154
  32.0 0.0 collective-permute-start.8
  32.0 0.0 collective-permute-done.11.refs_3_
  32.0 1.3 %collective-permute-done.9.refs_0_ = bf16[2,432,128]{2,1,0:T(8,128)(2,1)S(1)} collective-permute-done((bf16[2,432,128]{2,1,0:T(8,128)(2,1)S(1)}, bf16[2,432,128]{2,1,0:T(8,128)(2,1)S(1)}, u32[]{:S(2)}, u32[]{:S(2)}) %collective-permute-start.9) | collective-permute-done | bytes 221216 | tf_op jit(solution)/shard_map/ppermute | solution.py:520
  33.2 0.8 %collective-permute-done.10.refs_1_ = bf16[2,432,128]{2,1,0:T(8,128)(2,1)S(1)} collective-permute-done((bf16[2,432,128]{2,1,0:T(8,128)(2,1)S(1)}, bf16[2,432,128]{2,1,0:T(8,128)(2,1)S(1)}, u32[]{:S(2)}, u32[]{:S(2)}) %collective-permute-start.10) | collective-permute-done | bytes 221216 | tf_op jit(solution)/shard_map/ppermute | solution.py:520
  34.1 0.2 shard_map.93
  34.3 1.9 %collective-permute-start.14 = (s16[448,128]{1,0:T(8,128)(2,1)S(1)}, s16[448,128]{1,0:T(8,128)(2,1)S(1)}, u32[]{:S(2)}, u32[]{:S(2)}) collective-permute-start(s16[448,128]{1,0:T(8,128)(2,1)S(1)} %get-tuple-element.128), channel_id=1, source_target_pairs={{0,8},{8,0},{16,24},{24,16},{1,9},{9,1},{17,25},{25,17},{2,10},{10... | collective-permute-start | bytes 344072 | tf_op jit(solution)/shard_map/ppermute | solution.py:520
  36.2 0.0 collective-permute-done.7.xa
  36.3 0.0 collective-permute-done.8.xb
  36.3 0.8 %collective-permute-start.13 = (bf16[2,10,16,128]{3,2,1,0:T(8,128)(2,1)S(1)}, bf16[2,10,16,128]{3,2,1,0:T(8,128)(2,1)S(1)}, u32[]{:S(2)}, u32[]{:S(2)}) collective-permute-start(bf16[2,10,16,128]{3,2,1,0:T(8,128)(2,1)S(1)} %get-tuple-element.134), channel_id=1, source_target_pairs={{0,8},{1,2},{2,1},{3,4},{4,3},{5,6},{6,5},{7,15},{8,0},{9,10},{10,... | collective-permute-start | bytes 245768 | tf_op jit(solution)/shard_map/ppermute | solution.py:153
  37.1 0.9 %collective-permute-start.12 = (bf16[2,10,16,128]{3,2,1,0:T(8,128)(2,1)S(1)}, bf16[2,10,16,128]{3,2,1,0:T(8,128)(2,1)S(1)}, u32[]{:S(2)}, u32[]{:S(2)}) collective-permute-start(bf16[2,10,16,128]{3,2,1,0:T(8,128)(2,1)S(1)} %get-tuple-element.133), channel_id=1, source_target_pairs={{0,1},{1,0},{2,3},{3,2},{4,5},{5,4},{6,7},{7,6},{8,9},{9,8},{10,11... | collective-permute-start | bytes 245768 | tf_op jit(solution)/shard_map/ppermute | solution.py:154
  38.1 1.4 %collective-permute-done.14.came = s16[448,128]{1,0:T(8,128)(2,1)S(1)} collective-permute-done((s16[448,128]{1,0:T(8,128)(2,1)S(1)}, s16[448,128]{1,0:T(8,128)(2,1)S(1)}, u32[]{:S(2)}, u32[]{:S(2)}) %collective-permute-start.14) | collective-permute-done | bytes 114720 | tf_op jit(solution)/shard_map/ppermute | solution.py:520
  39.4 0.2 shard_map.95.own
  39.6 2.9 %collective-permute-start.15 = (s16[448,128]{1,0:T(8,128)(2,1)S(1)}, s16[448,128]{1,0:T(8,128)(2,1)S(1)}, u32[]{:S(2)}, u32[]{:S(2)}) collective-permute-start(s16[448,128]{1,0:T(8,128)(2,1)S(1)} %shard_map.95.own), channel_id=1, source_target_pairs={{0,16},{8,24},{16,0},{24,8},{1,17},{9,25},{17,1},{25,9},{2,18},{10... | collective-permute-start | bytes 344072 | tf_op jit(solution)/shard_map/ppermute | solution.py:520
  42.5 0.0 collective-permute-done.13.yb
  42.5 0.0 collective-permute-done.12.ya
  42.5 0.0 copy-done.3
  42.5 3.6 %shard_map.96 = bf16[8,16,16,128]{3,2,1,0:T(8,128)(2,1)} custom-call(f32[1,256,128]{2,1,0:T(8,128)S(1)} %get-tuple-element.117.mask, bf16[8,16,16,128]{3,2,1,0:T(8,128)(2,1)S(1)} %copy-done.3, bf16[8,16,16,128]{3,2,1,0:T(8,128)(2,1)S(1)} %get-tuple-element.98.hidden.field, bf16[2,16,16,128]{3,2,1,0:T(8,128)(2,1)S(1)} %collective-permute-done.7.xa, ...), custom_call_target="tpu_custom_call" | custom-call | flops 1811939328 | bytes 3145728 | tf_op jit(solution)/shard_map/pallas_call | solution.py:19
  46.1 1.1 %collective-permute-done.15.came = s16[448,128]{1,0:T(8,128)(2,1)S(1)} collective-permute-done((s16[448,128]{1,0:T(8,128)(2,1)S(1)}, s16[448,128]{1,0:T(8,128)(2,1)S(1)}, u32[]{:S(2)}, u32[]{:S(2)}) %collective-permute-start.15) | collective-permute-done | bytes 114720 | tf_op jit(solution)/shard_map/ppermute | solution.py:520
  47.2 0.2 shard_map.97.own
  47.4 0.1 collective-permute-start.16
  47.5 1.5 %shard_map.98 = (bf16[10,18,16,384]{3,2,1,0:T(8,128)(2,1)S(1)}, bf16[8,16,16,128]{3,2,1,0:T(8,128)(2,1)}) custom-call(f32[1,256,128]{2,1,0:T(8,128)S(1)} %get-tuple-element.117.mask, bf16[8,16,16,128]{3,2,1,0:T(8,128)(2,1)S(1)} %copy-done, bf16[12,384,256]{2,1,0:T(8,128)(2,1)S(1)} %get-tuple-element.141.taps, ...), custom_call_target="tpu_custom_call", output_to_operand_aliasing={{0}: (8, {})} | custom-call | bytes 3145728 | tf_op jit(solution)/shard_map/pallas_call | solution.py:19
  49.0 3.3 %collective-permute-done.16.came = s16[448,128]{1,0:T(8,128)(2,1)S(1)} collective-permute-done((s16[448,128]{1,0:T(8,128)(2,1)S(1)}, s16[448,128]{1,0:T(8,128)(2,1)S(1)}, u32[]{:S(2)}, u32[]{:S(2)}) %collective-permute-start.16) | collective-permute-done | bytes 114720 | tf_op jit(solution)/shard_map/ppermute | solution.py:520
  52.3 0.8 %shard_map.99 = (f32[27,16,128]{2,1,0:T(8,128)}, f32[27,16,128]{2,1,0:T(8,128)}) custom-call(s16[448,128]{1,0:T(8,128)(2,1)S(1)} %shard_map.97.own, s16[448,128]{1,0:T(8,128)(2,1)S(1)} %collective-permute-done.16.came), custom_call_target="tpu_custom_call" | custom-call | bytes 1048576 | tf_op jit(solution)/shard_map/pallas_call | solution.py:642
  (2 shorter events, 0.1 us)
Async XLA Ops:
  0.6 4.4 %copy-start.2 = (bf16[27,128,128]{2,1,0:T(8,128)(2,1)S(1)}, bf16[27,128,128]{2,1,0:T(8,128)(2,1)}, u32[]{:S(2)}) copy-start(bf16[27,128,128]{2,1,0:T(8,128)(2,1)} %w.6) | copy-start | bytes 2654212
  1.9 6.6 %collective-permute-start = (bf16[2,16,16,128]{3,2,1,0:T(8,128)(2,1)S(1)}, bf16[2,16,16,128]{3,2,1,0:T(8,128)(2,1)S(1)}, u32[]{:S(2)}, u32[]{:S(2)}) collective-permute-start(bf16[2,16,16,128]{3,2,1,0:T(8,128)(2,1)S(1)} %get-tuple-element.79), channel_id=1, source_target_pairs={{0,8},{1,9},{2,10},{3,11},{4,12},{5,13},{6,14},{7,15},{8,0},{9,1},... | collective-permute-start | bytes 393224 | tf_op jit(solution)/shard_map/ppermute | solution.py:154
  5.0 3.5 %collective-permute-start.1 = (bf16[2,16,16,128]{3,2,1,0:T(8,128)(2,1)S(1)}, bf16[2,16,16,128]{3,2,1,0:T(8,128)(2,1)S(1)}, u32[]{:S(2)}, u32[]{:S(2)}) collective-permute-start(bf16[2,16,16,128]{3,2,1,0:T(8,128)(2,1)S(1)} %get-tuple-element.80), channel_id=1, source_target_pairs={{0,1},{1,0},{2,3},{3,2},{4,5},{5,4},{6,7},{7,6},{8,16},{9,17},{10,... | collective-permute-start | bytes 393224 | tf_op jit(solution)/shard_map/ppermute | solution.py:153
  5.0 6.5 %copy-start = (bf16[8,16,16,128]{3,2,1,0:T(8,128)(2,1)S(1)}, bf16[8,16,16,128]{3,2,1,0:T(8,128)(2,1)}, u32[]{:S(2)}) copy-start(bf16[8,16,16,128]{3,2,1,0:T(8,128)(2,1)} %own.3) | copy-start | bytes 1572868
  5.0 6.5 %copy-start.1 = (bf16[27,128,128]{2,1,0:T(8,128)(2,1)S(1)}, bf16[27,128,128]{2,1,0:T(8,128)(2,1)}, u32[]{:S(2)}) copy-start(bf16[27,128,128]{2,1,0:T(8,128)(2,1)} %w.7) | copy-start | bytes 2654212
  8.5 6.5 %collective-permute-start.2 = (bf16[2,10,16,128]{3,2,1,0:T(8,128)(2,1)S(1)}, bf16[2,10,16,128]{3,2,1,0:T(8,128)(2,1)S(1)}, u32[]{:S(2)}, u32[]{:S(2)}) collective-permute-start(bf16[2,10,16,128]{3,2,1,0:T(8,128)(2,1)S(1)} %get-tuple-element.87), channel_id=1, source_target_pairs={{0,1},{1,0},{2,3},{3,2},{4,5},{5,4},{6,7},{7,6},{8,9},{9,8},{10,11... | collective-permute-start | bytes 245768 | tf_op jit(solution)/shard_map/ppermute | solution.py:154
  8.6 6.4 %collective-permute-start.3 = (bf16[2,10,16,128]{3,2,1,0:T(8,128)(2,1)S(1)}, bf16[2,10,16,128]{3,2,1,0:T(8,128)(2,1)S(1)}, u32[]{:S(2)}, u32[]{:S(2)}) collective-permute-start(bf16[2,10,16,128]{3,2,1,0:T(8,128)(2,1)S(1)} %get-tuple-element.88), channel_id=1, source_target_pairs={{0,8},{1,2},{2,1},{3,4},{4,3},{5,6},{6,5},{7,15},{8,0},{9,10},{10,... | collective-permute-start | bytes 245768 | tf_op jit(solution)/shard_map/ppermute | solution.py:153
  17.6 3.2 %collective-permute-start.4 = (f32[4,27,16,128]{3,2,1,0:T(8,128)S(1)}, f32[4,27,16,128]{3,2,1,0:T(8,128)S(1)}, u32[]{:S(2)}, u32[]{:S(2)}) collective-permute-start(f32[4,27,16,128]{3,2,1,0:T(8,128)S(1)} %get-tuple-element.106), channel_id=1, source_target_pairs={{0,1},{1,0},{2,3},{3,2},{4,5},{5,4},{6,7},{7,6},{8,9},{9,8},{10,11... | collective-permute-start | bytes 2654216 | tf_op jit(solution)/shard_map/ppermute | solution.py:520
  20.3 2.8 %collective-permute-start.6 = (bf16[4,27,16,128]{3,2,1,0:T(8,128)(2,1)S(1)}, bf16[4,27,16,128]{3,2,1,0:T(8,128)(2,1)S(1)}, u32[]{:S(2)}, u32[]{:S(2)}) collective-permute-start(bf16[4,27,16,128]{3,2,1,0:T(8,128)(2,1)S(1)} %get-tuple-element.111), channel_id=1, source_target_pairs={{0,1},{1,0},{2,3},{3,2},{4,5},{5,4},{6,7},{7,6},{8,9},{9,8},{10,11... | collective-permute-start | bytes 1327112 | tf_op jit(solution)/shard_map/ppermute | solution.py:520
  20.9 6.0 %collective-permute-start.5 = (bf16[432,128]{1,0:T(8,128)(2,1)S(1)}, bf16[432,128]{1,0:T(8,128)(2,1)S(1)}, u32[]{:S(2)}, u32[]{:S(2)}) collective-permute-start(bf16[432,128]{1,0:T(8,128)(2,1)S(1)} %get-tuple-element.109), channel_id=1, source_target_pairs={{0,6},{1,7},{2,4},{3,5},{4,2},{5,3},{6,0},{7,1},{8,14},{9,15},{10,... | collective-permute-start | bytes 331784 | tf_op jit(solution)/shard_map/ppermute | solution.py:520
  23.2 8.8 %collective-permute-start.11 = (bf16[432,128]{1,0:T(8,128)(2,1)S(1)}, bf16[432,128]{1,0:T(8,128)(2,1)S(1)}, u32[]{:S(2)}, u32[]{:S(2)}) collective-permute-start(bf16[432,128]{1,0:T(8,128)(2,1)S(1)} %get-tuple-element.123), channel_id=1, source_target_pairs={{0,6},{1,7},{2,4},{3,5},{4,2},{5,3},{6,0},{7,1},{8,14},{9,15},{10,... | collective-permute-start | bytes 331784 | tf_op jit(solution)/shard_map/ppermute | solution.py:520
  24.9 8.4 %collective-permute-start.9 = (bf16[2,432,128]{2,1,0:T(8,128)(2,1)S(1)}, bf16[2,432,128]{2,1,0:T(8,128)(2,1)S(1)}, u32[]{:S(2)}, u32[]{:S(2)}) collective-permute-start(bf16[2,432,128]{2,1,0:T(8,128)(2,1)S(1)} %get-tuple-element.121), channel_id=1, source_target_pairs={{0,2},{1,3},{2,0},{3,1},{4,6},{5,7},{6,4},{7,5},{8,10},{9,11},{10,... | collective-permute-start | bytes 663560 | tf_op jit(solution)/shard_map/ppermute | solution.py:520
  24.9 9.2 %collective-permute-start.10 = (bf16[2,432,128]{2,1,0:T(8,128)(2,1)S(1)}, bf16[2,432,128]{2,1,0:T(8,128)(2,1)S(1)}, u32[]{:S(2)}, u32[]{:S(2)}) collective-permute-start(bf16[2,432,128]{2,1,0:T(8,128)(2,1)S(1)} %get-tuple-element.122), channel_id=1, source_target_pairs={{0,4},{1,5},{2,6},{3,7},{4,0},{5,1},{6,2},{7,3},{8,12},{9,13},{10,... | collective-permute-start | bytes 663560 | tf_op jit(solution)/shard_map/ppermute | solution.py:520
  26.9 15.6 %copy-start.3 = (bf16[8,16,16,128]{3,2,1,0:T(8,128)(2,1)S(1)}, bf16[8,16,16,128]{3,2,1,0:T(8,128)(2,1)}, u32[]{:S(2)}) copy-start(bf16[8,16,16,128]{3,2,1,0:T(8,128)(2,1)} %own.2) | copy-start | bytes 1572868
  29.9 6.3 %collective-permute-start.7 = (bf16[2,16,16,128]{3,2,1,0:T(8,128)(2,1)S(1)}, bf16[2,16,16,128]{3,2,1,0:T(8,128)(2,1)S(1)}, u32[]{:S(2)}, u32[]{:S(2)}) collective-permute-start(bf16[2,16,16,128]{3,2,1,0:T(8,128)(2,1)S(1)} %get-tuple-element.119), channel_id=1, source_target_pairs={{0,8},{1,9},{2,10},{3,11},{4,12},{5,13},{6,14},{7,15},{8,0},{9,1},... | collective-permute-start | bytes 393224 | tf_op jit(solution)/shard_map/ppermute | solution.py:154
  32.0 4.3 %collective-permute-start.8 = (bf16[2,16,16,128]{3,2,1,0:T(8,128)(2,1)S(1)}, bf16[2,16,16,128]{3,2,1,0:T(8,128)(2,1)S(1)}, u32[]{:S(2)}, u32[]{:S(2)}) collective-permute-start(bf16[2,16,16,128]{3,2,1,0:T(8,128)(2,1)S(1)} %get-tuple-element.120), channel_id=1, source_target_pairs={{0,1},{1,0},{2,3},{3,2},{4,5},{5,4},{6,7},{7,6},{8,16},{9,17},{10,... | collective-permute-start | bytes 393224 | tf_op jit(solution)/shard_map/ppermute | solution.py:153
  34.3 5.1 %collective-permute-start.14 = (s16[448,128]{1,0:T(8,128)(2,1)S(1)}, s16[448,128]{1,0:T(8,128)(2,1)S(1)}, u32[]{:S(2)}, u32[]{:S(2)}) collective-permute-start(s16[448,128]{1,0:T(8,128)(2,1)S(1)} %get-tuple-element.128), channel_id=1, source_target_pairs={{0,8},{8,0},{16,24},{24,16},{1,9},{9,1},{17,25},{25,17},{2,10},{10... | collective-permute-start | bytes 344072 | tf_op jit(solution)/shard_map/ppermute | solution.py:520
  36.3 6.2 %collective-permute-start.13 = (bf16[2,10,16,128]{3,2,1,0:T(8,128)(2,1)S(1)}, bf16[2,10,16,128]{3,2,1,0:T(8,128)(2,1)S(1)}, u32[]{:S(2)}, u32[]{:S(2)}) collective-permute-start(bf16[2,10,16,128]{3,2,1,0:T(8,128)(2,1)S(1)} %get-tuple-element.134), channel_id=1, source_target_pairs={{0,8},{1,2},{2,1},{3,4},{4,3},{5,6},{6,5},{7,15},{8,0},{9,10},{10,... | collective-permute-start | bytes 245768 | tf_op jit(solution)/shard_map/ppermute | solution.py:153
  37.1 5.4 %collective-permute-start.12 = (bf16[2,10,16,128]{3,2,1,0:T(8,128)(2,1)S(1)}, bf16[2,10,16,128]{3,2,1,0:T(8,128)(2,1)S(1)}, u32[]{:S(2)}, u32[]{:S(2)}) collective-permute-start(bf16[2,10,16,128]{3,2,1,0:T(8,128)(2,1)S(1)} %get-tuple-element.133), channel_id=1, source_target_pairs={{0,1},{1,0},{2,3},{3,2},{4,5},{5,4},{6,7},{7,6},{8,9},{9,8},{10,11... | collective-permute-start | bytes 245768 | tf_op jit(solution)/shard_map/ppermute | solution.py:154
  39.6 7.6 %collective-permute-start.15 = (s16[448,128]{1,0:T(8,128)(2,1)S(1)}, s16[448,128]{1,0:T(8,128)(2,1)S(1)}, u32[]{:S(2)}, u32[]{:S(2)}) collective-permute-start(s16[448,128]{1,0:T(8,128)(2,1)S(1)} %shard_map.95.own), channel_id=1, source_target_pairs={{0,16},{8,24},{16,0},{24,8},{1,17},{9,25},{17,1},{25,9},{2,18},{10... | collective-permute-start | bytes 344072 | tf_op jit(solution)/shard_map/ppermute | solution.py:520
  47.4 4.9 %collective-permute-start.16 = (s16[448,128]{1,0:T(8,128)(2,1)S(1)}, s16[448,128]{1,0:T(8,128)(2,1)S(1)}, u32[]{:S(2)}, u32[]{:S(2)}) collective-permute-start(s16[448,128]{1,0:T(8,128)(2,1)S(1)} %shard_map.97.own), channel_id=1, source_target_pairs={{0,8},{8,0},{16,24},{24,16},{1,9},{9,1},{17,25},{25,17},{2,10},{10... | collective-permute-start | bytes 344072 | tf_op jit(solution)/shard_map/ppermute | solution.py:520

commit v5 on v4

--- a/solution.py
+++ b/solution.py
@@ -446,7 +446,7 @@
 
     return call(
         kernel,
-        (jax.ShapeDtypeStruct(shape, BF16), *terms_shape(channels, BF16), *side_shapes(shape)),
+        (jax.ShapeDtypeStruct(shape, BF16), *terms_shape(channels, F32), *side_shapes(shape)),
         (hidden, slope, zm, zu, taps, grad),
         [],
         scratch=[pltpu.VMEM(grad.shape, F32)],

time: 53.4 us -> 53.1 us (level)
  no operation moved by 1% of the time
where the time goes in v5:
time: 53.1 us; the launch traced here: 52.9 us
  Pallas kernels  22.4 us (42%)
  starting transfers between devices  21.2 us (40%)
  waiting for transfers between devices  8.37 us (16%)
  between operations  0.95 us (2%)
    pallas_call x15, Pallas kernels, call(): pl.pallas_call(kernel, out_shape=out_shapes, in_specs=list(spaces) + [VME...  21.6 us
    ppermute x9, starting transfers between devices, swap(): lax.ppermute(value, axis, [(i, i ^ bit) for i in range(lax.axis_size(axis...  11.4 us
    ppermute x9, waiting for transfers between devices, swap(): lax.ppermute(value, axis, [(i, i ^ bit) for i in range(lax.axis_size(axis...  7.73 us
    ppermute x4, starting transfers between devices, swap_neighbours(): first = lax.ppermute(first, ('gx', 'gy'), swap_pairs(axis, False))  6.05 us
    ppermute x4, starting transfers between devices, swap_neighbours(): second = lax.ppermute(second, ('gx', 'gy'), swap_pairs(axis, True))  3.72 us
  transfers between devices with their start and end apart: 17, of which 7 were waited for; matrix products, arithmetic and copies ran while one was open for 0% of the time, Pallas kernels for 33%

profile of v5, /device:TPU:0, one launch (start us, length us, event | category | flops | bytes accessed | tf_op | source)
XLA Modules:
  0.0 52.9 jit_solution(8245581784352181877)
XLA Ops:
  0.6 0.0 copy-start.2
  0.6 1.3 %shard_map.84 = (f32[1,256,128]{2,1,0:T(8,128)S(1)}, bf16[2,16,16,128]{3,2,1,0:T(8,128)(2,1)S(1)}, bf16[2,16,16,128]{3,2,1,0:T(8,128)(2,1)S(1)}, bf16[2,8,16,128...) custom-call(s32[1,2,2]{2,1,0:T(2,128)} %occ_hbm.1, ...), custom_call_target="tpu_custom_call" | custom-call | flops 8589934592 | bytes 1048576 | tf_op jit(solution)/shard_map/pallas_call | solution.py:19
  1.9 3.1 %collective-permute-start = (bf16[2,16,16,128]{3,2,1,0:T(8,128)(2,1)S(1)}, bf16[2,16,16,128]{3,2,1,0:T(8,128)(2,1)S(1)}, u32[]{:S(2)}, u32[]{:S(2)}) collective-permute-start(bf16[2,16,16,128]{3,2,1,0:T(8,128)(2,1)S(1)} %get-tuple-element.79), channel_id=1, source_target_pairs={{0,8},{1,9},{2,10},{3,11},{4,12},{5,13},{6,14},{7,15},{8,0},{9,1},... | collective-permute-start | bytes 393224 | tf_op jit(solution)/shard_map/ppermute | solution.py:154
  5.0 0.0 collective-permute-start.1
  5.0 0.0 copy-done.2
  5.0 0.0 copy-start
  5.0 0.0 copy-start.1
  5.0 2.8 %shard_map.85 = (bf16[10,18,16,384]{3,2,1,0:T(8,128)(2,1)S(1)}, bf16[12,384,256]{2,1,0:T(8,128)(2,1)S(1)}, f32[8,256,128]{2,1,0:T(8,128)S(1)}) custom-call(f32[1,256,128]{2,1,0:T(8,128)S(1)} %get-tuple-element.117.mask, bf16[8,16,16,128]{3,2,1,0:T(8,128)(2,1)S(1)} %get-tuple-element.81.field, bf16[27,128,128]{2,1,0:T(8,128)(2,1)S(1)} %copy-done.2), custom_call_target="tpu_custom_call" | custom-call | flops 1811939328 | bytes 4194304 | tf_op jit(solution)/shard_map/pallas_call | solution.py:19
  7.9 0.6 %collective-permute-done.xa = bf16[2,16,16,128]{3,2,1,0:T(8,128)(2,1)S(1)} collective-permute-done((bf16[2,16,16,128]{3,2,1,0:T(8,128)(2,1)S(1)}, bf16[2,16,16,128]{3,2,1,0:T(8,128)(2,1)S(1)}, u32[]{:S(2)}, u32[]{:S(2)}) %collective-permute-start) | collective-permute-done | bytes 131104 | tf_op jit(solution)/shard_map/ppermute | solution.py:154
  8.5 0.0 collective-permute-done.1.xb
  8.5 0.1 collective-permute-start.2
  8.6 2.9 %collective-permute-start.3 = (bf16[2,10,16,128]{3,2,1,0:T(8,128)(2,1)S(1)}, bf16[2,10,16,128]{3,2,1,0:T(8,128)(2,1)S(1)}, u32[]{:S(2)}, u32[]{:S(2)}) collective-permute-start(bf16[2,10,16,128]{3,2,1,0:T(8,128)(2,1)S(1)} %get-tuple-element.88), channel_id=1, source_target_pairs={{0,8},{1,2},{2,1},{3,4},{4,3},{5,6},{6,5},{7,15},{8,0},{9,10},{10,... | collective-permute-start | bytes 245768 | tf_op jit(solution)/shard_map/ppermute | solution.py:153
  11.5 0.0 copy-done
  11.5 0.0 copy-done.1
  11.5 3.4 %shard_map.87 = (bf16[10,18,16,384]{3,2,1,0:T(8,128)(2,1)S(1)}, bf16[12,384,256]{2,1,0:T(8,128)(2,1)S(1)}, f32[8,256,128]{2,1,0:T(8,128)S(1)}, bf16[10,18,16,384]{3,2,1,0:T(8,128)(2,1)S(1)}, f32[8,256,128]{2,1,0:T(8,128)S(1)}) custom-call(f32[1,256,128]{2,1,0:T(8,128)S(1)} %get-tuple-element.117.mask, ...), custom_call_target="tpu_custom_call", output_to_operand_aliasing={{3}: (6, {}), {4}: (7, {})} | custom-call | flops 1811939328 | bytes 4194304 | tf_op jit(solution)/shard_map/pallas_call | solution.py:19
  15.0 0.0 collective-permute-done.3.yb
  15.0 0.0 collective-permute-done.2.ya
  15.0 2.6 %shard_map.88 = (bf16[10,18,16,384]{3,2,1,0:T(8,128)(2,1)S(1)}, bf16[10,18,16,384]{3,2,1,0:T(8,128)(2,1)S(1)}, bf16[8,16,16,128]{3,2,1,0:T(8,128)(2,1)S(1)}, f32...) custom-call(f32[1,256,128]{2,1,0:T(8,128)S(1)} %get-tuple-element.11, ...), custom_call_target="tpu_custom_call", output_to_operand_aliasing={{0}: (5, {}), {1}: (6, {})} | custom-call | flops 1811939328 | bytes 8388608 | tf_op jit(solution)/shard_map/pallas_call | solution.py:19
  17.6 0.1 collective-permute-start.4
  17.7 2.6 %shard_map.89 = (bf16[8,16,16,128]{3,2,1,0:T(8,128)(2,1)S(1)}, f32[4,27,16,128]{3,2,1,0:T(8,128)S(1)}, f32[4,27,16,128]{3,2,1,0:T(8,128)S(1)}, bf16[2,16,16,128]...) custom-call(bf16[8,16,16,128]{3,2,1,0:T(8,128)(2,1)S(1)} %get-tuple-, ...), custom_call_target="tpu_custom_call" | custom-call | flops 1811939328 | bytes 8388608 | tf_op jit(solution)/shard_map/pallas_call | solution.py:19
  20.3 0.6 %collective-permute-start.6 = (f32[4,27,16,128]{3,2,1,0:T(8,128)S(1)}, f32[4,27,16,128]{3,2,1,0:T(8,128)S(1)}, u32[]{:S(2)}, u32[]{:S(2)}) collective-permute-start(f32[4,27,16,128]{3,2,1,0:T(8,128)S(1)} %get-tuple-element.111), channel_id=1, source_target_pairs={{0,1},{1,0},{2,3},{3,2},{4,5},{5,4},{6,7},{7,6},{8,9},{9,8},{10,11... | collective-permute-start | bytes 2654216 | tf_op jit(solution)/shard_map/ppermute | solution.py:520
  20.8 0.0 collective-permute-done.4.came
  20.8 0.1 shard_map.90
  20.9 2.2 %collective-permute-start.5 = (bf16[432,128]{1,0:T(8,128)(2,1)S(1)}, bf16[432,128]{1,0:T(8,128)(2,1)S(1)}, u32[]{:S(2)}, u32[]{:S(2)}) collective-permute-start(bf16[432,128]{1,0:T(8,128)(2,1)S(1)} %get-tuple-element.109), channel_id=1, source_target_pairs={{0,6},{1,7},{2,4},{3,5},{4,2},{5,3},{6,0},{7,1},{8,14},{9,15},{10,... | collective-permute-start | bytes 331784 | tf_op jit(solution)/shard_map/ppermute | solution.py:520
  23.1 0.0 collective-permute-done.6.came
  23.1 0.1 shard_map.91
  23.2 2.3 %collective-permute-start.11 = (bf16[432,128]{1,0:T(8,128)(2,1)S(1)}, bf16[432,128]{1,0:T(8,128)(2,1)S(1)}, u32[]{:S(2)}, u32[]{:S(2)}) collective-permute-start(bf16[432,128]{1,0:T(8,128)(2,1)S(1)} %get-tuple-element.123), channel_id=1, source_target_pairs={{0,6},{1,7},{2,4},{3,5},{4,2},{5,3},{6,0},{7,1},{8,14},{9,15},{10,... | collective-permute-start | bytes 331784 | tf_op jit(solution)/shard_map/ppermute | solution.py:520
  25.5 0.0 collective-permute-start.9
  25.5 1.2 %collective-permute-start.10 = (bf16[2,432,128]{2,1,0:T(8,128)(2,1)S(1)}, bf16[2,432,128]{2,1,0:T(8,128)(2,1)S(1)}, u32[]{:S(2)}, u32[]{:S(2)}) collective-permute-start(bf16[2,432,128]{2,1,0:T(8,128)(2,1)S(1)} %get-tuple-element.122), channel_id=1, source_target_pairs={{0,4},{1,5},{2,6},{3,7},{4,0},{5,1},{6,2},{7,3},{8,12},{9,13},{10,... | collective-permute-start | bytes 663560 | tf_op jit(solution)/shard_map/ppermute | solution.py:520
  26.7 0.1 collective-permute-done.5.refs_2_
  26.9 0.0 copy-start.3
  26.9 3.0 %shard_map.92 = (bf16[10,18,16,384]{3,2,1,0:T(8,128)(2,1)S(1)}, bf16[12,384,256]{2,1,0:T(8,128)(2,1)S(1)}, f32[8,256,128]{2,1,0:T(8,128)S(1)}) custom-call(f32[1,256,128]{2,1,0:T(8,128)S(1)} %get-tuple-element.117.mask, bf16[8,16,16,128]{3,2,1,0:T(8,128)(2,1)S(1)} %get-tuple-element.107.field, bf16[27,128,128]{2,1,0:T(8,128)(2,1)S(1)} %copy-done.2), custom_call_target="tpu_custom_call" | custom-call | flops 1811939328 | bytes 4194304 | tf_op jit(solution)/shard_map/pallas_call | solution.py:19
  29.9 1.9 %collective-permute-start.7 = (bf16[2,16,16,128]{3,2,1,0:T(8,128)(2,1)S(1)}, bf16[2,16,16,128]{3,2,1,0:T(8,128)(2,1)S(1)}, u32[]{:S(2)}, u32[]{:S(2)}) collective-permute-start(bf16[2,16,16,128]{3,2,1,0:T(8,128)(2,1)S(1)} %get-tuple-element.119), channel_id=1, source_target_pairs={{0,8},{1,9},{2,10},{3,11},{4,12},{5,13},{6,14},{7,15},{8,0},{9,1},... | collective-permute-start | bytes 393224 | tf_op jit(solution)/shard_map/ppermute | solution.py:154
  31.8 0.0 collective-permute-start.8
  31.8 0.0 collective-permute-done.11.refs_3_
  31.8 1.4 %collective-permute-done.9.refs_0_ = bf16[2,432,128]{2,1,0:T(8,128)(2,1)S(1)} collective-permute-done((bf16[2,432,128]{2,1,0:T(8,128)(2,1)S(1)}, bf16[2,432,128]{2,1,0:T(8,128)(2,1)S(1)}, u32[]{:S(2)}, u32[]{:S(2)}) %collective-permute-start.9) | collective-permute-done | bytes 221216 | tf_op jit(solution)/shard_map/ppermute | solution.py:520
  33.2 0.8 %collective-permute-done.10.refs_1_ = bf16[2,432,128]{2,1,0:T(8,128)(2,1)S(1)} collective-permute-done((bf16[2,432,128]{2,1,0:T(8,128)(2,1)S(1)}, bf16[2,432,128]{2,1,0:T(8,128)(2,1)S(1)}, u32[]{:S(2)}, u32[]{:S(2)}) %collective-permute-start.10) | collective-permute-done | bytes 221216 | tf_op jit(solution)/shard_map/ppermute | solution.py:520
  34.0 0.2 shard_map.93
  34.3 1.9 %collective-permute-start.14 = (s16[448,128]{1,0:T(8,128)(2,1)S(1)}, s16[448,128]{1,0:T(8,128)(2,1)S(1)}, u32[]{:S(2)}, u32[]{:S(2)}) collective-permute-start(s16[448,128]{1,0:T(8,128)(2,1)S(1)} %get-tuple-element.128), channel_id=1, source_target_pairs={{0,8},{8,0},{16,24},{24,16},{1,9},{9,1},{17,25},{25,17},{2,10},{10... | collective-permute-start | bytes 344072 | tf_op jit(solution)/shard_map/ppermute | solution.py:520
  36.2 0.0 collective-permute-done.7.xa
  36.2 0.0 collective-permute-done.8.xb
  36.3 0.8 %collective-permute-start.13 = (bf16[2,10,16,128]{3,2,1,0:T(8,128)(2,1)S(1)}, bf16[2,10,16,128]{3,2,1,0:T(8,128)(2,1)S(1)}, u32[]{:S(2)}, u32[]{:S(2)}) collective-permute-start(bf16[2,10,16,128]{3,2,1,0:T(8,128)(2,1)S(1)} %get-tuple-element.134), channel_id=1, source_target_pairs={{0,8},{1,2},{2,1},{3,4},{4,3},{5,6},{6,5},{7,15},{8,0},{9,10},{10,... | collective-permute-start | bytes 245768 | tf_op jit(solution)/shard_map/ppermute | solution.py:153
  37.0 1.0 %collective-permute-start.12 = (bf16[2,10,16,128]{3,2,1,0:T(8,128)(2,1)S(1)}, bf16[2,10,16,128]{3,2,1,0:T(8,128)(2,1)S(1)}, u32[]{:S(2)}, u32[]{:S(2)}) collective-permute-start(bf16[2,10,16,128]{3,2,1,0:T(8,128)(2,1)S(1)} %get-tuple-element.133), channel_id=1, source_target_pairs={{0,1},{1,0},{2,3},{3,2},{4,5},{5,4},{6,7},{7,6},{8,9},{9,8},{10,11... | collective-permute-start | bytes 245768 | tf_op jit(solution)/shard_map/ppermute | solution.py:154
  38.0 1.3 %collective-permute-done.14.came = s16[448,128]{1,0:T(8,128)(2,1)S(1)} collective-permute-done((s16[448,128]{1,0:T(8,128)(2,1)S(1)}, s16[448,128]{1,0:T(8,128)(2,1)S(1)}, u32[]{:S(2)}, u32[]{:S(2)}) %collective-permute-start.14) | collective-permute-done | bytes 114720 | tf_op jit(solution)/shard_map/ppermute | solution.py:520
  39.3 0.2 shard_map.95.own
  39.4 3.0 %collective-permute-start.15 = (s16[448,128]{1,0:T(8,128)(2,1)S(1)}, s16[448,128]{1,0:T(8,128)(2,1)S(1)}, u32[]{:S(2)}, u32[]{:S(2)}) collective-permute-start(s16[448,128]{1,0:T(8,128)(2,1)S(1)} %shard_map.95.own), channel_id=1, source_target_pairs={{0,16},{8,24},{16,0},{24,8},{1,17},{9,25},{17,1},{25,9},{2,18},{10... | collective-permute-start | bytes 344072 | tf_op jit(solution)/shard_map/ppermute | solution.py:520
  42.4 0.0 collective-permute-done.13.yb
  42.4 0.0 collective-permute-done.12.ya
  42.4 0.0 copy-done.3
  42.4 3.6 %shard_map.96 = bf16[8,16,16,128]{3,2,1,0:T(8,128)(2,1)} custom-call(f32[1,256,128]{2,1,0:T(8,128)S(1)} %get-tuple-element.117.mask, bf16[8,16,16,128]{3,2,1,0:T(8,128)(2,1)S(1)} %copy-done.3, bf16[8,16,16,128]{3,2,1,0:T(8,128)(2,1)S(1)} %get-tuple-element.98.hidden.field, bf16[2,16,16,128]{3,2,1,0:T(8,128)(2,1)S(1)} %collective-permute-done.7.xa, ...), custom_call_target="tpu_custom_call" | custom-call | flops 1811939328 | bytes 3145728 | tf_op jit(solution)/shard_map/pallas_call | solution.py:19
  46.1 0.9 %collective-permute-done.15.came = s16[448,128]{1,0:T(8,128)(2,1)S(1)} collective-permute-done((s16[448,128]{1,0:T(8,128)(2,1)S(1)}, s16[448,128]{1,0:T(8,128)(2,1)S(1)}, u32[]{:S(2)}, u32[]{:S(2)}) %collective-permute-start.15) | collective-permute-done | bytes 114720 | tf_op jit(solution)/shard_map/ppermute | solution.py:520
  46.9 0.2 shard_map.97.own
  47.1 0.2 collective-permute-start.16
  47.3 1.5 %shard_map.98 = (bf16[10,18,16,384]{3,2,1,0:T(8,128)(2,1)S(1)}, bf16[8,16,16,128]{3,2,1,0:T(8,128)(2,1)}) custom-call(f32[1,256,128]{2,1,0:T(8,128)S(1)} %get-tuple-element.117.mask, bf16[8,16,16,128]{3,2,1,0:T(8,128)(2,1)S(1)} %copy-done, bf16[12,384,256]{2,1,0:T(8,128)(2,1)S(1)} %get-tuple-element.141.taps, ...), custom_call_target="tpu_custom_call", output_to_operand_aliasing={{0}: (8, {})} | custom-call | bytes 3145728 | tf_op jit(solution)/shard_map/pallas_call | solution.py:19
  48.8 3.2 %collective-permute-done.16.came = s16[448,128]{1,0:T(8,128)(2,1)S(1)} collective-permute-done((s16[448,128]{1,0:T(8,128)(2,1)S(1)}, s16[448,128]{1,0:T(8,128)(2,1)S(1)}, u32[]{:S(2)}, u32[]{:S(2)}) %collective-permute-start.16) | collective-permute-done | bytes 114720 | tf_op jit(solution)/shard_map/ppermute | solution.py:520
  52.0 0.8 %shard_map.99 = (f32[27,16,128]{2,1,0:T(8,128)}, f32[27,16,128]{2,1,0:T(8,128)}) custom-call(s16[448,128]{1,0:T(8,128)(2,1)S(1)} %shard_map.97.own, s16[448,128]{1,0:T(8,128)(2,1)S(1)} %collective-permute-done.16.came), custom_call_target="tpu_custom_call" | custom-call | bytes 1048576 | tf_op jit(solution)/shard_map/pallas_call | solution.py:642
  (2 shorter events, 0.1 us)
Async XLA Ops:
  0.6 4.4 %copy-start.2 = (bf16[27,128,128]{2,1,0:T(8,128)(2,1)S(1)}, bf16[27,128,128]{2,1,0:T(8,128)(2,1)}, u32[]{:S(2)}) copy-start(bf16[27,128,128]{2,1,0:T(8,128)(2,1)} %w.6) | copy-start | bytes 2654212
  1.9 6.6 %collective-permute-start = (bf16[2,16,16,128]{3,2,1,0:T(8,128)(2,1)S(1)}, bf16[2,16,16,128]{3,2,1,0:T(8,128)(2,1)S(1)}, u32[]{:S(2)}, u32[]{:S(2)}) collective-permute-start(bf16[2,16,16,128]{3,2,1,0:T(8,128)(2,1)S(1)} %get-tuple-element.79), channel_id=1, source_target_pairs={{0,8},{1,9},{2,10},{3,11},{4,12},{5,13},{6,14},{7,15},{8,0},{9,1},... | collective-permute-start | bytes 393224 | tf_op jit(solution)/shard_map/ppermute | solution.py:154
  5.0 3.5 %collective-permute-start.1 = (bf16[2,16,16,128]{3,2,1,0:T(8,128)(2,1)S(1)}, bf16[2,16,16,128]{3,2,1,0:T(8,128)(2,1)S(1)}, u32[]{:S(2)}, u32[]{:S(2)}) collective-permute-start(bf16[2,16,16,128]{3,2,1,0:T(8,128)(2,1)S(1)} %get-tuple-element.80), channel_id=1, source_target_pairs={{0,1},{1,0},{2,3},{3,2},{4,5},{5,4},{6,7},{7,6},{8,16},{9,17},{10,... | collective-permute-start | bytes 393224 | tf_op jit(solution)/shard_map/ppermute | solution.py:153
  5.0 6.5 %copy-start = (bf16[8,16,16,128]{3,2,1,0:T(8,128)(2,1)S(1)}, bf16[8,16,16,128]{3,2,1,0:T(8,128)(2,1)}, u32[]{:S(2)}) copy-start(bf16[8,16,16,128]{3,2,1,0:T(8,128)(2,1)} %own.3) | copy-start | bytes 1572868
  5.0 6.5 %copy-start.1 = (bf16[27,128,128]{2,1,0:T(8,128)(2,1)S(1)}, bf16[27,128,128]{2,1,0:T(8,128)(2,1)}, u32[]{:S(2)}) copy-start(bf16[27,128,128]{2,1,0:T(8,128)(2,1)} %w.7) | copy-start | bytes 2654212
  8.5 6.5 %collective-permute-start.2 = (bf16[2,10,16,128]{3,2,1,0:T(8,128)(2,1)S(1)}, bf16[2,10,16,128]{3,2,1,0:T(8,128)(2,1)S(1)}, u32[]{:S(2)}, u32[]{:S(2)}) collective-permute-start(bf16[2,10,16,128]{3,2,1,0:T(8,128)(2,1)S(1)} %get-tuple-element.87), channel_id=1, source_target_pairs={{0,1},{1,0},{2,3},{3,2},{4,5},{5,4},{6,7},{7,6},{8,9},{9,8},{10,11... | collective-permute-start | bytes 245768 | tf_op jit(solution)/shard_map/ppermute | solution.py:154
  8.6 6.4 %collective-permute-start.3 = (bf16[2,10,16,128]{3,2,1,0:T(8,128)(2,1)S(1)}, bf16[2,10,16,128]{3,2,1,0:T(8,128)(2,1)S(1)}, u32[]{:S(2)}, u32[]{:S(2)}) collective-permute-start(bf16[2,10,16,128]{3,2,1,0:T(8,128)(2,1)S(1)} %get-tuple-element.88), channel_id=1, source_target_pairs={{0,8},{1,2},{2,1},{3,4},{4,3},{5,6},{6,5},{7,15},{8,0},{9,10},{10,... | collective-permute-start | bytes 245768 | tf_op jit(solution)/shard_map/ppermute | solution.py:153
  17.6 3.2 %collective-permute-start.4 = (f32[4,27,16,128]{3,2,1,0:T(8,128)S(1)}, f32[4,27,16,128]{3,2,1,0:T(8,128)S(1)}, u32[]{:S(2)}, u32[]{:S(2)}) collective-permute-start(f32[4,27,16,128]{3,2,1,0:T(8,128)S(1)} %get-tuple-element.106), channel_id=1, source_target_pairs={{0,1},{1,0},{2,3},{3,2},{4,5},{5,4},{6,7},{7,6},{8,9},{9,8},{10,11... | collective-permute-start | bytes 2654216 | tf_op jit(solution)/shard_map/ppermute | solution.py:520
  20.3 2.8 %collective-permute-start.6 = (f32[4,27,16,128]{3,2,1,0:T(8,128)S(1)}, f32[4,27,16,128]{3,2,1,0:T(8,128)S(1)}, u32[]{:S(2)}, u32[]{:S(2)}) collective-permute-start(f32[4,27,16,128]{3,2,1,0:T(8,128)S(1)} %get-tuple-element.111), channel_id=1, source_target_pairs={{0,1},{1,0},{2,3},{3,2},{4,5},{5,4},{6,7},{7,6},{8,9},{9,8},{10,11... | collective-permute-start | bytes 2654216 | tf_op jit(solution)/shard_map/ppermute | solution.py:520
  20.9 6.0 %collective-permute-start.5 = (bf16[432,128]{1,0:T(8,128)(2,1)S(1)}, bf16[432,128]{1,0:T(8,128)(2,1)S(1)}, u32[]{:S(2)}, u32[]{:S(2)}) collective-permute-start(bf16[432,128]{1,0:T(8,128)(2,1)S(1)} %get-tuple-element.109), channel_id=1, source_target_pairs={{0,6},{1,7},{2,4},{3,5},{4,2},{5,3},{6,0},{7,1},{8,14},{9,15},{10,... | collective-permute-start | bytes 331784 | tf_op jit(solution)/shard_map/ppermute | solution.py:520
  23.2 8.6 %collective-permute-start.11 = (bf16[432,128]{1,0:T(8,128)(2,1)S(1)}, bf16[432,128]{1,0:T(8,128)(2,1)S(1)}, u32[]{:S(2)}, u32[]{:S(2)}) collective-permute-start(bf16[432,128]{1,0:T(8,128)(2,1)S(1)} %get-tuple-element.123), channel_id=1, source_target_pairs={{0,6},{1,7},{2,4},{3,5},{4,2},{5,3},{6,0},{7,1},{8,14},{9,15},{10,... | collective-permute-start | bytes 331784 | tf_op jit(solution)/shard_map/ppermute | solution.py:520
  25.5 7.7 %collective-permute-start.9 = (bf16[2,432,128]{2,1,0:T(8,128)(2,1)S(1)}, bf16[2,432,128]{2,1,0:T(8,128)(2,1)S(1)}, u32[]{:S(2)}, u32[]{:S(2)}) collective-permute-start(bf16[2,432,128]{2,1,0:T(8,128)(2,1)S(1)} %get-tuple-element.121), channel_id=1, source_target_pairs={{0,2},{1,3},{2,0},{3,1},{4,6},{5,7},{6,4},{7,5},{8,10},{9,11},{10,... | collective-permute-start | bytes 663560 | tf_op jit(solution)/shard_map/ppermute | solution.py:520
  25.5 8.6 %collective-permute-start.10 = (bf16[2,432,128]{2,1,0:T(8,128)(2,1)S(1)}, bf16[2,432,128]{2,1,0:T(8,128)(2,1)S(1)}, u32[]{:S(2)}, u32[]{:S(2)}) collective-permute-start(bf16[2,432,128]{2,1,0:T(8,128)(2,1)S(1)} %get-tuple-element.122), channel_id=1, source_target_pairs={{0,4},{1,5},{2,6},{3,7},{4,0},{5,1},{6,2},{7,3},{8,12},{9,13},{10,... | collective-permute-start | bytes 663560 | tf_op jit(solution)/shard_map/ppermute | solution.py:520
  26.9 15.6 %copy-start.3 = (bf16[8,16,16,128]{3,2,1,0:T(8,128)(2,1)S(1)}, bf16[8,16,16,128]{3,2,1,0:T(8,128)(2,1)}, u32[]{:S(2)}) copy-start(bf16[8,16,16,128]{3,2,1,0:T(8,128)(2,1)} %own.2) | copy-start | bytes 1572868
  29.9 6.3 %collective-permute-start.7 = (bf16[2,16,16,128]{3,2,1,0:T(8,128)(2,1)S(1)}, bf16[2,16,16,128]{3,2,1,0:T(8,128)(2,1)S(1)}, u32[]{:S(2)}, u32[]{:S(2)}) collective-permute-start(bf16[2,16,16,128]{3,2,1,0:T(8,128)(2,1)S(1)} %get-tuple-element.119), channel_id=1, source_target_pairs={{0,8},{1,9},{2,10},{3,11},{4,12},{5,13},{6,14},{7,15},{8,0},{9,1},... | collective-permute-start | bytes 393224 | tf_op jit(solution)/shard_map/ppermute | solution.py:154
  31.8 4.4 %collective-permute-start.8 = (bf16[2,16,16,128]{3,2,1,0:T(8,128)(2,1)S(1)}, bf16[2,16,16,128]{3,2,1,0:T(8,128)(2,1)S(1)}, u32[]{:S(2)}, u32[]{:S(2)}) collective-permute-start(bf16[2,16,16,128]{3,2,1,0:T(8,128)(2,1)S(1)} %get-tuple-element.120), channel_id=1, source_target_pairs={{0,1},{1,0},{2,3},{3,2},{4,5},{5,4},{6,7},{7,6},{8,16},{9,17},{10,... | collective-permute-start | bytes 393224 | tf_op jit(solution)/shard_map/ppermute | solution.py:153
  34.3 5.0 %collective-permute-start.14 = (s16[448,128]{1,0:T(8,128)(2,1)S(1)}, s16[448,128]{1,0:T(8,128)(2,1)S(1)}, u32[]{:S(2)}, u32[]{:S(2)}) collective-permute-start(s16[448,128]{1,0:T(8,128)(2,1)S(1)} %get-tuple-element.128), channel_id=1, source_target_pairs={{0,8},{8,0},{16,24},{24,16},{1,9},{9,1},{17,25},{25,17},{2,10},{10... | collective-permute-start | bytes 344072 | tf_op jit(solution)/shard_map/ppermute | solution.py:520
  36.3 6.2 %collective-permute-start.13 = (bf16[2,10,16,128]{3,2,1,0:T(8,128)(2,1)S(1)}, bf16[2,10,16,128]{3,2,1,0:T(8,128)(2,1)S(1)}, u32[]{:S(2)}, u32[]{:S(2)}) collective-permute-start(bf16[2,10,16,128]{3,2,1,0:T(8,128)(2,1)S(1)} %get-tuple-element.134), channel_id=1, source_target_pairs={{0,8},{1,2},{2,1},{3,4},{4,3},{5,6},{6,5},{7,15},{8,0},{9,10},{10,... | collective-permute-start | bytes 245768 | tf_op jit(solution)/shard_map/ppermute | solution.py:153
  37.0 5.4 %collective-permute-start.12 = (bf16[2,10,16,128]{3,2,1,0:T(8,128)(2,1)S(1)}, bf16[2,10,16,128]{3,2,1,0:T(8,128)(2,1)S(1)}, u32[]{:S(2)}, u32[]{:S(2)}) collective-permute-start(bf16[2,10,16,128]{3,2,1,0:T(8,128)(2,1)S(1)} %get-tuple-element.133), channel_id=1, source_target_pairs={{0,1},{1,0},{2,3},{3,2},{4,5},{5,4},{6,7},{7,6},{8,9},{9,8},{10,11... | collective-permute-start | bytes 245768 | tf_op jit(solution)/shard_map/ppermute | solution.py:154
  39.4 7.5 %collective-permute-start.15 = (s16[448,128]{1,0:T(8,128)(2,1)S(1)}, s16[448,128]{1,0:T(8,128)(2,1)S(1)}, u32[]{:S(2)}, u32[]{:S(2)}) collective-permute-start(s16[448,128]{1,0:T(8,128)(2,1)S(1)} %shard_map.95.own), channel_id=1, source_target_pairs={{0,16},{8,24},{16,0},{24,8},{1,17},{9,25},{17,1},{25,9},{2,18},{10... | collective-permute-start | bytes 344072 | tf_op jit(solution)/shard_map/ppermute | solution.py:520
  47.1 4.9 %collective-permute-start.16 = (s16[448,128]{1,0:T(8,128)(2,1)S(1)}, s16[448,128]{1,0:T(8,128)(2,1)S(1)}, u32[]{:S(2)}, u32[]{:S(2)}) collective-permute-start(s16[448,128]{1,0:T(8,128)(2,1)S(1)} %shard_map.97.own), channel_id=1, source_target_pairs={{0,8},{8,0},{16,24},{24,16},{1,9},{9,1},{17,25},{25,17},{2,10},{10... | collective-permute-start | bytes 344072 | tf_op jit(solution)/shard_map/ppermute | solution.py:520

commit v6 on v5

--- a/solution.py
+++ b/solution.py
@@ -673,9 +673,10 @@
     (stays, *near), leaves = first_sum(1, keep_first, after(came, sums[0]), sums)
     near = [swap(value, "gy", 2 * p) for value, p in zip(near, (p for p in places if not is_far(p)))]
     far_first = [swap(value, "gy", 2 * p) for value, p in zip(leaves, filter(is_far, places))]
+    xa, xb = swap_neighbours("gx", *after((xa, xb), far_second, stays))
     behind = after(mask, far_second, stays)
     zp, *own_pre = own_terms(behind, pre_grad, w_first, turned)
-    xa, xb = swap_neighbours("gx", *after((xa, xb), own_pre[1]))
+    xa, xb = after((xa, xb), own_pre[1])
     stays, leaves = second_sums(stays, *after((near, (far_second, far_first)), own_pre[1]))
     xa, xb = after((xa, xb), leaves)
     came = swap(leaves, "gx", 1)

time: 53.1 us -> 52.8 us (level)
    ppermute x4, starting transfers between devices: 3.72 us -> 3.12 us  [swap_neighbours(): second = lax.ppermute(second, ('gx', 'gy'), swap_pairs(axis, True))]
    ppermute x9, starting transfers between devices: 11.4 us -> 12 us  [swap(): lax.ppermute(value, axis, [(i, i ^ bit) for i in range(lax.axis_size(axis...]
  transfers between devices with their start and end apart: 17 -> 17, of which waited for: 7 -> 6; matrix products, arithmetic and copies ran while one was open for 0% -> 0% of each run, Pallas kernels for 33% -> 33%
where the time goes in v6:
time: 52.8 us; the launch traced here: 52.7 us
  Pallas kernels  22.4 us (42%)
  starting transfers between devices  21 us (40%)
  waiting for transfers between devices  8.33 us (16%)
  between operations  0.95 us (2%)
    pallas_call x15, Pallas kernels, call(): pl.pallas_call(kernel, out_shape=out_shapes, in_specs=list(spaces) + [VME...  21.6 us
    ppermute x9, starting transfers between devices, swap(): lax.ppermute(value, axis, [(i, i ^ bit) for i in range(lax.axis_size(axis...  12 us
    ppermute x9, waiting for transfers between devices, swap(): lax.ppermute(value, axis, [(i, i ^ bit) for i in range(lax.axis_size(axis...  7.68 us
    ppermute x4, starting transfers between devices, swap_neighbours(): first = lax.ppermute(first, ('gx', 'gy'), swap_pairs(axis, False))  5.85 us
    ppermute x4, starting transfers between devices, swap_neighbours(): second = lax.ppermute(second, ('gx', 'gy'), swap_pairs(axis, True))  3.12 us
  transfers between devices with their start and end apart: 17, of which 6 were waited for; matrix products, arithmetic and copies ran while one was open for 0% of the time, Pallas kernels for 33%

profile of v6, /device:TPU:0, one launch (start us, length us, event | category | flops | bytes accessed | tf_op | source)
XLA Modules:
  0.0 52.7 jit_solution(11070193748181432473)
XLA Ops:
  0.6 0.0 copy-start.2
  0.6 1.3 %shard_map.84 = (f32[1,256,128]{2,1,0:T(8,128)S(1)}, bf16[2,16,16,128]{3,2,1,0:T(8,128)(2,1)S(1)}, bf16[2,16,16,128]{3,2,1,0:T(8,128)(2,1)S(1)}, bf16[2,8,16,128...) custom-call(s32[1,2,2]{2,1,0:T(2,128)} %occ_hbm.1, ...), custom_call_target="tpu_custom_call" | custom-call | flops 8589934592 | bytes 1048576 | tf_op jit(solution)/shard_map/pallas_call | solution.py:19
  1.9 3.1 %collective-permute-start = (bf16[2,16,16,128]{3,2,1,0:T(8,128)(2,1)S(1)}, bf16[2,16,16,128]{3,2,1,0:T(8,128)(2,1)S(1)}, u32[]{:S(2)}, u32[]{:S(2)}) collective-permute-start(bf16[2,16,16,128]{3,2,1,0:T(8,128)(2,1)S(1)} %get-tuple-element.81), channel_id=1, source_target_pairs={{0,8},{1,9},{2,10},{3,11},{4,12},{5,13},{6,14},{7,15},{8,0},{9,1},... | collective-permute-start | bytes 393224 | tf_op jit(solution)/shard_map/ppermute | solution.py:154
  5.0 0.0 collective-permute-start.1
  5.0 0.0 copy-done.2
  5.0 0.0 copy-start
  5.0 0.0 copy-start.1
  5.0 2.8 %shard_map.85 = (bf16[10,18,16,384]{3,2,1,0:T(8,128)(2,1)S(1)}, bf16[12,384,256]{2,1,0:T(8,128)(2,1)S(1)}, f32[8,256,128]{2,1,0:T(8,128)S(1)}) custom-call(f32[1,256,128]{2,1,0:T(8,128)S(1)} %get-tuple-element.121.mask, bf16[8,16,16,128]{3,2,1,0:T(8,128)(2,1)S(1)} %get-tuple-element.83.field, bf16[27,128,128]{2,1,0:T(8,128)(2,1)S(1)} %copy-done.2), custom_call_target="tpu_custom_call" | custom-call | flops 1811939328 | bytes 4194304 | tf_op jit(solution)/shard_map/pallas_call | solution.py:19
  7.9 0.6 %collective-permute-done.xa = bf16[2,16,16,128]{3,2,1,0:T(8,128)(2,1)S(1)} collective-permute-done((bf16[2,16,16,128]{3,2,1,0:T(8,128)(2,1)S(1)}, bf16[2,16,16,128]{3,2,1,0:T(8,128)(2,1)S(1)}, u32[]{:S(2)}, u32[]{:S(2)}) %collective-permute-start) | collective-permute-done | bytes 131104 | tf_op jit(solution)/shard_map/ppermute | solution.py:154
  8.5 0.0 collective-permute-done.1.xb
  8.5 0.1 collective-permute-start.2
  8.6 2.9 %collective-permute-start.3 = (bf16[2,10,16,128]{3,2,1,0:T(8,128)(2,1)S(1)}, bf16[2,10,16,128]{3,2,1,0:T(8,128)(2,1)S(1)}, u32[]{:S(2)}, u32[]{:S(2)}) collective-permute-start(bf16[2,10,16,128]{3,2,1,0:T(8,128)(2,1)S(1)} %get-tuple-element.90), channel_id=1, source_target_pairs={{0,8},{1,2},{2,1},{3,4},{4,3},{5,6},{6,5},{7,15},{8,0},{9,10},{10,... | collective-permute-start | bytes 245768 | tf_op jit(solution)/shard_map/ppermute | solution.py:153
  11.5 0.0 copy-done
  11.5 0.0 copy-done.1
  11.5 3.4 %shard_map.87 = (bf16[10,18,16,384]{3,2,1,0:T(8,128)(2,1)S(1)}, bf16[12,384,256]{2,1,0:T(8,128)(2,1)S(1)}, f32[8,256,128]{2,1,0:T(8,128)S(1)}, bf16[10,18,16,384]{3,2,1,0:T(8,128)(2,1)S(1)}, f32[8,256,128]{2,1,0:T(8,128)S(1)}) custom-call(f32[1,256,128]{2,1,0:T(8,128)S(1)} %get-tuple-element.121.mask, ...), custom_call_target="tpu_custom_call", output_to_operand_aliasing={{3}: (6, {}), {4}: (7, {})} | custom-call | flops 1811939328 | bytes 4194304 | tf_op jit(solution)/shard_map/pallas_call | solution.py:19
  15.0 0.0 collective-permute-done.3.yb
  15.0 0.0 collective-permute-done.2.ya
  15.0 2.6 %shard_map.88 = (bf16[10,18,16,384]{3,2,1,0:T(8,128)(2,1)S(1)}, bf16[10,18,16,384]{3,2,1,0:T(8,128)(2,1)S(1)}, bf16[8,16,16,128]{3,2,1,0:T(8,128)(2,1)S(1)}, f32...) custom-call(f32[1,256,128]{2,1,0:T(8,128)S(1)} %get-tuple-element.12, ...), custom_call_target="tpu_custom_call", output_to_operand_aliasing={{0}: (5, {}), {1}: (6, {})} | custom-call | flops 1811939328 | bytes 8388608 | tf_op jit(solution)/shard_map/pallas_call | solution.py:19
  17.6 0.1 collective-permute-start.4
  17.7 2.6 %shard_map.89 = (bf16[8,16,16,128]{3,2,1,0:T(8,128)(2,1)S(1)}, f32[4,27,16,128]{3,2,1,0:T(8,128)S(1)}, f32[4,27,16,128]{3,2,1,0:T(8,128)S(1)}, bf16[2,16,16,128]...) custom-call(bf16[8,16,16,128]{3,2,1,0:T(8,128)(2,1)S(1)} %get-tuple-, ...), custom_call_target="tpu_custom_call" | custom-call | flops 1811939328 | bytes 8388608 | tf_op jit(solution)/shard_map/pallas_call | solution.py:19
  20.3 0.6 %collective-permute-start.6 = (f32[4,27,16,128]{3,2,1,0:T(8,128)S(1)}, f32[4,27,16,128]{3,2,1,0:T(8,128)S(1)}, u32[]{:S(2)}, u32[]{:S(2)}) collective-permute-start(f32[4,27,16,128]{3,2,1,0:T(8,128)S(1)} %get-tuple-element.113), channel_id=1, source_target_pairs={{0,1},{1,0},{2,3},{3,2},{4,5},{5,4},{6,7},{7,6},{8,9},{9,8},{10,11... | collective-permute-start | bytes 2654216 | tf_op jit(solution)/shard_map/ppermute | solution.py:520
  20.8 0.0 collective-permute-done.4.came
  20.8 0.1 shard_map.90
  20.9 2.2 %collective-permute-start.5 = (bf16[432,128]{1,0:T(8,128)(2,1)S(1)}, bf16[432,128]{1,0:T(8,128)(2,1)S(1)}, u32[]{:S(2)}, u32[]{:S(2)}) collective-permute-start(bf16[432,128]{1,0:T(8,128)(2,1)S(1)} %get-tuple-element.111), channel_id=1, source_target_pairs={{0,6},{1,7},{2,4},{3,5},{4,2},{5,3},{6,0},{7,1},{8,14},{9,15},{10,... | collective-permute-start | bytes 331784 | tf_op jit(solution)/shard_map/ppermute | solution.py:520
  23.1 0.0 collective-permute-done.6.came
  23.1 0.1 shard_map.91
  23.2 0.6 %collective-permute-start.9 = (bf16[2,432,128]{2,1,0:T(8,128)(2,1)S(1)}, bf16[2,432,128]{2,1,0:T(8,128)(2,1)S(1)}, u32[]{:S(2)}, u32[]{:S(2)}) collective-permute-start(bf16[2,432,128]{2,1,0:T(8,128)(2,1)S(1)} %get-tuple-element.125), channel_id=1, source_target_pairs={{0,2},{1,3},{2,0},{3,1},{4,6},{5,7},{6,4},{7,5},{8,10},{9,11},{10,... | collective-permute-start | bytes 663560 | tf_op jit(solution)/shard_map/ppermute | solution.py:520
  23.7 2.3 %collective-permute-start.10 = (bf16[2,432,128]{2,1,0:T(8,128)(2,1)S(1)}, bf16[2,432,128]{2,1,0:T(8,128)(2,1)S(1)}, u32[]{:S(2)}, u32[]{:S(2)}) collective-permute-start(bf16[2,432,128]{2,1,0:T(8,128)(2,1)S(1)} %get-tuple-element.126), channel_id=1, source_target_pairs={{0,4},{1,5},{2,6},{3,7},{4,0},{5,1},{6,2},{7,3},{8,12},{9,13},{10,... | collective-permute-start | bytes 663560 | tf_op jit(solution)/shard_map/ppermute | solution.py:520
  26.0 0.7 %collective-permute-start.11 = (bf16[432,128]{1,0:T(8,128)(2,1)S(1)}, bf16[432,128]{1,0:T(8,128)(2,1)S(1)}, u32[]{:S(2)}, u32[]{:S(2)}) collective-permute-start(bf16[432,128]{1,0:T(8,128)(2,1)S(1)} %get-tuple-element.127), channel_id=1, source_target_pairs={{0,6},{1,7},{2,4},{3,5},{4,2},{5,3},{6,0},{7,1},{8,14},{9,15},{10,... | collective-permute-start | bytes 331784 | tf_op jit(solution)/shard_map/ppermute | solution.py:520
  26.7 0.5 collective-permute-done.5.refs_2_
  27.2 0.0 copy-start.3
  27.2 1.2 %collective-permute-start.7 = (bf16[2,16,16,128]{3,2,1,0:T(8,128)(2,1)S(1)}, bf16[2,16,16,128]{3,2,1,0:T(8,128)(2,1)S(1)}, u32[]{:S(2)}, u32[]{:S(2)}) collective-permute-start(bf16[2,16,16,128]{3,2,1,0:T(8,128)(2,1)S(1)} %get-tuple-element.119), channel_id=1, source_target_pairs={{0,8},{1,9},{2,10},{3,11},{4,12},{5,13},{6,14},{7,15},{8,0},{9,1},... | collective-permute-start | bytes 393224 | tf_op jit(solution)/shard_map/ppermute | solution.py:154
  28.4 0.0 collective-permute-start.8
  28.4 3.0 %shard_map.92 = (bf16[10,18,16,384]{3,2,1,0:T(8,128)(2,1)S(1)}, bf16[12,384,256]{2,1,0:T(8,128)(2,1)S(1)}, f32[8,256,128]{2,1,0:T(8,128)S(1)}) custom-call(f32[1,256,128]{2,1,0:T(8,128)S(1)} %get-tuple-element.121.mask, bf16[8,16,16,128]{3,2,1,0:T(8,128)(2,1)S(1)} %get-tuple-element.109.field, bf16[27,128,128]{2,1,0:T(8,128)(2,1)S(1)} %copy-done.2), custom_call_target="tpu_custom_call" | custom-call | flops 1811939328 | bytes 4194304 | tf_op jit(solution)/shard_map/pallas_call | solution.py:19
  31.5 2.6 %collective-permute-done.11.refs_3_ = bf16[432,128]{1,0:T(8,128)(2,1)S(1)} collective-permute-done((bf16[432,128]{1,0:T(8,128)(2,1)S(1)}, bf16[432,128]{1,0:T(8,128)(2,1)S(1)}, u32[]{:S(2)}, u32[]{:S(2)}) %collective-permute-start.11) | collective-permute-done | bytes 110624 | tf_op jit(solution)/shard_map/ppermute | solution.py:520
  34.1 0.0 collective-permute-done.9.refs_0_
  34.1 0.0 collective-permute-done.10.refs_1_
  34.1 0.2 shard_map.93
  34.4 2.0 %collective-permute-start.14 = (s16[448,128]{1,0:T(8,128)(2,1)S(1)}, s16[448,128]{1,0:T(8,128)(2,1)S(1)}, u32[]{:S(2)}, u32[]{:S(2)}) collective-permute-start(s16[448,128]{1,0:T(8,128)(2,1)S(1)} %get-tuple-element.132), channel_id=1, source_target_pairs={{0,8},{8,0},{16,24},{24,16},{1,9},{9,1},{17,25},{25,17},{2,10},{10... | collective-permute-start | bytes 344072 | tf_op jit(solution)/shard_map/ppermute | solution.py:520
  36.3 0.0 collective-permute-done.7.xa
  36.3 0.0 collective-permute-done.8.xb
  36.4 0.2 collective-permute-start.13
  36.6 1.5 %collective-permute-start.12 = (bf16[2,10,16,128]{3,2,1,0:T(8,128)(2,1)S(1)}, bf16[2,10,16,128]{3,2,1,0:T(8,128)(2,1)S(1)}, u32[]{:S(2)}, u32[]{:S(2)}) collective-permute-start(bf16[2,10,16,128]{3,2,1,0:T(8,128)(2,1)S(1)} %get-tuple-element.137), channel_id=1, source_target_pairs={{0,1},{1,0},{2,3},{3,2},{4,5},{5,4},{6,7},{7,6},{8,9},{9,8},{10,11... | collective-permute-start | bytes 245768 | tf_op jit(solution)/shard_map/ppermute | solution.py:154
  38.0 1.2 %collective-permute-done.14.came = s16[448,128]{1,0:T(8,128)(2,1)S(1)} collective-permute-done((s16[448,128]{1,0:T(8,128)(2,1)S(1)}, s16[448,128]{1,0:T(8,128)(2,1)S(1)}, u32[]{:S(2)}, u32[]{:S(2)}) %collective-permute-start.14) | collective-permute-done | bytes 114720 | tf_op jit(solution)/shard_map/ppermute | solution.py:520
  39.2 0.2 shard_map.95.own
  39.4 3.2 %collective-permute-start.15 = (s16[448,128]{1,0:T(8,128)(2,1)S(1)}, s16[448,128]{1,0:T(8,128)(2,1)S(1)}, u32[]{:S(2)}, u32[]{:S(2)}) collective-permute-start(s16[448,128]{1,0:T(8,128)(2,1)S(1)} %shard_map.95.own), channel_id=1, source_target_pairs={{0,16},{8,24},{16,0},{24,8},{1,17},{9,25},{17,1},{25,9},{2,18},{10... | collective-permute-start | bytes 344072 | tf_op jit(solution)/shard_map/ppermute | solution.py:520
  42.5 0.0 collective-permute-done.13.yb
  42.5 0.0 collective-permute-done.12.ya
  42.5 0.0 copy-done.3
  42.5 3.6 %shard_map.96 = bf16[8,16,16,128]{3,2,1,0:T(8,128)(2,1)} custom-call(f32[1,256,128]{2,1,0:T(8,128)S(1)} %get-tuple-element.121.mask, bf16[8,16,16,128]{3,2,1,0:T(8,128)(2,1)S(1)} %copy-done.3, bf16[8,16,16,128]{3,2,1,0:T(8,128)(2,1)S(1)} %get-tuple-element.100.hidden.field, bf16[2,16,16,128]{3,2,1,0:T(8,128)(2,1)S(1)} %collective-permute-done.7.xa, ...), custom_call_target="tpu_custom_call" | custom-call | flops 1811939328 | bytes 3145728 | tf_op jit(solution)/shard_map/pallas_call | solution.py:19
  46.2 0.5 collective-permute-done.15.came
  46.7 0.2 shard_map.97.own
  46.9 0.5 collective-permute-start.16
  47.4 1.5 %shard_map.98 = (bf16[10,18,16,384]{3,2,1,0:T(8,128)(2,1)S(1)}, bf16[8,16,16,128]{3,2,1,0:T(8,128)(2,1)}) custom-call(f32[1,256,128]{2,1,0:T(8,128)S(1)} %get-tuple-element.121.mask, bf16[8,16,16,128]{3,2,1,0:T(8,128)(2,1)S(1)} %copy-done, bf16[12,384,256]{2,1,0:T(8,128)(2,1)S(1)} %get-tuple-element.145.taps, ...), custom_call_target="tpu_custom_call", output_to_operand_aliasing={{0}: (8, {})} | custom-call | bytes 3145728 | tf_op jit(solution)/shard_map/pallas_call | solution.py:19
  48.9 2.8 %collective-permute-done.16.came = s16[448,128]{1,0:T(8,128)(2,1)S(1)} collective-permute-done((s16[448,128]{1,0:T(8,128)(2,1)S(1)}, s16[448,128]{1,0:T(8,128)(2,1)S(1)}, u32[]{:S(2)}, u32[]{:S(2)}) %collective-permute-start.16) | collective-permute-done | bytes 114720 | tf_op jit(solution)/shard_map/ppermute | solution.py:520
  51.7 0.8 %shard_map.99 = (f32[27,16,128]{2,1,0:T(8,128)}, f32[27,16,128]{2,1,0:T(8,128)}) custom-call(s16[448,128]{1,0:T(8,128)(2,1)S(1)} %shard_map.97.own, s16[448,128]{1,0:T(8,128)(2,1)S(1)} %collective-permute-done.16.came), custom_call_target="tpu_custom_call" | custom-call | bytes 1048576 | tf_op jit(solution)/shard_map/pallas_call | solution.py:642
  (2 shorter events, 0.1 us)
Async XLA Ops:
  0.6 4.4 %copy-start.2 = (bf16[27,128,128]{2,1,0:T(8,128)(2,1)S(1)}, bf16[27,128,128]{2,1,0:T(8,128)(2,1)}, u32[]{:S(2)}) copy-start(bf16[27,128,128]{2,1,0:T(8,128)(2,1)} %w.6) | copy-start | bytes 2654212
  1.9 6.6 %collective-permute-start = (bf16[2,16,16,128]{3,2,1,0:T(8,128)(2,1)S(1)}, bf16[2,16,16,128]{3,2,1,0:T(8,128)(2,1)S(1)}, u32[]{:S(2)}, u32[]{:S(2)}) collective-permute-start(bf16[2,16,16,128]{3,2,1,0:T(8,128)(2,1)S(1)} %get-tuple-element.81), channel_id=1, source_target_pairs={{0,8},{1,9},{2,10},{3,11},{4,12},{5,13},{6,14},{7,15},{8,0},{9,1},... | collective-permute-start | bytes 393224 | tf_op jit(solution)/shard_map/ppermute | solution.py:154
  5.0 3.5 %collective-permute-start.1 = (bf16[2,16,16,128]{3,2,1,0:T(8,128)(2,1)S(1)}, bf16[2,16,16,128]{3,2,1,0:T(8,128)(2,1)S(1)}, u32[]{:S(2)}, u32[]{:S(2)}) collective-permute-start(bf16[2,16,16,128]{3,2,1,0:T(8,128)(2,1)S(1)} %get-tuple-element.82), channel_id=1, source_target_pairs={{0,1},{1,0},{2,3},{3,2},{4,5},{5,4},{6,7},{7,6},{8,16},{9,17},{10,... | collective-permute-start | bytes 393224 | tf_op jit(solution)/shard_map/ppermute | solution.py:153
  5.0 6.5 %copy-start = (bf16[8,16,16,128]{3,2,1,0:T(8,128)(2,1)S(1)}, bf16[8,16,16,128]{3,2,1,0:T(8,128)(2,1)}, u32[]{:S(2)}) copy-start(bf16[8,16,16,128]{3,2,1,0:T(8,128)(2,1)} %own.3) | copy-start | bytes 1572868
  5.0 6.5 %copy-start.1 = (bf16[27,128,128]{2,1,0:T(8,128)(2,1)S(1)}, bf16[27,128,128]{2,1,0:T(8,128)(2,1)}, u32[]{:S(2)}) copy-start(bf16[27,128,128]{2,1,0:T(8,128)(2,1)} %w.7) | copy-start | bytes 2654212
  8.5 6.5 %collective-permute-start.2 = (bf16[2,10,16,128]{3,2,1,0:T(8,128)(2,1)S(1)}, bf16[2,10,16,128]{3,2,1,0:T(8,128)(2,1)S(1)}, u32[]{:S(2)}, u32[]{:S(2)}) collective-permute-start(bf16[2,10,16,128]{3,2,1,0:T(8,128)(2,1)S(1)} %get-tuple-element.89), channel_id=1, source_target_pairs={{0,1},{1,0},{2,3},{3,2},{4,5},{5,4},{6,7},{7,6},{8,9},{9,8},{10,11... | collective-permute-start | bytes 245768 | tf_op jit(solution)/shard_map/ppermute | solution.py:154
  8.6 6.4 %collective-permute-start.3 = (bf16[2,10,16,128]{3,2,1,0:T(8,128)(2,1)S(1)}, bf16[2,10,16,128]{3,2,1,0:T(8,128)(2,1)S(1)}, u32[]{:S(2)}, u32[]{:S(2)}) collective-permute-start(bf16[2,10,16,128]{3,2,1,0:T(8,128)(2,1)S(1)} %get-tuple-element.90), channel_id=1, source_target_pairs={{0,8},{1,2},{2,1},{3,4},{4,3},{5,6},{6,5},{7,15},{8,0},{9,10},{10,... | collective-permute-start | bytes 245768 | tf_op jit(solution)/shard_map/ppermute | solution.py:153
  17.6 3.2 %collective-permute-start.4 = (f32[4,27,16,128]{3,2,1,0:T(8,128)S(1)}, f32[4,27,16,128]{3,2,1,0:T(8,128)S(1)}, u32[]{:S(2)}, u32[]{:S(2)}) collective-permute-start(f32[4,27,16,128]{3,2,1,0:T(8,128)S(1)} %get-tuple-element.108), channel_id=1, source_target_pairs={{0,1},{1,0},{2,3},{3,2},{4,5},{5,4},{6,7},{7,6},{8,9},{9,8},{10,11... | collective-permute-start | bytes 2654216 | tf_op jit(solution)/shard_map/ppermute | solution.py:520
  20.3 2.8 %collective-permute-start.6 = (f32[4,27,16,128]{3,2,1,0:T(8,128)S(1)}, f32[4,27,16,128]{3,2,1,0:T(8,128)S(1)}, u32[]{:S(2)}, u32[]{:S(2)}) collective-permute-start(f32[4,27,16,128]{3,2,1,0:T(8,128)S(1)} %get-tuple-element.113), channel_id=1, source_target_pairs={{0,1},{1,0},{2,3},{3,2},{4,5},{5,4},{6,7},{7,6},{8,9},{9,8},{10,11... | collective-permute-start | bytes 2654216 | tf_op jit(solution)/shard_map/ppermute | solution.py:520
  20.9 6.3 %collective-permute-start.5 = (bf16[432,128]{1,0:T(8,128)(2,1)S(1)}, bf16[432,128]{1,0:T(8,128)(2,1)S(1)}, u32[]{:S(2)}, u32[]{:S(2)}) collective-permute-start(bf16[432,128]{1,0:T(8,128)(2,1)S(1)} %get-tuple-element.111), channel_id=1, source_target_pairs={{0,6},{1,7},{2,4},{3,5},{4,2},{5,3},{6,0},{7,1},{8,14},{9,15},{10,... | collective-permute-start | bytes 331784 | tf_op jit(solution)/shard_map/ppermute | solution.py:520
  23.2 10.9 %collective-permute-start.9 = (bf16[2,432,128]{2,1,0:T(8,128)(2,1)S(1)}, bf16[2,432,128]{2,1,0:T(8,128)(2,1)S(1)}, u32[]{:S(2)}, u32[]{:S(2)}) collective-permute-start(bf16[2,432,128]{2,1,0:T(8,128)(2,1)S(1)} %get-tuple-element.125), channel_id=1, source_target_pairs={{0,2},{1,3},{2,0},{3,1},{4,6},{5,7},{6,4},{7,5},{8,10},{9,11},{10,... | collective-permute-start | bytes 663560 | tf_op jit(solution)/shard_map/ppermute | solution.py:520
  23.7 10.4 %collective-permute-start.10 = (bf16[2,432,128]{2,1,0:T(8,128)(2,1)S(1)}, bf16[2,432,128]{2,1,0:T(8,128)(2,1)S(1)}, u32[]{:S(2)}, u32[]{:S(2)}) collective-permute-start(bf16[2,432,128]{2,1,0:T(8,128)(2,1)S(1)} %get-tuple-element.126), channel_id=1, source_target_pairs={{0,4},{1,5},{2,6},{3,7},{4,0},{5,1},{6,2},{7,3},{8,12},{9,13},{10,... | collective-permute-start | bytes 663560 | tf_op jit(solution)/shard_map/ppermute | solution.py:520
  26.0 8.0 %collective-permute-start.11 = (bf16[432,128]{1,0:T(8,128)(2,1)S(1)}, bf16[432,128]{1,0:T(8,128)(2,1)S(1)}, u32[]{:S(2)}, u32[]{:S(2)}) collective-permute-start(bf16[432,128]{1,0:T(8,128)(2,1)S(1)} %get-tuple-element.127), channel_id=1, source_target_pairs={{0,6},{1,7},{2,4},{3,5},{4,2},{5,3},{6,0},{7,1},{8,14},{9,15},{10,... | collective-permute-start | bytes 331784 | tf_op jit(solution)/shard_map/ppermute | solution.py:520
  27.2 15.3 %copy-start.3 = (bf16[8,16,16,128]{3,2,1,0:T(8,128)(2,1)S(1)}, bf16[8,16,16,128]{3,2,1,0:T(8,128)(2,1)}, u32[]{:S(2)}) copy-start(bf16[8,16,16,128]{3,2,1,0:T(8,128)(2,1)} %own.2) | copy-start | bytes 1572868
  27.2 9.1 %collective-permute-start.7 = (bf16[2,16,16,128]{3,2,1,0:T(8,128)(2,1)S(1)}, bf16[2,16,16,128]{3,2,1,0:T(8,128)(2,1)S(1)}, u32[]{:S(2)}, u32[]{:S(2)}) collective-permute-start(bf16[2,16,16,128]{3,2,1,0:T(8,128)(2,1)S(1)} %get-tuple-element.119), channel_id=1, source_target_pairs={{0,8},{1,9},{2,10},{3,11},{4,12},{5,13},{6,14},{7,15},{8,0},{9,1},... | collective-permute-start | bytes 393224 | tf_op jit(solution)/shard_map/ppermute | solution.py:154
  28.4 7.9 %collective-permute-start.8 = (bf16[2,16,16,128]{3,2,1,0:T(8,128)(2,1)S(1)}, bf16[2,16,16,128]{3,2,1,0:T(8,128)(2,1)S(1)}, u32[]{:S(2)}, u32[]{:S(2)}) collective-permute-start(bf16[2,16,16,128]{3,2,1,0:T(8,128)(2,1)S(1)} %get-tuple-element.120), channel_id=1, source_target_pairs={{0,1},{1,0},{2,3},{3,2},{4,5},{5,4},{6,7},{7,6},{8,16},{9,17},{10,... | collective-permute-start | bytes 393224 | tf_op jit(solution)/shard_map/ppermute | solution.py:153
  34.4 4.9 %collective-permute-start.14 = (s16[448,128]{1,0:T(8,128)(2,1)S(1)}, s16[448,128]{1,0:T(8,128)(2,1)S(1)}, u32[]{:S(2)}, u32[]{:S(2)}) collective-permute-start(s16[448,128]{1,0:T(8,128)(2,1)S(1)} %get-tuple-element.132), channel_id=1, source_target_pairs={{0,8},{8,0},{16,24},{24,16},{1,9},{9,1},{17,25},{25,17},{2,10},{10... | collective-permute-start | bytes 344072 | tf_op jit(solution)/shard_map/ppermute | solution.py:520
  36.4 6.2 %collective-permute-start.13 = (bf16[2,10,16,128]{3,2,1,0:T(8,128)(2,1)S(1)}, bf16[2,10,16,128]{3,2,1,0:T(8,128)(2,1)S(1)}, u32[]{:S(2)}, u32[]{:S(2)}) collective-permute-start(bf16[2,10,16,128]{3,2,1,0:T(8,128)(2,1)S(1)} %get-tuple-element.138), channel_id=1, source_target_pairs={{0,8},{1,2},{2,1},{3,4},{4,3},{5,6},{6,5},{7,15},{8,0},{9,10},{10,... | collective-permute-start | bytes 245768 | tf_op jit(solution)/shard_map/ppermute | solution.py:153
  36.6 6.0 %collective-permute-start.12 = (bf16[2,10,16,128]{3,2,1,0:T(8,128)(2,1)S(1)}, bf16[2,10,16,128]{3,2,1,0:T(8,128)(2,1)S(1)}, u32[]{:S(2)}, u32[]{:S(2)}) collective-permute-start(bf16[2,10,16,128]{3,2,1,0:T(8,128)(2,1)S(1)} %get-tuple-element.137), channel_id=1, source_target_pairs={{0,1},{1,0},{2,3},{3,2},{4,5},{5,4},{6,7},{7,6},{8,9},{9,8},{10,11... | collective-permute-start | bytes 245768 | tf_op jit(solution)/shard_map/ppermute | solution.py:154
  39.4 7.3 %collective-permute-start.15 = (s16[448,128]{1,0:T(8,128)(2,1)S(1)}, s16[448,128]{1,0:T(8,128)(2,1)S(1)}, u32[]{:S(2)}, u32[]{:S(2)}) collective-permute-start(s16[448,128]{1,0:T(8,128)(2,1)S(1)} %shard_map.95.own), channel_id=1, source_target_pairs={{0,16},{8,24},{16,0},{24,8},{1,17},{9,25},{17,1},{25,9},{2,18},{10... | collective-permute-start | bytes 344072 | tf_op jit(solution)/shard_map/ppermute | solution.py:520
  46.9 4.9 %collective-permute-start.16 = (s16[448,128]{1,0:T(8,128)(2,1)S(1)}, s16[448,128]{1,0:T(8,128)(2,1)S(1)}, u32[]{:S(2)}, u32[]{:S(2)}) collective-permute-start(s16[448,128]{1,0:T(8,128)(2,1)S(1)} %shard_map.97.own), channel_id=1, source_target_pairs={{0,8},{8,0},{16,24},{24,16},{1,9},{9,1},{17,25},{25,17},{2,10},{10... | collective-permute-start | bytes 344072 | tf_op jit(solution)/shard_map/ppermute | solution.py:520

commit v7 on v6

--- a/solution.py
+++ b/solution.py
@@ -673,7 +673,7 @@
     (stays, *near), leaves = first_sum(1, keep_first, after(came, sums[0]), sums)
     near = [swap(value, "gy", 2 * p) for value, p in zip(near, (p for p in places if not is_far(p)))]
     far_first = [swap(value, "gy", 2 * p) for value, p in zip(leaves, filter(is_far, places))]
-    xa, xb = swap_neighbours("gx", *after((xa, xb), far_second, stays))
+    xa, xb = swap_neighbours("gx", *after((xa, xb), far_second))
     behind = after(mask, far_second, stays)
     zp, *own_pre = own_terms(behind, pre_grad, w_first, turned)
     xa, xb = after((xa, xb), own_pre[1])

time: 52.8 us -> 52.8 us (level)
  no operation moved by 1% of the time
where the time goes in v7:
time: 52.8 us; the launch traced here: 52.7 us
  Pallas kernels  22.4 us (42%)
  starting transfers between devices  21 us (40%)
  waiting for transfers between devices  8.33 us (16%)
  between operations  0.95 us (2%)
    pallas_call x15, Pallas kernels, call(): pl.pallas_call(kernel, out_shape=out_shapes, in_specs=list(spaces) + [VME...  21.6 us
    ppermute x9, starting transfers between devices, swap(): lax.ppermute(value, axis, [(i, i ^ bit) for i in range(lax.axis_size(axis...  12 us
    ppermute x9, waiting for transfers between devices, swap(): lax.ppermute(value, axis, [(i, i ^ bit) for i in range(lax.axis_size(axis...  7.68 us
    ppermute x4, starting transfers between devices, swap_neighbours(): first = lax.ppermute(first, ('gx', 'gy'), swap_pairs(axis, False))  5.85 us
    ppermute x4, starting transfers between devices, swap_neighbours(): second = lax.ppermute(second, ('gx', 'gy'), swap_pairs(axis, True))  3.12 us
  transfers between devices with their start and end apart: 17, of which 6 were waited for; matrix products, arithmetic and copies ran while one was open for 0% of the time, Pallas kernels for 33%

profile of v7, /device:TPU:0, one launch (start us, length us, event | category | flops | bytes accessed | tf_op | source)
XLA Modules:
  0.0 52.7 jit_solution(11070193748181432473)
XLA Ops:
  0.6 0.0 copy-start.2
  0.6 1.3 %shard_map.84 = (f32[1,256,128]{2,1,0:T(8,128)S(1)}, bf16[2,16,16,128]{3,2,1,0:T(8,128)(2,1)S(1)}, bf16[2,16,16,128]{3,2,1,0:T(8,128)(2,1)S(1)}, bf16[2,8,16,128...) custom-call(s32[1,2,2]{2,1,0:T(2,128)} %occ_hbm.1, ...), custom_call_target="tpu_custom_call" | custom-call | flops 8589934592 | bytes 1048576 | tf_op jit(solution)/shard_map/pallas_call | solution.py:19
  1.9 3.1 %collective-permute-start = (bf16[2,16,16,128]{3,2,1,0:T(8,128)(2,1)S(1)}, bf16[2,16,16,128]{3,2,1,0:T(8,128)(2,1)S(1)}, u32[]{:S(2)}, u32[]{:S(2)}) collective-permute-start(bf16[2,16,16,128]{3,2,1,0:T(8,128)(2,1)S(1)} %get-tuple-element.81), channel_id=1, source_target_pairs={{0,8},{1,9},{2,10},{3,11},{4,12},{5,13},{6,14},{7,15},{8,0},{9,1},... | collective-permute-start | bytes 393224 | tf_op jit(solution)/shard_map/ppermute | solution.py:154
  5.0 0.0 collective-permute-start.1
  5.0 0.0 copy-done.2
  5.0 0.0 copy-start
  5.0 0.0 copy-start.1
  5.0 2.8 %shard_map.85 = (bf16[10,18,16,384]{3,2,1,0:T(8,128)(2,1)S(1)}, bf16[12,384,256]{2,1,0:T(8,128)(2,1)S(1)}, f32[8,256,128]{2,1,0:T(8,128)S(1)}) custom-call(f32[1,256,128]{2,1,0:T(8,128)S(1)} %get-tuple-element.121.mask, bf16[8,16,16,128]{3,2,1,0:T(8,128)(2,1)S(1)} %get-tuple-element.83.field, bf16[27,128,128]{2,1,0:T(8,128)(2,1)S(1)} %copy-done.2), custom_call_target="tpu_custom_call" | custom-call | flops 1811939328 | bytes 4194304 | tf_op jit(solution)/shard_map/pallas_call | solution.py:19
  7.9 0.6 %collective-permute-done.xa = bf16[2,16,16,128]{3,2,1,0:T(8,128)(2,1)S(1)} collective-permute-done((bf16[2,16,16,128]{3,2,1,0:T(8,128)(2,1)S(1)}, bf16[2,16,16,128]{3,2,1,0:T(8,128)(2,1)S(1)}, u32[]{:S(2)}, u32[]{:S(2)}) %collective-permute-start) | collective-permute-done | bytes 131104 | tf_op jit(solution)/shard_map/ppermute | solution.py:154
  8.5 0.0 collective-permute-done.1.xb
  8.5 0.1 collective-permute-start.2
  8.6 2.9 %collective-permute-start.3 = (bf16[2,10,16,128]{3,2,1,0:T(8,128)(2,1)S(1)}, bf16[2,10,16,128]{3,2,1,0:T(8,128)(2,1)S(1)}, u32[]{:S(2)}, u32[]{:S(2)}) collective-permute-start(bf16[2,10,16,128]{3,2,1,0:T(8,128)(2,1)S(1)} %get-tuple-element.90), channel_id=1, source_target_pairs={{0,8},{1,2},{2,1},{3,4},{4,3},{5,6},{6,5},{7,15},{8,0},{9,10},{10,... | collective-permute-start | bytes 245768 | tf_op jit(solution)/shard_map/ppermute | solution.py:153
  11.5 0.0 copy-done
  11.5 0.0 copy-done.1
  11.5 3.4 %shard_map.87 = (bf16[10,18,16,384]{3,2,1,0:T(8,128)(2,1)S(1)}, bf16[12,384,256]{2,1,0:T(8,128)(2,1)S(1)}, f32[8,256,128]{2,1,0:T(8,128)S(1)}, bf16[10,18,16,384]{3,2,1,0:T(8,128)(2,1)S(1)}, f32[8,256,128]{2,1,0:T(8,128)S(1)}) custom-call(f32[1,256,128]{2,1,0:T(8,128)S(1)} %get-tuple-element.121.mask, ...), custom_call_target="tpu_custom_call", output_to_operand_aliasing={{3}: (6, {}), {4}: (7, {})} | custom-call | flops 1811939328 | bytes 4194304 | tf_op jit(solution)/shard_map/pallas_call | solution.py:19
  15.0 0.0 collective-permute-done.3.yb
  15.0 0.0 collective-permute-done.2.ya
  15.0 2.6 %shard_map.88 = (bf16[10,18,16,384]{3,2,1,0:T(8,128)(2,1)S(1)}, bf16[10,18,16,384]{3,2,1,0:T(8,128)(2,1)S(1)}, bf16[8,16,16,128]{3,2,1,0:T(8,128)(2,1)S(1)}, f32...) custom-call(f32[1,256,128]{2,1,0:T(8,128)S(1)} %get-tuple-element.12, ...), custom_call_target="tpu_custom_call", output_to_operand_aliasing={{0}: (5, {}), {1}: (6, {})} | custom-call | flops 1811939328 | bytes 8388608 | tf_op jit(solution)/shard_map/pallas_call | solution.py:19
  17.6 0.1 collective-permute-start.4
  17.7 2.6 %shard_map.89 = (bf16[8,16,16,128]{3,2,1,0:T(8,128)(2,1)S(1)}, f32[4,27,16,128]{3,2,1,0:T(8,128)S(1)}, f32[4,27,16,128]{3,2,1,0:T(8,128)S(1)}, bf16[2,16,16,128]...) custom-call(bf16[8,16,16,128]{3,2,1,0:T(8,128)(2,1)S(1)} %get-tuple-, ...), custom_call_target="tpu_custom_call" | custom-call | flops 1811939328 | bytes 8388608 | tf_op jit(solution)/shard_map/pallas_call | solution.py:19
  20.3 0.6 %collective-permute-start.8 = (f32[4,27,16,128]{3,2,1,0:T(8,128)S(1)}, f32[4,27,16,128]{3,2,1,0:T(8,128)S(1)}, u32[]{:S(2)}, u32[]{:S(2)}) collective-permute-start(f32[4,27,16,128]{3,2,1,0:T(8,128)S(1)} %get-tuple-element.115), channel_id=1, source_target_pairs={{0,1},{1,0},{2,3},{3,2},{4,5},{5,4},{6,7},{7,6},{8,9},{9,8},{10,11... | collective-permute-start | bytes 2654216 | tf_op jit(solution)/shard_map/ppermute | solution.py:520
  20.8 0.0 collective-permute-done.4.came
  20.8 0.1 shard_map.90
  20.9 2.2 %collective-permute-start.5 = (bf16[432,128]{1,0:T(8,128)(2,1)S(1)}, bf16[432,128]{1,0:T(8,128)(2,1)S(1)}, u32[]{:S(2)}, u32[]{:S(2)}) collective-permute-start(bf16[432,128]{1,0:T(8,128)(2,1)S(1)} %get-tuple-element.111), channel_id=1, source_target_pairs={{0,6},{1,7},{2,4},{3,5},{4,2},{5,3},{6,0},{7,1},{8,14},{9,15},{10,... | collective-permute-start | bytes 331784 | tf_op jit(solution)/shard_map/ppermute | solution.py:520
  23.1 0.0 collective-permute-done.8.came
  23.1 0.1 shard_map.91
  23.2 0.6 %collective-permute-start.9 = (bf16[2,432,128]{2,1,0:T(8,128)(2,1)S(1)}, bf16[2,432,128]{2,1,0:T(8,128)(2,1)S(1)}, u32[]{:S(2)}, u32[]{:S(2)}) collective-permute-start(bf16[2,432,128]{2,1,0:T(8,128)(2,1)S(1)} %get-tuple-element.125), channel_id=1, source_target_pairs={{0,2},{1,3},{2,0},{3,1},{4,6},{5,7},{6,4},{7,5},{8,10},{9,11},{10,... | collective-permute-start | bytes 663560 | tf_op jit(solution)/shard_map/ppermute | solution.py:520
  23.7 2.3 %collective-permute-start.10 = (bf16[2,432,128]{2,1,0:T(8,128)(2,1)S(1)}, bf16[2,432,128]{2,1,0:T(8,128)(2,1)S(1)}, u32[]{:S(2)}, u32[]{:S(2)}) collective-permute-start(bf16[2,432,128]{2,1,0:T(8,128)(2,1)S(1)} %get-tuple-element.126), channel_id=1, source_target_pairs={{0,4},{1,5},{2,6},{3,7},{4,0},{5,1},{6,2},{7,3},{8,12},{9,13},{10,... | collective-permute-start | bytes 663560 | tf_op jit(solution)/shard_map/ppermute | solution.py:520
  26.0 0.7 %collective-permute-start.11 = (bf16[432,128]{1,0:T(8,128)(2,1)S(1)}, bf16[432,128]{1,0:T(8,128)(2,1)S(1)}, u32[]{:S(2)}, u32[]{:S(2)}) collective-permute-start(bf16[432,128]{1,0:T(8,128)(2,1)S(1)} %get-tuple-element.127), channel_id=1, source_target_pairs={{0,6},{1,7},{2,4},{3,5},{4,2},{5,3},{6,0},{7,1},{8,14},{9,15},{10,... | collective-permute-start | bytes 331784 | tf_op jit(solution)/shard_map/ppermute | solution.py:520
  26.7 0.5 collective-permute-done.5.refs_2_
  27.2 0.0 copy-start.3
  27.2 1.2 %collective-permute-start.6 = (bf16[2,16,16,128]{3,2,1,0:T(8,128)(2,1)S(1)}, bf16[2,16,16,128]{3,2,1,0:T(8,128)(2,1)S(1)}, u32[]{:S(2)}, u32[]{:S(2)}) collective-permute-start(bf16[2,16,16,128]{3,2,1,0:T(8,128)(2,1)S(1)} %get-tuple-element.112), channel_id=1, source_target_pairs={{0,8},{1,9},{2,10},{3,11},{4,12},{5,13},{6,14},{7,15},{8,0},{9,1},... | collective-permute-start | bytes 393224 | tf_op jit(solution)/shard_map/ppermute | solution.py:154
  28.4 0.0 collective-permute-start.7
  28.4 3.0 %shard_map.92 = (bf16[10,18,16,384]{3,2,1,0:T(8,128)(2,1)S(1)}, bf16[12,384,256]{2,1,0:T(8,128)(2,1)S(1)}, f32[8,256,128]{2,1,0:T(8,128)S(1)}) custom-call(f32[1,256,128]{2,1,0:T(8,128)S(1)} %get-tuple-element.121.mask, bf16[8,16,16,128]{3,2,1,0:T(8,128)(2,1)S(1)} %get-tuple-element.109.field, bf16[27,128,128]{2,1,0:T(8,128)(2,1)S(1)} %copy-done.2), custom_call_target="tpu_custom_call" | custom-call | flops 1811939328 | bytes 4194304 | tf_op jit(solution)/shard_map/pallas_call | solution.py:19
  31.5 2.6 %collective-permute-done.11.refs_3_ = bf16[432,128]{1,0:T(8,128)(2,1)S(1)} collective-permute-done((bf16[432,128]{1,0:T(8,128)(2,1)S(1)}, bf16[432,128]{1,0:T(8,128)(2,1)S(1)}, u32[]{:S(2)}, u32[]{:S(2)}) %collective-permute-start.11) | collective-permute-done | bytes 110624 | tf_op jit(solution)/shard_map/ppermute | solution.py:520
  34.1 0.0 collective-permute-done.9.refs_0_
  34.1 0.0 collective-permute-done.10.refs_1_
  34.1 0.2 shard_map.93
  34.4 2.0 %collective-permute-start.14 = (s16[448,128]{1,0:T(8,128)(2,1)S(1)}, s16[448,128]{1,0:T(8,128)(2,1)S(1)}, u32[]{:S(2)}, u32[]{:S(2)}) collective-permute-start(s16[448,128]{1,0:T(8,128)(2,1)S(1)} %get-tuple-element.132), channel_id=1, source_target_pairs={{0,8},{8,0},{16,24},{24,16},{1,9},{9,1},{17,25},{25,17},{2,10},{10... | collective-permute-start | bytes 344072 | tf_op jit(solution)/shard_map/ppermute | solution.py:520
  36.3 0.0 collective-permute-done.6.xa
  36.3 0.0 collective-permute-done.7.xb
  36.4 0.2 collective-permute-start.13
  36.6 1.5 %collective-permute-start.12 = (bf16[2,10,16,128]{3,2,1,0:T(8,128)(2,1)S(1)}, bf16[2,10,16,128]{3,2,1,0:T(8,128)(2,1)S(1)}, u32[]{:S(2)}, u32[]{:S(2)}) collective-permute-start(bf16[2,10,16,128]{3,2,1,0:T(8,128)(2,1)S(1)} %get-tuple-element.137), channel_id=1, source_target_pairs={{0,1},{1,0},{2,3},{3,2},{4,5},{5,4},{6,7},{7,6},{8,9},{9,8},{10,11... | collective-permute-start | bytes 245768 | tf_op jit(solution)/shard_map/ppermute | solution.py:154
  38.0 1.2 %collective-permute-done.14.came = s16[448,128]{1,0:T(8,128)(2,1)S(1)} collective-permute-done((s16[448,128]{1,0:T(8,128)(2,1)S(1)}, s16[448,128]{1,0:T(8,128)(2,1)S(1)}, u32[]{:S(2)}, u32[]{:S(2)}) %collective-permute-start.14) | collective-permute-done | bytes 114720 | tf_op jit(solution)/shard_map/ppermute | solution.py:520
  39.2 0.2 shard_map.95.own
  39.4 3.2 %collective-permute-start.15 = (s16[448,128]{1,0:T(8,128)(2,1)S(1)}, s16[448,128]{1,0:T(8,128)(2,1)S(1)}, u32[]{:S(2)}, u32[]{:S(2)}) collective-permute-start(s16[448,128]{1,0:T(8,128)(2,1)S(1)} %shard_map.95.own), channel_id=1, source_target_pairs={{0,16},{8,24},{16,0},{24,8},{1,17},{9,25},{17,1},{25,9},{2,18},{10... | collective-permute-start | bytes 344072 | tf_op jit(solution)/shard_map/ppermute | solution.py:520
  42.5 0.0 collective-permute-done.13.yb
  42.5 0.0 collective-permute-done.12.ya
  42.5 0.0 copy-done.3
  42.5 3.6 %shard_map.96 = bf16[8,16,16,128]{3,2,1,0:T(8,128)(2,1)} custom-call(f32[1,256,128]{2,1,0:T(8,128)S(1)} %get-tuple-element.121.mask, bf16[8,16,16,128]{3,2,1,0:T(8,128)(2,1)S(1)} %copy-done.3, bf16[8,16,16,128]{3,2,1,0:T(8,128)(2,1)S(1)} %get-tuple-element.100.hidden.field, bf16[2,16,16,128]{3,2,1,0:T(8,128)(2,1)S(1)} %collective-permute-done.6.xa, ...), custom_call_target="tpu_custom_call" | custom-call | flops 1811939328 | bytes 3145728 | tf_op jit(solution)/shard_map/pallas_call | solution.py:19
  46.2 0.5 collective-permute-done.15.came
  46.7 0.2 shard_map.97.own
  46.9 0.5 collective-permute-start.16
  47.4 1.5 %shard_map.98 = (bf16[10,18,16,384]{3,2,1,0:T(8,128)(2,1)S(1)}, bf16[8,16,16,128]{3,2,1,0:T(8,128)(2,1)}) custom-call(f32[1,256,128]{2,1,0:T(8,128)S(1)} %get-tuple-element.121.mask, bf16[8,16,16,128]{3,2,1,0:T(8,128)(2,1)S(1)} %copy-done, bf16[12,384,256]{2,1,0:T(8,128)(2,1)S(1)} %get-tuple-element.145.taps, ...), custom_call_target="tpu_custom_call", output_to_operand_aliasing={{0}: (8, {})} | custom-call | bytes 3145728 | tf_op jit(solution)/shard_map/pallas_call | solution.py:19
  48.9 2.8 %collective-permute-done.16.came = s16[448,128]{1,0:T(8,128)(2,1)S(1)} collective-permute-done((s16[448,128]{1,0:T(8,128)(2,1)S(1)}, s16[448,128]{1,0:T(8,128)(2,1)S(1)}, u32[]{:S(2)}, u32[]{:S(2)}) %collective-permute-start.16) | collective-permute-done | bytes 114720 | tf_op jit(solution)/shard_map/ppermute | solution.py:520
  51.7 0.8 %shard_map.99 = (f32[27,16,128]{2,1,0:T(8,128)}, f32[27,16,128]{2,1,0:T(8,128)}) custom-call(s16[448,128]{1,0:T(8,128)(2,1)S(1)} %shard_map.97.own, s16[448,128]{1,0:T(8,128)(2,1)S(1)} %collective-permute-done.16.came), custom_call_target="tpu_custom_call" | custom-call | bytes 1048576 | tf_op jit(solution)/shard_map/pallas_call | solution.py:642
  (2 shorter events, 0.1 us)
Async XLA Ops:
  0.6 4.4 %copy-start.2 = (bf16[27,128,128]{2,1,0:T(8,128)(2,1)S(1)}, bf16[27,128,128]{2,1,0:T(8,128)(2,1)}, u32[]{:S(2)}) copy-start(bf16[27,128,128]{2,1,0:T(8,128)(2,1)} %w.6) | copy-start | bytes 2654212
  1.9 6.6 %collective-permute-start = (bf16[2,16,16,128]{3,2,1,0:T(8,128)(2,1)S(1)}, bf16[2,16,16,128]{3,2,1,0:T(8,128)(2,1)S(1)}, u32[]{:S(2)}, u32[]{:S(2)}) collective-permute-start(bf16[2,16,16,128]{3,2,1,0:T(8,128)(2,1)S(1)} %get-tuple-element.81), channel_id=1, source_target_pairs={{0,8},{1,9},{2,10},{3,11},{4,12},{5,13},{6,14},{7,15},{8,0},{9,1},... | collective-permute-start | bytes 393224 | tf_op jit(solution)/shard_map/ppermute | solution.py:154
  5.0 3.5 %collective-permute-start.1 = (bf16[2,16,16,128]{3,2,1,0:T(8,128)(2,1)S(1)}, bf16[2,16,16,128]{3,2,1,0:T(8,128)(2,1)S(1)}, u32[]{:S(2)}, u32[]{:S(2)}) collective-permute-start(bf16[2,16,16,128]{3,2,1,0:T(8,128)(2,1)S(1)} %get-tuple-element.82), channel_id=1, source_target_pairs={{0,1},{1,0},{2,3},{3,2},{4,5},{5,4},{6,7},{7,6},{8,16},{9,17},{10,... | collective-permute-start | bytes 393224 | tf_op jit(solution)/shard_map/ppermute | solution.py:153
  5.0 6.5 %copy-start = (bf16[8,16,16,128]{3,2,1,0:T(8,128)(2,1)S(1)}, bf16[8,16,16,128]{3,2,1,0:T(8,128)(2,1)}, u32[]{:S(2)}) copy-start(bf16[8,16,16,128]{3,2,1,0:T(8,128)(2,1)} %own.3) | copy-start | bytes 1572868
  5.0 6.5 %copy-start.1 = (bf16[27,128,128]{2,1,0:T(8,128)(2,1)S(1)}, bf16[27,128,128]{2,1,0:T(8,128)(2,1)}, u32[]{:S(2)}) copy-start(bf16[27,128,128]{2,1,0:T(8,128)(2,1)} %w.7) | copy-start | bytes 2654212
  8.5 6.5 %collective-permute-start.2 = (bf16[2,10,16,128]{3,2,1,0:T(8,128)(2,1)S(1)}, bf16[2,10,16,128]{3,2,1,0:T(8,128)(2,1)S(1)}, u32[]{:S(2)}, u32[]{:S(2)}) collective-permute-start(bf16[2,10,16,128]{3,2,1,0:T(8,128)(2,1)S(1)} %get-tuple-element.89), channel_id=1, source_target_pairs={{0,1},{1,0},{2,3},{3,2},{4,5},{5,4},{6,7},{7,6},{8,9},{9,8},{10,11... | collective-permute-start | bytes 245768 | tf_op jit(solution)/shard_map/ppermute | solution.py:154
  8.6 6.4 %collective-permute-start.3 = (bf16[2,10,16,128]{3,2,1,0:T(8,128)(2,1)S(1)}, bf16[2,10,16,128]{3,2,1,0:T(8,128)(2,1)S(1)}, u32[]{:S(2)}, u32[]{:S(2)}) collective-permute-start(bf16[2,10,16,128]{3,2,1,0:T(8,128)(2,1)S(1)} %get-tuple-element.90), channel_id=1, source_target_pairs={{0,8},{1,2},{2,1},{3,4},{4,3},{5,6},{6,5},{7,15},{8,0},{9,10},{10,... | collective-permute-start | bytes 245768 | tf_op jit(solution)/shard_map/ppermute | solution.py:153
  17.6 3.2 %collective-permute-start.4 = (f32[4,27,16,128]{3,2,1,0:T(8,128)S(1)}, f32[4,27,16,128]{3,2,1,0:T(8,128)S(1)}, u32[]{:S(2)}, u32[]{:S(2)}) collective-permute-start(f32[4,27,16,128]{3,2,1,0:T(8,128)S(1)} %get-tuple-element.108), channel_id=1, source_target_pairs={{0,1},{1,0},{2,3},{3,2},{4,5},{5,4},{6,7},{7,6},{8,9},{9,8},{10,11... | collective-permute-start | bytes 2654216 | tf_op jit(solution)/shard_map/ppermute | solution.py:520
  20.3 2.8 %collective-permute-start.8 = (f32[4,27,16,128]{3,2,1,0:T(8,128)S(1)}, f32[4,27,16,128]{3,2,1,0:T(8,128)S(1)}, u32[]{:S(2)}, u32[]{:S(2)}) collective-permute-start(f32[4,27,16,128]{3,2,1,0:T(8,128)S(1)} %get-tuple-element.115), channel_id=1, source_target_pairs={{0,1},{1,0},{2,3},{3,2},{4,5},{5,4},{6,7},{7,6},{8,9},{9,8},{10,11... | collective-permute-start | bytes 2654216 | tf_op jit(solution)/shard_map/ppermute | solution.py:520
  20.9 6.3 %collective-permute-start.5 = (bf16[432,128]{1,0:T(8,128)(2,1)S(1)}, bf16[432,128]{1,0:T(8,128)(2,1)S(1)}, u32[]{:S(2)}, u32[]{:S(2)}) collective-permute-start(bf16[432,128]{1,0:T(8,128)(2,1)S(1)} %get-tuple-element.111), channel_id=1, source_target_pairs={{0,6},{1,7},{2,4},{3,5},{4,2},{5,3},{6,0},{7,1},{8,14},{9,15},{10,... | collective-permute-start | bytes 331784 | tf_op jit(solution)/shard_map/ppermute | solution.py:520
  23.2 10.9 %collective-permute-start.9 = (bf16[2,432,128]{2,1,0:T(8,128)(2,1)S(1)}, bf16[2,432,128]{2,1,0:T(8,128)(2,1)S(1)}, u32[]{:S(2)}, u32[]{:S(2)}) collective-permute-start(bf16[2,432,128]{2,1,0:T(8,128)(2,1)S(1)} %get-tuple-element.125), channel_id=1, source_target_pairs={{0,2},{1,3},{2,0},{3,1},{4,6},{5,7},{6,4},{7,5},{8,10},{9,11},{10,... | collective-permute-start | bytes 663560 | tf_op jit(solution)/shard_map/ppermute | solution.py:520
  23.7 10.4 %collective-permute-start.10 = (bf16[2,432,128]{2,1,0:T(8,128)(2,1)S(1)}, bf16[2,432,128]{2,1,0:T(8,128)(2,1)S(1)}, u32[]{:S(2)}, u32[]{:S(2)}) collective-permute-start(bf16[2,432,128]{2,1,0:T(8,128)(2,1)S(1)} %get-tuple-element.126), channel_id=1, source_target_pairs={{0,4},{1,5},{2,6},{3,7},{4,0},{5,1},{6,2},{7,3},{8,12},{9,13},{10,... | collective-permute-start | bytes 663560 | tf_op jit(solution)/shard_map/ppermute | solution.py:520
  26.0 8.0 %collective-permute-start.11 = (bf16[432,128]{1,0:T(8,128)(2,1)S(1)}, bf16[432,128]{1,0:T(8,128)(2,1)S(1)}, u32[]{:S(2)}, u32[]{:S(2)}) collective-permute-start(bf16[432,128]{1,0:T(8,128)(2,1)S(1)} %get-tuple-element.127), channel_id=1, source_target_pairs={{0,6},{1,7},{2,4},{3,5},{4,2},{5,3},{6,0},{7,1},{8,14},{9,15},{10,... | collective-permute-start | bytes 331784 | tf_op jit(solution)/shard_map/ppermute | solution.py:520
  27.2 15.3 %copy-start.3 = (bf16[8,16,16,128]{3,2,1,0:T(8,128)(2,1)S(1)}, bf16[8,16,16,128]{3,2,1,0:T(8,128)(2,1)}, u32[]{:S(2)}) copy-start(bf16[8,16,16,128]{3,2,1,0:T(8,128)(2,1)} %own.2) | copy-start | bytes 1572868
  27.2 9.1 %collective-permute-start.6 = (bf16[2,16,16,128]{3,2,1,0:T(8,128)(2,1)S(1)}, bf16[2,16,16,128]{3,2,1,0:T(8,128)(2,1)S(1)}, u32[]{:S(2)}, u32[]{:S(2)}) collective-permute-start(bf16[2,16,16,128]{3,2,1,0:T(8,128)(2,1)S(1)} %get-tuple-element.112), channel_id=1, source_target_pairs={{0,8},{1,9},{2,10},{3,11},{4,12},{5,13},{6,14},{7,15},{8,0},{9,1},... | collective-permute-start | bytes 393224 | tf_op jit(solution)/shard_map/ppermute | solution.py:154
  28.4 7.9 %collective-permute-start.7 = (bf16[2,16,16,128]{3,2,1,0:T(8,128)(2,1)S(1)}, bf16[2,16,16,128]{3,2,1,0:T(8,128)(2,1)S(1)}, u32[]{:S(2)}, u32[]{:S(2)}) collective-permute-start(bf16[2,16,16,128]{3,2,1,0:T(8,128)(2,1)S(1)} %get-tuple-element.113), channel_id=1, source_target_pairs={{0,1},{1,0},{2,3},{3,2},{4,5},{5,4},{6,7},{7,6},{8,16},{9,17},{10,... | collective-permute-start | bytes 393224 | tf_op jit(solution)/shard_map/ppermute | solution.py:153
  34.4 4.9 %collective-permute-start.14 = (s16[448,128]{1,0:T(8,128)(2,1)S(1)}, s16[448,128]{1,0:T(8,128)(2,1)S(1)}, u32[]{:S(2)}, u32[]{:S(2)}) collective-permute-start(s16[448,128]{1,0:T(8,128)(2,1)S(1)} %get-tuple-element.132), channel_id=1, source_target_pairs={{0,8},{8,0},{16,24},{24,16},{1,9},{9,1},{17,25},{25,17},{2,10},{10... | collective-permute-start | bytes 344072 | tf_op jit(solution)/shard_map/ppermute | solution.py:520
  36.4 6.2 %collective-permute-start.13 = (bf16[2,10,16,128]{3,2,1,0:T(8,128)(2,1)S(1)}, bf16[2,10,16,128]{3,2,1,0:T(8,128)(2,1)S(1)}, u32[]{:S(2)}, u32[]{:S(2)}) collective-permute-start(bf16[2,10,16,128]{3,2,1,0:T(8,128)(2,1)S(1)} %get-tuple-element.138), channel_id=1, source_target_pairs={{0,8},{1,2},{2,1},{3,4},{4,3},{5,6},{6,5},{7,15},{8,0},{9,10},{10,... | collective-permute-start | bytes 245768 | tf_op jit(solution)/shard_map/ppermute | solution.py:153
  36.6 6.0 %collective-permute-start.12 = (bf16[2,10,16,128]{3,2,1,0:T(8,128)(2,1)S(1)}, bf16[2,10,16,128]{3,2,1,0:T(8,128)(2,1)S(1)}, u32[]{:S(2)}, u32[]{:S(2)}) collective-permute-start(bf16[2,10,16,128]{3,2,1,0:T(8,128)(2,1)S(1)} %get-tuple-element.137), channel_id=1, source_target_pairs={{0,1},{1,0},{2,3},{3,2},{4,5},{5,4},{6,7},{7,6},{8,9},{9,8},{10,11... | collective-permute-start | bytes 245768 | tf_op jit(solution)/shard_map/ppermute | solution.py:154
  39.4 7.3 %collective-permute-start.15 = (s16[448,128]{1,0:T(8,128)(2,1)S(1)}, s16[448,128]{1,0:T(8,128)(2,1)S(1)}, u32[]{:S(2)}, u32[]{:S(2)}) collective-permute-start(s16[448,128]{1,0:T(8,128)(2,1)S(1)} %shard_map.95.own), channel_id=1, source_target_pairs={{0,16},{8,24},{16,0},{24,8},{1,17},{9,25},{17,1},{25,9},{2,18},{10... | collective-permute-start | bytes 344072 | tf_op jit(solution)/shard_map/ppermute | solution.py:520
  46.9 4.9 %collective-permute-start.16 = (s16[448,128]{1,0:T(8,128)(2,1)S(1)}, s16[448,128]{1,0:T(8,128)(2,1)S(1)}, u32[]{:S(2)}, u32[]{:S(2)}) collective-permute-start(s16[448,128]{1,0:T(8,128)(2,1)S(1)} %shard_map.97.own), channel_id=1, source_target_pairs={{0,8},{8,0},{16,24},{24,16},{1,9},{9,1},{17,25},{25,17},{2,10},{10... | collective-permute-start | bytes 344072 | tf_op jit(solution)/shard_map/ppermute | solution.py:520
